TPU v7x, 32 devices: a whole 2x2x4 slice. The times are simulated.
32 devices in a mesh: expert: 16 (over z, y, x), shard: 2 (over core).
Axes of the slice: x: 2, y: 2, z: 4, core: 2. Of those that a mesh axis runs over, the one named last changes fastest.
Arguments:
- tokens: bfloat16 [4096, 768], P('expert'), may hold values from -6 to 6
- attn_gain: float32 [768], replicated, may hold values from 0.25 to 1.75
- query_weight: bfloat16 [768, 768], P(None, 'shard'), may hold values from -0.21875 to 0.21875
- key_weight: bfloat16 [768, 768], P(None, 'shard'), may hold values from -0.21875 to 0.21875
- value_weight: bfloat16 [768, 768], P(None, 'shard'), may hold values from -0.21875 to 0.21875
- output_weight: bfloat16 [768, 768], P('shard'), may hold values from -1.25 to 1.25
- bias_table: float32 [32, 12], P(None, 'shard'), may hold values from -5 to 5
- ffn_gain: float32 [768], replicated, may hold values from 0.25 to 1.75
- router_weight: bfloat16 [768, 16], replicated, may hold values from -0.15625 to 0.15625
- expert_in: bfloat16 [16, 768, 3072], P('expert', None, 'shard'), may hold values from -0.21875 to 0.21875
- expert_out: bfloat16 [16, 3072, 768], P('expert', 'shard'), may hold values from -3.5 to 3.5
- routes: int32 [4096, 1], P(('expert', 'shard')), may hold values from 0 to 15; in each aligned block of 128 rows (0 to 127, 128 to 255, ...) at most 16 rows name the same one
- lengths: int32 [16, 4], P('expert'), may hold values from 1 to 128, as said below
- cotangent: bfloat16 [4096, 768], P(('expert', 'shard')), may hold values from -6 to 6
Outputs:
- block_out: bfloat16 [4096, 768], P(('expert', 'shard'))
- grad_tokens: float32 [4096, 768], P('expert')
- grad_attn_gain: float32 [768], replicated
- grad_query: float32 [768, 768], P(None, 'shard')
- grad_key: float32 [768, 768], P(None, 'shard')
- grad_value: float32 [768, 768], P(None, 'shard')
- grad_output: float32 [768, 768], P('shard')
- grad_table: float32 [32, 12], P(None, 'shard')
- grad_ffn_gain: float32 [768], replicated
- grad_router: float32 [768, 16], replicated
- grad_expert_in: float32 [16, 768, 3072], P('expert', None, 'shard')
- grad_expert_out: float32 [16, 3072, 768], P('expert', 'shard')
Inputs may be any that keep to these rules, and one draw needn't show every extreme that they name: Each row gives the lengths of the 4 sequences of one token group in order; they sum to 256, and one of them is exactly 128 long. `routes`: within the 128 rows of one device (aligned blocks), no expert is named by more than 16 rows.
All inputs are finite; a program needn't handle non-finite values.
Results may differ from a plain program's by a relative error of at most 0.017.
Values may be sent and summed in bfloat16 or wider, within the bound.
No kernel may reach another device: no remote copies, remote signals or barrier semaphores. Data moves between devices by JAX's collectives and lax.ppermute only.
A program may use at most 128 MiB of HBM per device.

v0:
```python
import functools

import jax
import jax.numpy as jnp
from jax import lax
from jax.experimental import pallas as pl
from jax.experimental.pallas import tpu as pltpu
from jax.sharding import PartitionSpec as P

EPSILON = 1e-06
BORDERS = (12, 16, 23, 32, 46, 64, 91)
HIGHEST = lax.Precision.HIGHEST
EXCLUDED = -1e30
PLANE = 4
LINE = 4
LOW = jnp.bfloat16
FULL = jnp.float32
GRANT = 56 * 1024 * 1024


def inverse_rms(rows):
    return lax.rsqrt(jnp.mean(rows * rows, axis=-1, keepdims=True) + EPSILON)


def norm_back(rows, scale_rows, gain, grad_normed):
    scaled = grad_normed * gain
    grad_rows = scale_rows * scaled - rows * scale_rows**3 * jnp.mean(
        scaled * rows, axis=-1, keepdims=True
    )
    grad_gain = jnp.sum(grad_normed * rows * scale_rows, axis=0, keepdims=True)
    return (grad_rows, grad_gain)


def product(left, right, left_dim=1, right_dim=0, precision=None):
    return lax.dot_general(
        left,
        right,
        (((left_dim,), (right_dim,)), ((), ())),
        precision=precision,
        preferred_element_type=FULL,
    )


def wrapped_buckets(bucket_total, columns):
    column = lax.broadcasted_iota(jnp.int32, (bucket_total, columns), 1)
    offset = jnp.where(column < columns // 2, column, column - columns)
    magnitude = jnp.abs(offset)
    bucket = jnp.minimum(magnitude, 8)
    for border in BORDERS:
        bucket = bucket + (magnitude >= border).astype(jnp.int32)
    bucket = bucket + 16 * (offset > 0).astype(jnp.int32)
    rows = lax.broadcasted_iota(jnp.int32, (bucket_total, columns), 0)
    return (bucket == rows).astype(FULL)


def run(kernel, outs, operands, scratch=(), scalars=0, after=()):
    count = len(operands)

    def body(*refs):
        kernel(*refs[:count], *refs[count + len(after) :])

    def whole(shape):
        return pl.BlockSpec(shape, lambda: (0,) * len(shape))

    in_specs = [pl.BlockSpec(memory_space=pltpu.SMEM)] * scalars
    in_specs += [whole(item.shape) for item in operands[scalars:]]
    in_specs += [pl.BlockSpec(memory_space=pl.ANY)] * len(after)
    return pl.pallas_call(
        body,
        out_shape=[jax.ShapeDtypeStruct(shape, dtype) for shape, dtype in outs],
        in_specs=in_specs,
        out_specs=[whole(shape) for shape, _ in outs],
        scratch_shapes=list(scratch),
        compiler_params=pltpu.CompilerParams(vmem_limit_bytes=GRANT),
        cost_estimate=pl.CostEstimate(flops=0, bytes_accessed=0, transcendentals=0),
    )(*operands, *after)


def plan_kernel(routes_ref, cotangent_ref, place_ref, sent_ref, *, experts, capacity):
    own_rows, slots = place_ref.shape
    chosen = routes_ref[...]
    picked = chosen == lax.broadcasted_iota(jnp.int32, (own_rows, experts), 1)
    picked_float = picked.astype(FULL)
    earlier = lax.broadcasted_iota(jnp.int32, (own_rows, own_rows), 1) < lax.broadcasted_iota(
        jnp.int32, (own_rows, own_rows), 0
    )
    ranks = product(earlier.astype(FULL).astype(LOW), picked_float.astype(LOW))
    rank = jnp.sum(ranks * picked_float, axis=1, keepdims=True)
    target = chosen * capacity + rank.astype(jnp.int32)
    place = target == lax.broadcasted_iota(jnp.int32, (own_rows, slots), 1)
    place = place.astype(FULL).astype(LOW)
    place_ref[...] = place
    sent_ref[...] = product(place, cotangent_ref[...], 0, 0).astype(LOW)


def forward_kernel(
    lengths_ref,
    tokens_ref,
    gain_ref,
    query_ref,
    key_ref,
    value_ref,
    output_ref,
    table_ref,
    own_ref,
    other_ref,
    qkv_ref,
    probs_ref,
    normed_turned_ref,
    mixed_turned_ref,
    whole_ref,
    turned_ref,
    *,
    head_size,
):
    group_rows = tokens_ref.shape[0]
    own_rows = own_ref.shape[0]
    heads = table_ref.shape[1]
    columns = heads * head_size
    scale = head_size ** (-0.5)
    half = lax.axis_index("shard")
    own_at = pl.multiple_of(half * own_rows, own_rows)
    other_at = pl.multiple_of((1 - half) * own_rows, own_rows)
    inputs = tokens_ref[...].astype(FULL)
    normed = inputs * inverse_rms(inputs) * gain_ref[...]
    whole_ref[...] = normed
    normed_turned_ref[0:own_rows, :] = whole_ref[pl.ds(own_at, own_rows), :].astype(LOW)
    normed_turned_ref[own_rows:, :] = whole_ref[pl.ds(other_at, own_rows), :].astype(LOW)
    normed = normed.astype(LOW)
    queries = product(normed, query_ref[...]).astype(LOW)
    keys = product(normed, key_ref[...]).astype(LOW)
    values = product(normed, value_ref[...]).astype(LOW)
    qkv_ref[:, 0:columns] = queries
    qkv_ref[:, columns : 2 * columns] = keys
    qkv_ref[:, 2 * columns : 3 * columns] = values
    per_offset = product(
        table_ref[...], wrapped_buckets(table_ref.shape[0], group_rows), 0, 0, HIGHEST
    )
    row_at = lax.broadcasted_iota(jnp.int32, (group_rows, group_rows), 0)
    column_at = lax.broadcasted_iota(jnp.int32, (group_rows, group_rows), 1)
    row_part = jnp.zeros((group_rows, group_rows), jnp.int32)
    column_part = jnp.zeros((group_rows, group_rows), jnp.int32)
    end = 0
    for part in range(lengths_ref.shape[1] - 1):
        end = end + lengths_ref[0, part]
        row_part = row_part + (row_at >= end).astype(jnp.int32)
        column_part = column_part + (column_at >= end).astype(jnp.int32)
    same = row_part == column_part
    mixed_parts = []
    for head in range(heads):
        here = slice(head * head_size, (head + 1) * head_size)
        bias = pltpu.roll(
            jnp.broadcast_to(per_offset[head : head + 1, :], (group_rows, group_rows)),
            0,
            1,
            stride=1,
            stride_axis=0,
        )
        scores = product(queries[:, here], keys[:, here], 1, 1)
        scores = jnp.where(same, scores * scale + bias, EXCLUDED)
        raised = jnp.exp(scores - jnp.max(scores, axis=-1, keepdims=True))
        probs = raised * (1.0 / jnp.sum(raised, axis=-1, keepdims=True))
        probs_ref[head] = probs
        mixed_parts.append(product(probs.astype(LOW), values[:, here]))
    mixed = jnp.concatenate(mixed_parts, axis=1)
    turned_ref[...] = mixed
    mixed = mixed.astype(LOW)
    mixed_turned_ref[0:own_rows, :] = turned_ref[pl.ds(own_at, own_rows), :].astype(LOW)
    mixed_turned_ref[own_rows:, :] = turned_ref[pl.ds(other_at, own_rows), :].astype(LOW)
    whole_ref[...] = product(mixed, output_ref[...])
    own_ref[...] = whole_ref[pl.ds(own_at, own_rows), :]
    other_ref[...] = whole_ref[pl.ds(other_at, own_rows), :]


def hidden_kernel(tokens_ref, own_ref, came_ref, gain_ref, place_ref, hidden_ref, sent_ref):
    own_rows = own_ref.shape[0]
    own_at = pl.multiple_of(lax.axis_index("shard") * own_rows, own_rows)
    inputs = tokens_ref[pl.ds(own_at, own_rows), :].astype(FULL)
    hidden = inputs + (own_ref[...] + came_ref[...])
    hidden_ref[...] = hidden
    normed = (hidden * inverse_rms(hidden) * gain_ref[...]).astype(LOW)
    sent_ref[...] = product(place_ref[...], normed, 0, 0).astype(LOW)


def gate_kernel(
    rows_ref,
    grads_ref,
    router_ref,
    normed_ref,
    mixed_ref,
    chances_ref,
    grad_produced_ref,
    normed_own_ref,
    mixed_out_ref,
):
    logits = product(rows_ref[...], router_ref[...])
    raised = jnp.exp(logits - jnp.max(logits, axis=-1, keepdims=True))
    chances = raised * (1.0 / jnp.sum(raised, axis=-1, keepdims=True))
    chosen = lax.broadcasted_iota(jnp.int32, chances.shape, 1) == lax.axis_index("expert")
    gate = jnp.sum(jnp.where(chosen, chances, 0.0), axis=1, keepdims=True)
    chances_ref[...] = chances
    grad_produced_ref[...] = (gate * grads_ref[...].astype(FULL)).astype(LOW)
    normed_own_ref[...] = normed_ref[0 : normed_own_ref.shape[0], :]
    mixed_out_ref[...] = mixed_ref[...]


def expert_kernel(
    rows_ref,
    grad_produced_ref,
    in_own_ref,
    in_came_ref,
    out_own_ref,
    out_came_ref,
    produced_ref,
    grad_rows_ref,
    active_own_ref,
    active_came_ref,
    grad_pre_own_ref,
    grad_pre_came_ref,
    *,
    steps,
):
    step = pl.program_id(0)

    @pl.when(step == 0)
    def _():
        produced_ref[...] = jnp.zeros_like(produced_ref)
        grad_rows_ref[...] = jnp.zeros_like(grad_rows_ref)

    def block(in_ref, out_ref, active_ref, grad_pre_ref):
        pre = product(rows_ref[...], in_ref[...])
        grad_active = product(grad_produced_ref[...], out_ref[...], 1, 1)
        steep = 1.0 / (1.0 + 0.2316419 * jnp.abs(pre))
        density = jnp.exp(-0.5 * pre * pre) * 0.3989422804014327
        tail = 1.330274429
        for factor in (-1.821255978, 1.781477937, -0.356563782, 0.319381530):
            tail = tail * steep + factor
        tail = tail * steep * density
        cumulative = jnp.where(pre >= 0.0, 1.0 - tail, tail)
        active = (pre * cumulative).astype(LOW)
        grad_pre = (grad_active * (cumulative + pre * density)).astype(LOW)
        active_ref[...] = active
        grad_pre_ref[...] = grad_pre
        produced_ref[...] += product(active, out_ref[...])
        grad_rows_ref[...] += product(grad_pre, in_ref[...], 1, 1)

    @pl.when(step < steps // 2)
    def _():
        block(in_own_ref, out_own_ref, active_own_ref, grad_pre_own_ref)

    @pl.when(step >= steps // 2)
    def _():
        block(in_came_ref, out_came_ref, active_came_ref, grad_pre_came_ref)


def finish_kernel(
    produced_ref,
    grad_rows_ref,
    grads_ref,
    chances_ref,
    rows_ref,
    router_ref,
    back_ref,
    grad_back_ref,
    grad_router_ref,
):
    chances = chances_ref[...]
    chosen = lax.broadcasted_iota(jnp.int32, chances.shape, 1) == lax.axis_index("expert")
    gate = jnp.sum(jnp.where(chosen, chances, 0.0), axis=1, keepdims=True)
    produced = produced_ref[...].astype(LOW).astype(FULL)
    back_ref[...] = (gate * produced).astype(LOW)
    grad_gate = jnp.sum(grads_ref[...].astype(FULL) * produced, axis=1, keepdims=True)
    grad_logits = (grad_gate * chances * (chosen.astype(FULL) - gate)).astype(LOW)
    grad_router_ref[...] = product(grad_logits, rows_ref[...], 0, 0)
    grad_back_ref[...] = (
        grad_rows_ref[...] + product(grad_logits, router_ref[...], 1, 1)
    ).astype(LOW)


def apply_expert(rows, grad_produced, in_own, in_came, out_own, out_came):
    slots, width = rows.shape
    units = in_own.shape[1]
    block = 512
    half = units // block
    steps = 2 * half

    def early(step):
        return jnp.minimum(step, half - 1)

    def late(step):
        return jnp.maximum(step - half, 0)

    def fixed(shape):
        return pl.BlockSpec(shape, lambda step: (0, 0))

    def across(rows_here, place):
        return pl.BlockSpec((rows_here, block), lambda step: (0, place(step)))

    def down(place):
        return pl.BlockSpec((block, width), lambda step: (place(step), 0))

    shapes = [
        ((slots, width), FULL),
        ((slots, width), FULL),
    ] + [((slots, units), LOW)] * 4
    return pl.pallas_call(
        functools.partial(expert_kernel, steps=steps),
        grid=(steps,),
        out_shape=[jax.ShapeDtypeStruct(shape, dtype) for shape, dtype in shapes],
        in_specs=[
            fixed((slots, width)),
            fixed((slots, width)),
            across(width, early),
            across(width, late),
            down(early),
            down(late),
        ],
        out_specs=[
            fixed((slots, width)),
            fixed((slots, width)),
            across(slots, early),
            across(slots, late),
            across(slots, early),
            across(slots, late),
        ],
        compiler_params=pltpu.CompilerParams(vmem_limit_bytes=GRANT),
        cost_estimate=pl.CostEstimate(flops=0, bytes_accessed=0, transcendentals=0),
    )(rows, grad_produced, in_own, in_came, out_own, out_came)


def grad_hidden_kernel(
    place_ref,
    returned_ref,
    hidden_ref,
    gain_ref,
    cotangent_ref,
    grad_router_ref,
    attention_ref,
    small_ref,
):
    experts = grad_router_ref.shape[0]
    width = hidden_ref.shape[1]
    hidden = hidden_ref[...]
    grad_normed = product(place_ref[...], returned_ref[...])
    grad_rows, grad_gain = norm_back(hidden, inverse_rms(hidden), gain_ref[...], grad_normed)
    attention_ref[...] = (cotangent_ref[...].astype(FULL) + grad_rows).astype(LOW)
    small_ref[0:experts, :] = grad_router_ref[...]
    small_ref[experts:, :] = jnp.concatenate(
        [grad_gain, jnp.zeros((small_ref.shape[0] - experts - 1, width), FULL)], axis=0
    )


def halves(own_rows):
    half = lax.axis_index("shard")
    own_at = pl.multiple_of(half * own_rows, own_rows)
    other_at = pl.multiple_of((1 - half) * own_rows, own_rows)
    return (own_at, other_at)


def value_back_kernel(
    attention_own_ref,
    attention_came_ref,
    output_ref,
    probs_ref,
    grad_mixed_ref,
    grad_values_ref,
    part_ref,
    part_one_ref,
    part_two_ref,
    part_three_ref,
    attention_ref,
    values_ref,
    turned_ref,
    *,
    head_size,
):
    own_rows = attention_own_ref.shape[0]
    heads = probs_ref.shape[0]
    columns = heads * head_size
    own_at, other_at = halves(own_rows)
    attention_ref[pl.ds(own_at, own_rows), :] = attention_own_ref[...]
    attention_ref[pl.ds(other_at, own_rows), :] = attention_came_ref[...]
    grad_mixed = product(attention_ref[...], output_ref[...], 1, 1).astype(LOW)
    grad_mixed_ref[...] = grad_mixed
    grad_values = []
    for head in range(heads):
        here = slice(head * head_size, (head + 1) * head_size)
        grad_values.append(product(probs_ref[head].astype(LOW), grad_mixed[:, here], 0, 0))
    grad_values = jnp.concatenate(grad_values, axis=1)
    grad_values_ref[...] = grad_values.astype(LOW)
    values_ref[...] = grad_values
    turned_ref[0:columns, 0:own_rows] = values_ref[pl.ds(own_at, own_rows), :].T
    turned_ref[0:columns, own_rows:] = values_ref[pl.ds(other_at, own_rows), :].T
    turned_ref[columns:, 0:own_rows] = attention_own_ref[...].astype(FULL).T
    turned_ref[columns:, own_rows:] = attention_came_ref[...].astype(FULL).T
    mine = lax.rem(lax.axis_index("expert"), PLANE)
    rows = columns // PLANE
    more = attention_own_ref.shape[1] // PLANE
    refs = (part_ref, part_one_ref, part_two_ref, part_three_ref)
    for other, ref in enumerate(refs):
        at = pl.multiple_of((mine ^ other) * rows, 16)
        ref[0:rows, :] = turned_ref[pl.ds(at, rows), :].astype(LOW)
        at = pl.multiple_of((mine ^ other) * more + columns, 16)
        ref[rows:, :] = turned_ref[pl.ds(at, more), :].astype(LOW)


def query_back_kernel(
    grad_mixed_ref,
    grad_values_ref,
    qkv_ref,
    probs_ref,
    query_ref,
    key_ref,
    value_ref,
    back_ref,
    grad_normed_ref,
    grad_table_ref,
    back_out_ref,
    part_ref,
    part_one_ref,
    part_two_ref,
    part_three_ref,
    grads_ref,
    turned_ref,
    *,
    head_size,
    bucket_total,
):
    group_rows = grad_mixed_ref.shape[0]
    own_rows = group_rows // 2
    heads = probs_ref.shape[0]
    columns = heads * head_size
    scale = head_size ** (-0.5)
    own_at, other_at = halves(own_rows)
    back_out_ref[...] = back_ref[...]
    reversal = (
        lax.broadcasted_iota(jnp.int32, (group_rows, group_rows), 0)
        + lax.broadcasted_iota(jnp.int32, (group_rows, group_rows), 1)
        == group_rows - 1
    )
    reversal = reversal.astype(FULL).astype(LOW)
    grad_queries, grad_keys, sums = [], [], []
    for head in range(heads):
        first = head * head_size
        queries = qkv_ref[:, first : first + head_size]
        keys = qkv_ref[:, columns + first : columns + first + head_size]
        values = qkv_ref[:, 2 * columns + first : 2 * columns + first + head_size]
        probs = probs_ref[head]
        grad_probs = product(grad_mixed_ref[:, first : first + head_size], values, 1, 1)
        inner = jnp.sum(probs * grad_probs, axis=-1, keepdims=True)
        grad_scores = probs * (grad_probs - inner)
        upper = grad_scores.astype(LOW)
        rest = (grad_scores - upper.astype(FULL)).astype(LOW)
        backwards = product(reversal, upper) + product(reversal, rest)
        aligned = pltpu.roll(backwards, 1, 1, stride=1, stride_axis=0)
        sums.append(jnp.sum(aligned, axis=0, keepdims=True))
        grad_queries.append(product(upper, keys) * scale)
        grad_keys.append(product(upper, queries, 0, 0) * scale)
    grad_table_ref[...] = product(
        jnp.concatenate(sums, axis=0), wrapped_buckets(bucket_total, group_rows), 1, 1, HIGHEST
    )
    grad_queries = jnp.concatenate(grad_queries, axis=1)
    grad_keys = jnp.concatenate(grad_keys, axis=1)
    grads_ref[:, 0:columns] = grad_queries
    grads_ref[:, columns:] = grad_keys
    turned_ref[:, 0:own_rows] = grads_ref[pl.ds(own_at, own_rows), :].T
    turned_ref[:, own_rows:] = grads_ref[pl.ds(other_at, own_rows), :].T
    mine = lax.rem(lax.axis_index("expert"), PLANE)
    rows = columns // PLANE
    refs = (part_ref, part_one_ref, part_two_ref, part_three_ref)
    for other, ref in enumerate(refs):
        at = pl.multiple_of((mine ^ other) * rows, 16)
        ref[0:rows, :] = turned_ref[pl.ds(at, rows), :].astype(LOW)
        ref[rows:, :] = turned_ref[pl.ds(pl.multiple_of(at + columns, 16), rows), :].astype(LOW)
    grad_normed = product(grad_queries.astype(LOW), query_ref[...], 1, 1)
    grad_normed = grad_normed + product(grad_keys.astype(LOW), key_ref[...], 1, 1)
    grad_normed = grad_normed + product(grad_values_ref[...], value_ref[...], 1, 1)
    grad_normed_ref[...] = grad_normed.astype(LOW)


def grad_tokens_kernel(
    tokens_ref,
    gain_ref,
    normed_own_ref,
    normed_came_ref,
    attention_own_ref,
    attention_came_ref,
    small_own_ref,
    small_came_ref,
    table_ref,
    grad_tokens_ref,
    small_ref,
):
    own_rows = attention_own_ref.shape[0]
    width = tokens_ref.shape[1]
    heads, buckets = table_ref.shape
    half = lax.axis_index("shard")
    own_at = pl.multiple_of(half * own_rows, own_rows)
    other_at = pl.multiple_of((1 - half) * own_rows, own_rows)
    inputs = tokens_ref[...].astype(FULL)
    grad_normed = normed_own_ref[...].astype(FULL) + normed_came_ref[...].astype(FULL)
    grad_rows, grad_gain = norm_back(inputs, inverse_rms(inputs), gain_ref[...], grad_normed)
    grad_tokens_ref[...] = grad_rows
    grad_tokens_ref[pl.ds(own_at, own_rows), :] += attention_own_ref[...].astype(FULL)
    grad_tokens_ref[pl.ds(other_at, own_rows), :] += attention_came_ref[...].astype(FULL)
    summed = small_own_ref[...] + small_came_ref[...]
    table = jnp.concatenate([table_ref[...], jnp.zeros((heads, width - buckets), FULL)], axis=1)
    more = small_ref.shape[0] - summed.shape[0] - heads - 1
    small_ref[...] = jnp.concatenate(
        [summed, grad_gain, table, jnp.zeros((more, width), FULL)], axis=0
    ).astype(small_ref.dtype)


def line_chunks(totals, refs, total_refs):
    mine = lax.rem(lax.axis_index("expert") // PLANE, LINE)
    width = refs[0].shape[1]
    for total, total_ref in zip(totals, total_refs):
        total_ref[...] = total
    for other, ref in enumerate(refs):
        chunks = []
        for total_ref in total_refs:
            rows = total_ref.shape[0] // LINE
            at = pl.multiple_of((mine ^ other) * rows, 8)
            chunk = total_ref[pl.ds(at, rows), :]
            cut = rows * chunk.shape[1] // width
            chunks.append(
                jnp.concatenate(
                    [chunk[start : start + cut] for start in range(0, rows, cut)], axis=1
                )
                if cut != rows
                else chunk
            )
        ref[...] = jnp.concatenate(chunks, axis=0).astype(ref.dtype)


def met(part, normed_near, normed_far):
    own_rows = normed_near.shape[0]
    return product(part[:, 0:own_rows], normed_near) + product(part[:, own_rows:], normed_far)


def first_sums_kernel(*refs):
    parts, nears, fars, mixeds, outs = (refs[4 * at : 4 * at + 4] for at in range(5))
    columns = mixeds[0].shape[1]
    rows = columns // PLANE
    value_total = 0.0
    output_total = 0.0
    for part, near, far, mixed in zip(parts, nears, fars, mixeds):
        value_total = value_total + met(part[0:rows, :], near[...], far[...])
        output_total = output_total + product(part[rows:, :], mixed[...])
    line_chunks((value_total, output_total), outs, refs[20:22])


def second_sums_kernel(*refs):
    parts, nears, fars, outs = (refs[4 * at : 4 * at + 4] for at in range(4))
    total = 0.0
    for part, near, far in zip(parts, nears, fars):
        total = total + met(part[...], near[...], far[...])
    rows = total.shape[0] // 2
    line_chunks((total[0:rows], total[rows:]), outs, refs[16:18])


def line_sum_kernel(first_ref, second_ref, third_ref, fourth_ref, out_ref):
    near = first_ref[...].astype(FULL) + second_ref[...].astype(FULL)
    far = third_ref[...].astype(FULL) + fourth_ref[...].astype(FULL)
    out_ref[...] = (near + far).astype(out_ref.dtype)


def gathered(refs, upper_ref, lower_ref):
    member = lax.rem(lax.axis_index("expert"), PLANE)
    floor = lax.rem(lax.axis_index("expert") // PLANE, LINE)
    owns, rests = refs[0:PLANE], refs[PLANE:]
    chunk_rows = owns[0].shape[0]
    for across in range(PLANE):
        for along in range(LINE):
            if along == 0:
                chunk = owns[across][...]
            else:
                chunk = rests[across][(along - 1) * chunk_rows : along * chunk_rows, :]
            chunk = chunk.astype(FULL)
            first = 0
            for out_ref in (upper_ref, lower_ref):
                rows = out_ref.shape[0] // PLANE // LINE
                at = ((member ^ across) * LINE + (floor ^ along)) * rows
                cut = rows * out_ref.shape[1] // chunk.shape[1]
                for piece in range(rows // cut):
                    place = pl.multiple_of(at + piece * cut, 8)
                    side = slice(piece * out_ref.shape[1], (piece + 1) * out_ref.shape[1])
                    out_ref[pl.ds(place, cut), :] = chunk[first : first + cut, side]
                first = first + cut


def assemble_kernel(*refs):
    upper_ref, lower_ref = refs[2 * PLANE], refs[2 * PLANE + 1]
    gathered(refs[0 : 2 * PLANE], refs[2 * PLANE + 2], refs[2 * PLANE + 3])
    upper_ref[...] = refs[2 * PLANE + 2][...].T
    lower_ref[...] = refs[2 * PLANE + 3][...].T


def shards(
    tokens,
    attn_gain,
    query_weight,
    key_weight,
    value_weight,
    output_weight,
    bias_table,
    ffn_gain,
    router_weight,
    expert_in,
    expert_out,
    routes,
    lengths,
    cotangent,
):
    group_rows, width = tokens.shape
    own_rows = cotangent.shape[0]
    heads = bias_table.shape[1]
    buckets = bias_table.shape[0]
    columns = query_weight.shape[1]
    head_size = columns // heads
    sources = lax.axis_size("expert")
    experts = router_weight.shape[1]
    capacity = 2 * own_rows // experts
    slots = experts * capacity
    beyond = sources // (PLANE * LINE)
    attn_gain = attn_gain.reshape(1, width)
    ffn_gain = ffn_gain.reshape(1, width)

    def swap(item):
        return lax.ppermute(item, "shard", [(0, 1), (1, 0)])

    def hop(item, distance):
        return lax.ppermute(item, "expert", [(at, at ^ distance) for at in range(sources)])

    def around(items, stride):
        return tuple(hop(item, stride * (step + 1)) for step, item in enumerate(items))

    def exchange(rows):
        parts = rows.reshape(sources, capacity * experts // sources, width)
        came = lax.all_to_all(parts, "expert", split_axis=0, concat_axis=0, tiled=True)
        return came.reshape(slots, width)

    def beyond_sum(item):
        if beyond == 1:
            return item
        groups = [
            [near + PLANE * LINE * far for far in range(beyond)] for near in range(PLANE * LINE)
        ]
        return lax.psum(item, "expert", axis_index_groups=groups)

    place, sent_grads = run(
        functools.partial(plan_kernel, experts=experts, capacity=capacity),
        [((own_rows, slots), LOW), ((slots, width), LOW)],
        (routes, cotangent),
    )
    grads = exchange(sent_grads)
    in_own, out_own = expert_in[0], expert_out[0]
    in_came, out_came = swap(in_own), swap(out_own)
    own, other, qkv, probs, normed, mixed = run(
        functools.partial(forward_kernel, head_size=head_size),
        [
            ((own_rows, width), FULL),
            ((own_rows, width), FULL),
            ((group_rows, 3 * columns), LOW),
            ((heads, group_rows, group_rows), FULL),
            ((group_rows, width), LOW),
            ((group_rows, columns), LOW),
        ],
        (
            lengths,
            tokens,
            attn_gain,
            query_weight,
            key_weight,
            value_weight,
            output_weight,
            bias_table,
        ),
        scratch=(pltpu.VMEM((group_rows, width), FULL), pltpu.VMEM((group_rows, columns), FULL)),
        scalars=1,
        after=(place,),
    )
    hidden, sent_rows = run(
        hidden_kernel,
        [((own_rows, width), FULL), ((slots, width), LOW)],
        (tokens, own, swap(other), ffn_gain, place),
        after=(grads, in_came, out_came),
    )
    rows = exchange(sent_rows)
    chances, grad_produced, normed_own, mixed = run(
        gate_kernel,
        [
            ((slots, experts), FULL),
            ((slots, width), LOW),
            ((own_rows, width), LOW),
            ((group_rows, columns), LOW),
        ],
        (rows, grads, router_weight, normed, mixed),
    )
    normed_near = around((normed_own,) * 3, 1)
    mixed_near = around((mixed,) * 3, 1)
    (
        produced,
        grad_rows,
        active_own,
        active_came,
        grad_pre_own,
        grad_pre_came,
    ) = apply_expert(rows, grad_produced, in_own, in_came, out_own, out_came)
    back, grad_back, grad_router = run(
        finish_kernel,
        [((slots, width), LOW), ((slots, width), LOW), ((experts, width), FULL)],
        (produced, grad_rows, grads, chances, rows, router_weight),
        after=normed_near + mixed_near,
    )
    returned_grads = exchange(grad_back)
    grad_in_other = product(rows, grad_pre_came, 0, 0).astype(jnp.bfloat16)
    grad_out_other = product(active_came, grad_produced, 0, 0).astype(jnp.bfloat16)
    small_rows = -(-(experts + 1) // 8) * 8
    attention_own, small_own = run(
        grad_hidden_kernel,
        [((own_rows, width), LOW), ((small_rows, width), FULL)],
        (place, returned_grads, hidden, ffn_gain, cotangent, grad_router),
        after=(grad_in_other, grad_out_other),
    )
    grad_in_came, grad_out_came = swap(grad_in_other), swap(grad_out_other)
    attention_came = swap(attention_own)
    part_rows = columns // PLANE
    grad_mixed, grad_values, *first_parts = run(
        functools.partial(value_back_kernel, head_size=head_size),
        [((group_rows, columns), LOW), ((group_rows, columns), LOW)]
        + [((part_rows + width // PLANE, group_rows), LOW)] * PLANE,
        (attention_own, attention_came, output_weight, probs),
        scratch=(
            pltpu.VMEM((group_rows, width), LOW),
            pltpu.VMEM((group_rows, columns), FULL),
            pltpu.VMEM((columns + width, group_rows), FULL),
        ),
    )
    first_parts = (first_parts[0],) + around(first_parts[1:], 1)
    grad_normed_own, grad_table, back, *second_parts = run(
        functools.partial(query_back_kernel, head_size=head_size, bucket_total=buckets),
        [((group_rows, width), LOW), ((heads, buckets), FULL), ((slots, width), LOW)]
        + [((2 * part_rows, group_rows), LOW)] * PLANE,
        (
            grad_mixed,
            grad_values,
            qkv,
            probs,
            query_weight,
            key_weight,
            value_weight,
            back,
        ),
        scratch=(
            pltpu.VMEM((group_rows, 2 * columns), FULL),
            pltpu.VMEM((2 * columns, group_rows), FULL),
        ),
    )
    second_parts = (second_parts[0],) + around(second_parts[1:], 1)
    grad_normed_came = swap(grad_normed_own)
    small_came = swap(small_own)
    nears = (normed[0:own_rows],) + normed_near
    fars = (normed[own_rows:],) + tuple(swap(item) for item in normed_near)
    line_rows = part_rows // LINE
    first_chunks = run(
        first_sums_kernel,
        [((2 * line_rows, width), LOW)] * LINE,
        first_parts + nears + fars + (mixed,) + mixed_near,
        scratch=(pltpu.VMEM((part_rows, width), FULL), pltpu.VMEM((width // PLANE, columns), FULL)),
    )
    first_chunks = (first_chunks[0],) + around(first_chunks[1:], PLANE)
    grad_tokens, small = run(
        grad_tokens_kernel,
        [
            ((group_rows, width), FULL),
            ((small_rows + -(-(heads + 1) // 8) * 8, width), LOW),
        ],
        (
            tokens,
            attn_gain,
            grad_normed_own,
            grad_normed_came,
            attention_own,
            attention_came,
            small_own,
            small_came,
            grad_table,
        ),
    )
    second_chunks = run(
        second_sums_kernel,
        [((2 * line_rows, width), LOW)] * LINE,
        second_parts + nears + fars,
        scratch=(pltpu.VMEM((part_rows, width), FULL), pltpu.VMEM((part_rows, width), FULL)),
    )
    second_chunks = (second_chunks[0],) + around(second_chunks[1:], PLANE)
    returned = exchange(back)
    block_out = (
        hidden + jnp.dot(place, returned, preferred_element_type=jnp.float32)
    ).astype(jnp.bfloat16)

    def line_sum(chunks, dtype):
        (chunk,) = run(line_sum_kernel, [(chunks[0].shape, dtype)], chunks)
        return chunk

    def gather(chunks):
        chunk = line_sum(chunks, FULL if beyond > 1 else LOW)
        chunk = beyond_sum(chunk).astype(LOW)
        along = jnp.concatenate(around((chunk,) * 3, PLANE), axis=0)
        across = (chunk,) + around((chunk,) * 3, 1)
        return across + (along,) + around((along,) * 3, 1)

    small = (small,) + around((small,) * 3, PLANE)
    small = beyond_sum(line_sum(small, FULL)).astype(LOW)
    small = (small,) + around((small,) * 3, 1)
    small = line_sum(small, FULL)
    first_all = gather(first_chunks)
    second_all = gather(second_chunks)
    grad_expert_in = product(rows, grad_pre_own, 0, 0) + grad_in_came.astype(jnp.float32)
    grad_expert_out = product(active_own, grad_produced, 0, 0) + grad_out_came.astype(jnp.float32)
    grad_value, grad_output = run(
        assemble_kernel,
        [((width, columns), FULL), ((columns, width), FULL)],
        first_all,
        scratch=(pltpu.VMEM((columns, width), FULL), pltpu.VMEM((width, columns), FULL)),
        after=(grad_expert_in, grad_expert_out),
    )
    grad_query, grad_key = run(
        assemble_kernel,
        [((width, columns), FULL)] * 2,
        second_all,
        scratch=(pltpu.VMEM((columns, width), FULL), pltpu.VMEM((columns, width), FULL)),
    )
    grad_router = small[0:experts].T
    grad_ffn_gain = small[experts]
    grad_attn_gain = small[small_rows]
    grad_table = small[small_rows + 1 : small_rows + 1 + heads, 0:buckets].T

    return (
        block_out,
        grad_tokens,
        grad_attn_gain,
        grad_query,
        grad_key,
        grad_value,
        grad_output,
        grad_table,
        grad_ffn_gain,
        grad_router,
        grad_expert_in[None],
        grad_expert_out[None],
    )


def solution(mesh):
    return jax.shard_map(
        shards,
        mesh=mesh,
        in_specs=(
            P("expert", None),
            P(),
            P(None, "shard"),
            P(None, "shard"),
            P(None, "shard"),
            P("shard", None),
            P(None, "shard"),
            P(),
            P(),
            P("expert", None, "shard"),
            P("expert", "shard", None),
            P(("expert", "shard"), None),
            P("expert", None),
            P(("expert", "shard"), None),
        ),
        out_specs=(
            P(("expert", "shard"), None),
            P("expert", None),
            P(),
            P(None, "shard"),
            P(None, "shard"),
            P(None, "shard"),
            P("shard", None),
            P(None, "shard"),
            P(),
            P(),
            P("expert", None, "shard"),
            P("expert", "shard", None),
        ),
        check_vma=False,
    )
```

profile of v0, /device:TPU:0, one launch (start us, length us, event | category | flops | bytes accessed | tf_op | source)
XLA Modules:
  0.0 223.7 jit_solution(13836947335829691)
XLA Ops:
  1.3 1.4 copy.26.refs_0_
  2.6 2.4 %shard_map.229 = (bf16[128,256]{1,0:T(8,128)(2,1)}, bf16[256,768]{1,0:T(8,128)(2,1)}) custom-call(s32[128,1]{1,0:T(8,128)} %copy.26.refs_0_, bf16[128,768]{1,0:T(8,128)(2,1)} %refs_4_.4), custom_call_target="tpu_custom_call" | custom-call | tf_op jit(solution)/shard_map/pallas_call | solution.py:68
  5.0 8.3 %all-to-all-start = ((bf16[16,16,768]{2,1,0:T(8,128)(2,1)}), bf16[16,16,768]{2,1,0:T(8,128)(2,1)S(1)}, u32[]{:S(2)}, u32[]{:S(2)}) async-start(bf16[16,16,768]{2,1,0:T(8,128)(2,1)} %bitcast.41), calls=%async_computation | async-start | bytes 786432 | tf_op jit(solution)/shard_map/all_to_all | solution.py:640
  13.3 1.3 reshape.54.refs_2_.refs_1_
  14.6 1.4 copy.27.refs_7_
  15.9 6.4 %shard_map.230 = (f32[128,768]{1,0:T(8,128)}, f32[128,768]{1,0:T(8,128)}, bf16[256,1152]{1,0:T(8,128)(2,1)}, f32[6,256,256]{2,1,0:T(8,128)}, bf16[256,768]{1,0:T(8,128)(2,1)}, /*index=5*/bf16[256,384]{1,0:T(8,128)(2,1)}) custom-call(s32[1,4]{1,0:T(1,128)} %refs_0_.4, bf16[256,768]{1,0:T(8,128)(2,1)} %refs_0_.6, f32[1,768]{1,0:T(1,128)} %reshape.54.refs_2_.refs_1_, ...), custom_call_target="tpu_custom_call" | custom-call | tf_op jit(solution)/shard_map/pallas_call | solution.py:68
  23.0 1.3 collective-permute-done.refs_2_
  24.3 1.8 all-to-all-done
  27.7 2.4 %shard_map.231 = (f32[128,768]{1,0:T(8,128)}, bf16[256,768]{1,0:T(8,128)(2,1)}) custom-call(bf16[256,768]{1,0:T(8,128)(2,1)} %refs_0_.6, f32[128,768]{1,0:T(8,128)} %get-tuple-element.65.refs_1_, f32[128,768]{1,0:T(8,128)} %copy-done.25, f32[1,768]{1,0:T(1,128)} %reshape.55.refs_3_, bf16[128,256]{1,0:T(8,128)(2,1)} %get-tuple-element.64.refs_8_.refs_4_.refs_0_, ...), custom_call_target="tpu_custom_call" | custom-call | tf_op jit(solution)/shard_map/pallas_call | solution.py:68
  30.1 5.2 %all-to-all-start.1 = ((bf16[16,16,768]{2,1,0:T(8,128)(2,1)}), bf16[16,16,768]{2,1,0:T(8,128)(2,1)S(1)}, u32[]{:S(2)}, u32[]{:S(2)}) async-start(bf16[16,16,768]{2,1,0:T(8,128)(2,1)} %bitcast.43), calls=%async_computation.1 | async-start | bytes 786432 | tf_op jit(solution)/shard_map/all_to_all | solution.py:640
  36.1 12.1 %all-to-all-done.1 = bf16[16,16,768]{2,1,0:T(8,128)(2,1)S(1)} async-done(((bf16[16,16,768]{2,1,0:T(8,128)(2,1)}), bf16[16,16,768]{2,1,0:T(8,128)(2,1)S(1)}, u32[]{:S(2)}, u32[]{:S(2)}) %all-to-all-start.1) | async-done | bytes 393248 | tf_op jit(solution)/shard_map/all_to_all | solution.py:640
  49.0 2.7 %shard_map.232 = (f32[256,16]{1,0:T(8,128)}, bf16[256,768]{1,0:T(8,128)(2,1)}, bf16[128,768]{1,0:T(8,128)(2,1)}, bf16[256,384]{1,0:T(8,128)(2,1)}) custom-call(bf16[256,768]{1,0:T(8,128)(2,1)} %bitcast.28, bf16[256,768]{1,0:T(8,128)(2,1)} %bitcast.34, bf16[768,16]{1,0:T(8,128)(2,1)} %copy.28.refs_2_.refs_5_, bf16[256,768]{1,0:T(8,128)(2,1)} %get-tuple-element.70.refs_3_, ...), custom_call_target="tpu_custom_call" | custom-call | tf_op jit(solution)/shard_map/pallas_call | solution.py:68
  53.7 1.5 collective-permute-start.3
  57.2 3.5 %collective-permute-done.5.refs_8_.refs_7_ = bf16[128,768]{1,0:T(8,128)(2,1)S(1)} collective-permute-done((bf16[128,768]{1,0:T(8,128)(2,1)}, bf16[128,768]{1,0:T(8,128)(2,1)S(1)}, u32[]{:S(2)}, u32[]{:S(2)}) %collective-permute-start.5) | collective-permute-done | bytes 196640 | tf_op jit(solution)/shard_map/ppermute | solution.py:633
  61.3 12.2 %shard_map.233 = (f32[256,768]{1,0:T(8,128)}, f32[256,768]{1,0:T(8,128)}, bf16[256,1536]{1,0:T(8,128)(2,1)}, bf16[256,1536]{1,0:T(8,128)(2,1)}, bf16[256,1536]{1,0:T(8,128)(2,1)}, /*index=5*/bf16[256,1536]{1,0:T(8,128)(2,1)}) custom-call(bf16[256,768]{1,0:T(8,128)(2,1)} %bitcast.29, bf16[256,768]{1,0:T(8,128)(2,1)} %get-tuple-element.72.grad_produced_ref, ...), custom_call_target="tpu_custom_call" | custom-call | tf_op jit(solution)/shard_map/pallas_call | solution.py:306
  74.5 2.9 %shard_map.234 = (bf16[256,768]{1,0:T(8,128)(2,1)}, bf16[256,768]{1,0:T(8,128)(2,1)}, f32[16,768]{1,0:T(8,128)}) custom-call(f32[256,768]{1,0:T(8,128)} %get-tuple-element.73.refs_0_, f32[256,768]{1,0:T(8,128)} %get-tuple-element.74.refs_1_, bf16[256,768]{1,0:T(8,128)(2,1)} %bitcast.35, f32[256,16]{1,0:T(8,128)} %get-tuple-element.75.refs_3_, ...), custom_call_target="tpu_custom_call" | custom-call | tf_op jit(solution)/shard_map/pallas_call | solution.py:68
  77.4 4.5 %all-to-all-start.2 = ((bf16[16,16,768]{2,1,0:T(8,128)(2,1)}), bf16[16,16,768]{2,1,0:T(8,128)(2,1)S(1)}, u32[]{:S(2)}, u32[]{:S(2)}) async-start(bf16[16,16,768]{2,1,0:T(8,128)(2,1)} %bitcast.42), calls=%async_computation.2 | async-start | bytes 786432 | tf_op jit(solution)/shard_map/all_to_all | solution.py:640
  82.0 2.2 convolution_convert_fusion.1.refs_6_
  84.2 2.2 convolution_convert_fusion.refs_7_
  86.4 5.2 %all-to-all-done.2 = bf16[16,16,768]{2,1,0:T(8,128)(2,1)S(1)} async-done(((bf16[16,16,768]{2,1,0:T(8,128)(2,1)}), bf16[16,16,768]{2,1,0:T(8,128)(2,1)S(1)}, u32[]{:S(2)}, u32[]{:S(2)}) %all-to-all-start.2) | async-done | bytes 393248 | tf_op jit(solution)/shard_map/all_to_all | solution.py:640
  92.4 2.3 %shard_map.235 = (bf16[128,768]{1,0:T(8,128)(2,1)}, f32[24,768]{1,0:T(8,128)}) custom-call(bf16[128,256]{1,0:T(8,128)(2,1)} %get-tuple-element.64.refs_8_.refs_4_.refs_0_, bf16[256,768]{1,0:T(8,128)(2,1)} %bitcast.40, f32[128,768]{1,0:T(8,128)} %get-tuple-element.68.refs_2_, f32[1,768]{1,0:T(1,128)} %reshape.55.refs_3_, bf16[128,768]{1,0:T(8,128)(2,1)} %refs_4_.4, ...), custom_call_target="tpu_custom_call" | custom-call | tf_op jit(solution)/shard_map/pallas_call | solution.py:68
  97.0 3.8 %shard_map.236 = (bf16[256,384]{1,0:T(8,128)(2,1)}, bf16[256,384]{1,0:T(8,128)(2,1)}, bf16[288,256]{1,0:T(8,128)(2,1)}, bf16[288,256]{1,0:T(8,128)(2,1)}, bf16[2...) custom-call(bf16[128,768]{1,0:T(8,128)(2,1)} %get-tuple-element.82.refs_0_.refs_4_, bf16[128,768]{1,0:T(8,128)(2,1)} %copy-done.17, ...), custom_call_target="tpu_custom_call" | custom-call | tf_op jit(solution)/shard_map/pallas_call | solution.py:68
  100.8 7.1 %shard_map.237 = (bf16[256,768]{1,0:T(8,128)(2,1)}, f32[6,32]{1,0:T(8,128)}, bf16[256,768]{1,0:T(8,128)(2,1)}, bf16[192,256]{1,0:T(8,128)(2,1)}, bf16[192,256]{1...) custom-call(bf16[256,384]{1,0:T(8,128)(2,1)} %get-tuple-element.84.refs_0_, ...), custom_call_target="tpu_custom_call" | custom-call | tf_op jit(solution)/shard_map/pallas_call | solution.py:68
  107.9 1.5 collective-permute-start.18
  109.5 1.9 collective-permute-start.20
  111.5 1.5 collective-permute-done.18.refs_1_
  113.0 2.1 collective-permute-start.36
  116.4 1.5 collective-permute-start.38
  118.7 3.1 %shard_map.241 = (bf16[48,768]{1,0:T(8,128)(2,1)}, bf16[48,768]{1,0:T(8,128)(2,1)}, bf16[48,768]{1,0:T(8,128)(2,1)}, bf16[48,768]{1,0:T(8,128)(2,1)}) custom-call(bf16[192,256]{1,0:T(8,128)(2,1)} %get-tuple-element.94.refs_0_, bf16[192,256]{1,0:T(8,128)(2,1)} %copy-done.39, bf16[192,256]{1,0:T(8,128)(2,1)} %copy-done.40, bf16[192,256]{1,0:T(8,128)(2,1)} %copy-done.41, ...), custom_call_target="tpu_custom_call" | custom-call | tf_op jit(solution)/shard_map/pallas_call | solution.py:68
  121.9 1.8 collective-permute-done.37.refs_2_
  124.8 3.3 %shard_map.244 = (bf16[48,768]{1,0:T(8,128)(2,1)}, bf16[48,768]{1,0:T(8,128)(2,1)}, bf16[48,768]{1,0:T(8,128)(2,1)}, bf16[48,768]{1,0:T(8,128)(2,1)}) custom-call(bf16[288,256]{1,0:T(8,128)(2,1)} %get-tuple-element.104.refs_0_, bf16[288,256]{1,0:T(8,128)(2,1)} %copy-done.36, bf16[288,256]{1,0:T(8,128)(2,1)} %copy-done.37, bf16[288,256]{1,0:T(8,128)(2,1)} %copy-done.38, ...), custom_call_target="tpu_custom_call" | custom-call | tf_op jit(solution)/shard_map/pallas_call | solution.py:68
  128.8 3.2 %collective-permute-start.26 = (bf16[48,768]{1,0:T(8,128)(2,1)S(1)}, bf16[48,768]{1,0:T(8,128)(2,1)S(1)}, u32[]{:S(2)}, u32[]{:S(2)}) collective-permute-start(bf16[48,768]{1,0:T(8,128)(2,1)S(1)} %copy-done.63), channel_id=1, source_target_pairs={{0,24},{2,26},{4,28},{6,30},{8,16},{10,18},{12,20},{14,22},{16,8},... | collective-permute-start | bytes 221192 | tf_op jit(solution)/shard_map/ppermute | solution.py:633
  132.2 3.1 %collective-permute-done.26.refs_3_ = bf16[48,768]{1,0:T(8,128)(2,1)S(1)} collective-permute-done((bf16[48,768]{1,0:T(8,128)(2,1)S(1)}, bf16[48,768]{1,0:T(8,128)(2,1)S(1)}, u32[]{:S(2)}, u32[]{:S(2)}) %collective-permute-start.26) | collective-permute-done | bytes 73760 | tf_op jit(solution)/shard_map/ppermute | solution.py:633
  135.3 1.3 collective-permute-done.39.refs_1_
  136.6 1.7 collective-permute-start.41
  138.3 1.7 shard_map.242.refs_0_
  140.0 3.2 %collective-permute-done.40.refs_2_ = bf16[48,768]{1,0:T(8,128)(2,1)S(1)} collective-permute-done((bf16[48,768]{1,0:T(8,128)(2,1)}, bf16[48,768]{1,0:T(8,128)(2,1)S(1)}, u32[]{:S(2)}, u32[]{:S(2)}) %collective-permute-start.40) | collective-permute-done | bytes 73760 | tf_op jit(solution)/shard_map/ppermute | solution.py:633
  143.1 2.6 %collective-permute-start.32 = (bf16[48,768]{1,0:T(8,128)(2,1)}, bf16[48,768]{1,0:T(8,128)(2,1)}, u32[]{:S(2)}, u32[]{:S(2)}) collective-permute-start(bf16[48,768]{1,0:T(8,128)(2,1)} %shard_map.242.refs_0_), channel_id=1, source_target_pairs={{0,24},{2,26},{4,28},{6,30},{8,16},{10,18},{12,20},{14,22},{16,8},... | collective-permute-start | bytes 221192 | tf_op jit(solution)/shard_map/ppermute | solution.py:633
  146.9 2.7 %collective-permute-done.32 = bf16[48,768]{1,0:T(8,128)(2,1)} collective-permute-done((bf16[48,768]{1,0:T(8,128)(2,1)}, bf16[48,768]{1,0:T(8,128)(2,1)}, u32[]{:S(2)}, u32[]{:S(2)}) %collective-permute-start.32) | collective-permute-done | bytes 73760 | tf_op jit(solution)/shard_map/ppermute | solution.py:633
  149.6 2.5 %collective-permute-done.31 = bf16[48,768]{1,0:T(8,128)(2,1)} collective-permute-done((bf16[48,768]{1,0:T(8,128)(2,1)}, bf16[48,768]{1,0:T(8,128)(2,1)}, u32[]{:S(2)}, u32[]{:S(2)}) %collective-permute-start.31) | collective-permute-done | bytes 73760 | tf_op jit(solution)/shard_map/ppermute | solution.py:633
  152.6 5.0 %all-to-all-start.3 = ((bf16[16,16,768]{2,1,0:T(8,128)(2,1)}), bf16[16,16,768]{2,1,0:T(8,128)(2,1)}, u32[]{:S(2)}, u32[]{:S(2)}) async-start(bf16[16,16,768]{2,1,0:T(8,128)(2,1)} %bitcast.8), calls=%async_computation.3 | async-start | bytes 786432 | tf_op jit(solution)/shard_map/all_to_all | solution.py:640
  157.7 1.7 shard_map.245.refs_0_
  159.3 1.9 collective-permute-start.28
  161.2 1.5 collective-permute-start.27
  164.4 3.2 %collective-permute-start.47 = (bf16[48,768]{1,0:T(8,128)(2,1)}, bf16[48,768]{1,0:T(8,128)(2,1)S(1)}, u32[]{:S(2)}, u32[]{:S(2)}) collective-permute-start(bf16[48,768]{1,0:T(8,128)(2,1)} %shard_map.245.refs_0_), channel_id=1, source_target_pairs={{0,24},{2,26},{4,28},{6,30},{8,16},{10,18},{12,20},{14,22},{16,8},... | collective-permute-start | bytes 221192 | tf_op jit(solution)/shard_map/ppermute | solution.py:633
  168.1 1.8 collective-permute-start.45
  170.8 2.8 %shard_map.238 = (f32[256,768]{1,0:T(8,128)}, bf16[32,768]{1,0:T(8,128)(2,1)}) custom-call(bf16[256,768]{1,0:T(8,128)(2,1)} %refs_0_.6, f32[1,768]{1,0:T(1,128)} %reshape.54.refs_2_.refs_1_, bf16[256,768]{1,0:T(8,128)(2,1)} %get-tuple-element.89.refs_2_, bf16[256,768]{1,0:T(8,128)(2,1)} %collective-permute-done.10.refs_3_, ...), custom_call_target="tpu_custom_call" | custom-call | tf_op jit(solution)/shard_map/pallas_call | solution.py:68
  173.7 2.0 collective-permute-start.14
  175.7 2.4 %collective-permute-start.12 = (bf16[32,768]{1,0:T(8,128)(2,1)}, bf16[32,768]{1,0:T(8,128)(2,1)S(1)}, u32[]{:S(2)}, u32[]{:S(2)}) collective-permute-start(bf16[32,768]{1,0:T(8,128)(2,1)} %get-tuple-element.93.refs_0_), channel_id=1, source_target_pairs={{0,8},{2,10},{4,12},{6,14},{8,0},{10,2},{12,4},{14,6},{16,24},{18,... | collective-permute-start | bytes 147464 | tf_op jit(solution)/shard_map/ppermute | solution.py:633
  179.8 1.4 collective-permute-start.35
  182.4 1.5 collective-permute-start.33
  183.9 1.5 shard_map.239
  186.8 1.7 collective-permute-start.17
  191.3 3.3 %shard_map.243 = (f32[768,384]{1,0:T(8,128)}, f32[768,384]{1,0:T(8,128)}) custom-call(bf16[48,768]{1,0:T(8,128)(2,1)} %shard_map.242.refs_0_, bf16[48,768]{1,0:T(8,128)(2,1)} %copy-done.45, bf16[48,768]{1,0:T(8,128)(2,1)} %copy-done.44, bf16[48,768]{1,0:T(8,128)(2,1)} %collective-permute-done.29.refs_3_, bf16[144,768]{1,0:T(8,128)(2,1)} %copy-done.26, ...), custom_call_target="tpu_custom_call" | custom-call | tf_op jit(solution)/shard_map/pallas_call | solution.py:68
  194.6 1.5 collective-permute-start.44
  198.2 1.5 shard_map.240
  199.8 1.4 slice_reduce_fusion
  201.1 1.3 slice_bitcast_fusion.1
  202.4 1.4 slice_bitcast_fusion
  203.8 1.9 fusion
  205.8 1.4 collective-permute-start.50
  207.2 5.0 %convert_add_fusion.refs_9_ = f32[1536,768]{1,0:T(8,128)} fusion(bf16[1536,768]{1,0:T(8,128)(2,1)} %collective-permute-done.52, bf16[256,1536]{1,0:T(8,128)(2,1)} %get-tuple-element.113, bf16[256,768]{1,0:T(8,128)(2,1)S(1)} %copy-done.5), kind=kOutput, calls=%fused_computation | convolution fusion | flops 606339072 | bytes 8257536 | tf_op jit(solution)/shard_map/dot_general | solution.py:35
  214.3 4.7 %convert_add_fusion.1.refs_8_ = f32[768,1536]{1,0:T(8,128)} fusion(bf16[768,1536]{1,0:T(8,128)(2,1)} %collective-permute-done.51, bf16[256,768]{1,0:T(8,128)(2,1)S(1)} %bitcast.32, bf16[256,1536]{1,0:T(8,128)(2,1)S(1)} %copy-done.24), kind=kOutput, calls=%fused_computation.1 | convolution fusion | flops 606339072 | bytes 8257536 | tf_op jit(solution)/shard_map/dot_general | solution.py:35
  220.4 3.2 %shard_map.246 = (f32[768,384]{1,0:T(8,128)}, f32[384,768]{1,0:T(8,128)}) custom-call(bf16[48,768]{1,0:T(8,128)(2,1)} %shard_map.245.refs_0_, bf16[48,768]{1,0:T(8,128)(2,1)} %collective-permute-done.42.refs_1_, bf16[48,768]{1,0:T(8,128)(2,1)} %collective-permute-done.43.refs_2_, bf16[48,768]{1,0:T(8,128)(2,1)} %collective-permute-done.44.refs_3_, ...), custom_call_target="tpu_custom_call" | custom-call | tf_op jit(solution)/shard_map/pallas_call | solution.py:68
  (217 shorter events, 34.5 us)
Async XLA Ops:
  0.6 21.7 %copy-start.59 = (f32[768]{0:T(1024)S(1)}, f32[768]{0:T(1024)}, u32[]{:S(2)}) copy-start(f32[768]{0:T(1024)} %param.21) | copy-start | bytes 9220
  0.7 25.5 %collective-permute-start.1 = (bf16[768,1536]{1,0:T(8,128)(2,1)}, bf16[768,1536]{1,0:T(8,128)(2,1)S(1)}, u32[]{:S(2)}, u32[]{:S(2)}) collective-permute-start(bf16[768,1536]{1,0:T(8,128)(2,1)} %bitcast.36), channel_id=1, source_target_pairs={{0,1},{1,0},{2,3},{3,2},{4,5},{5,4},{6,7},{7,6},{8,9},{9,8},{10,11... | collective-permute-start | bytes 7077896 | tf_op jit(solution)/shard_map/ppermute | solution.py:630
  1.2 25.0 %collective-permute-start.2 = (bf16[1536,768]{1,0:T(8,128)(2,1)}, bf16[1536,768]{1,0:T(8,128)(2,1)}, u32[]{:S(2)}, u32[]{:S(2)}) collective-permute-start(bf16[1536,768]{1,0:T(8,128)(2,1)} %bitcast.38), channel_id=1, source_target_pairs={{0,1},{1,0},{2,3},{3,2},{4,5},{5,4},{6,7},{7,6},{8,9},{9,8},{10,11... | collective-permute-start | bytes 7077896 | tf_op jit(solution)/shard_map/ppermute | solution.py:630
  5.0 21.1 %all-to-all-start = ((bf16[16,16,768]{2,1,0:T(8,128)(2,1)}), bf16[16,16,768]{2,1,0:T(8,128)(2,1)S(1)}, u32[]{:S(2)}, u32[]{:S(2)}) async-start(bf16[16,16,768]{2,1,0:T(8,128)(2,1)} %bitcast.41), calls=%async_computation | async-start | bytes 786432 | tf_op jit(solution)/shard_map/all_to_all | solution.py:640
  22.4 1.9 collective-permute-start
  30.1 18.1 %all-to-all-start.1 = ((bf16[16,16,768]{2,1,0:T(8,128)(2,1)}), bf16[16,16,768]{2,1,0:T(8,128)(2,1)S(1)}, u32[]{:S(2)}, u32[]{:S(2)}) async-start(bf16[16,16,768]{2,1,0:T(8,128)(2,1)} %bitcast.43), calls=%async_computation.1 | async-start | bytes 786432 | tf_op jit(solution)/shard_map/all_to_all | solution.py:640
  51.7 9.1 %collective-permute-start.5 = (bf16[128,768]{1,0:T(8,128)(2,1)}, bf16[128,768]{1,0:T(8,128)(2,1)S(1)}, u32[]{:S(2)}, u32[]{:S(2)}) collective-permute-start(bf16[128,768]{1,0:T(8,128)(2,1)} %get-tuple-element.76), channel_id=1, source_target_pairs={{0,6},{2,4},{4,2},{6,0},{8,14},{10,12},{12,10},{14,8},{16,22},{18,... | collective-permute-start | bytes 589832 | tf_op jit(solution)/shard_map/ppermute | solution.py:633
  52.5 21.0 %collective-permute-start.4 = (bf16[128,768]{1,0:T(8,128)(2,1)}, bf16[128,768]{1,0:T(8,128)(2,1)S(1)}, u32[]{:S(2)}, u32[]{:S(2)}) collective-permute-start(bf16[128,768]{1,0:T(8,128)(2,1)} %get-tuple-element.76), channel_id=1, source_target_pairs={{0,4},{2,6},{4,0},{6,2},{8,12},{10,14},{12,8},{14,10},{16,20},{18,... | collective-permute-start | bytes 589832 | tf_op jit(solution)/shard_map/ppermute | solution.py:633
  53.7 19.8 %collective-permute-start.3 = (bf16[128,768]{1,0:T(8,128)(2,1)}, bf16[128,768]{1,0:T(8,128)(2,1)S(1)}, u32[]{:S(2)}, u32[]{:S(2)}) collective-permute-start(bf16[128,768]{1,0:T(8,128)(2,1)} %get-tuple-element.76), channel_id=1, source_target_pairs={{0,2},{2,0},{4,6},{6,4},{8,10},{10,8},{12,14},{14,12},{16,18},{18,... | collective-permute-start | bytes 589832 | tf_op jit(solution)/shard_map/ppermute | solution.py:633
  55.2 18.4 %collective-permute-start.8 = (bf16[256,384]{1,0:T(8,128)(2,1)}, bf16[256,384]{1,0:T(8,128)(2,1)S(1)}, u32[]{:S(2)}, u32[]{:S(2)}) collective-permute-start(bf16[256,384]{1,0:T(8,128)(2,1)} %get-tuple-element.77.refs_12_), channel_id=1, source_target_pairs={{0,6},{2,4},{4,2},{6,0},{8,14},{10,12},{12,10},{14,8},{16,22},{18,... | collective-permute-start | bytes 589832 | tf_op jit(solution)/shard_map/ppermute | solution.py:633
  56.0 17.6 %collective-permute-start.7 = (bf16[256,384]{1,0:T(8,128)(2,1)}, bf16[256,384]{1,0:T(8,128)(2,1)S(1)}, u32[]{:S(2)}, u32[]{:S(2)}) collective-permute-start(bf16[256,384]{1,0:T(8,128)(2,1)} %get-tuple-element.77.refs_12_), channel_id=1, source_target_pairs={{0,4},{2,6},{4,0},{6,2},{8,12},{10,14},{12,8},{14,10},{16,20},{18,... | collective-permute-start | bytes 589832 | tf_op jit(solution)/shard_map/ppermute | solution.py:633
  60.8 12.9 %collective-permute-start.6 = (bf16[256,384]{1,0:T(8,128)(2,1)}, bf16[256,384]{1,0:T(8,128)(2,1)S(1)}, u32[]{:S(2)}, u32[]{:S(2)}) collective-permute-start(bf16[256,384]{1,0:T(8,128)(2,1)} %get-tuple-element.77.refs_12_), channel_id=1, source_target_pairs={{0,2},{2,0},{4,6},{6,4},{8,10},{10,8},{12,14},{14,12},{16,18},{18,... | collective-permute-start | bytes 589832 | tf_op jit(solution)/shard_map/ppermute | solution.py:633
  77.4 14.2 %all-to-all-start.2 = ((bf16[16,16,768]{2,1,0:T(8,128)(2,1)}), bf16[16,16,768]{2,1,0:T(8,128)(2,1)S(1)}, u32[]{:S(2)}, u32[]{:S(2)}) async-start(bf16[16,16,768]{2,1,0:T(8,128)(2,1)} %bitcast.42), calls=%async_computation.2 | async-start | bytes 786432 | tf_op jit(solution)/shard_map/all_to_all | solution.py:640
  94.7 1.7 collective-permute-start.9
  94.7 14.7 %collective-permute-start.23 = (bf16[128,768]{1,0:T(8,128)(2,1)S(1)}, bf16[128,768]{1,0:T(8,128)(2,1)S(1)}, u32[]{:S(2)}, u32[]{:S(2)}) collective-permute-start(bf16[128,768]{1,0:T(8,128)(2,1)S(1)} %copy-done.7), channel_id=1, source_target_pairs={{0,1},{1,0},{2,3},{3,2},{4,5},{5,4},{6,7},{7,6},{8,9},{9,8},{10,11... | collective-permute-start | bytes 589832 | tf_op jit(solution)/shard_map/ppermute | solution.py:630
  95.2 14.3 %collective-permute-start.22 = (bf16[128,768]{1,0:T(8,128)(2,1)S(1)}, bf16[128,768]{1,0:T(8,128)(2,1)S(1)}, u32[]{:S(2)}, u32[]{:S(2)}) collective-permute-start(bf16[128,768]{1,0:T(8,128)(2,1)S(1)} %copy-done.9), channel_id=1, source_target_pairs={{0,1},{1,0},{2,3},{3,2},{4,5},{5,4},{6,7},{7,6},{8,9},{9,8},{10,11... | collective-permute-start | bytes 589832 | tf_op jit(solution)/shard_map/ppermute | solution.py:630
  95.3 110.5 %collective-permute-start.52 = (bf16[1536,768]{1,0:T(8,128)(2,1)}, bf16[1536,768]{1,0:T(8,128)(2,1)}, u32[]{:S(2)}, u32[]{:S(2)}) collective-permute-start(bf16[1536,768]{1,0:T(8,128)(2,1)} %convolution_convert_fusion.refs_7_), channel_id=1, source_target_pairs={{0,1},{1,0},{2,3},{3,2},{4,5},{5,4},{6,7},{7,6},{8,9},{9,8},{10,11... | collective-permute-start | bytes 7077896 | tf_op jit(solution)/shard_map/ppermute | solution.py:630
  95.7 15.7 %collective-permute-start.21 = (bf16[128,768]{1,0:T(8,128)(2,1)S(1)}, bf16[128,768]{1,0:T(8,128)(2,1)S(1)}, u32[]{:S(2)}, u32[]{:S(2)}) collective-permute-start(bf16[128,768]{1,0:T(8,128)(2,1)S(1)} %copy-done.11), channel_id=1, source_target_pairs={{0,1},{1,0},{2,3},{3,2},{4,5},{5,4},{6,7},{7,6},{8,9},{9,8},{10,11... | collective-permute-start | bytes 589832 | tf_op jit(solution)/shard_map/ppermute | solution.py:630
  100.8 15.6 %copy-start.60 = (bf16[288,256]{1,0:T(8,128)(2,1)S(1)}, bf16[288,256]{1,0:T(8,128)(2,1)}, u32[]{:S(2)}) copy-start(bf16[288,256]{1,0:T(8,128)(2,1)} %get-tuple-element.107) | copy-start | bytes 442372
  100.8 17.1 %copy-start.14 = (bf16[256,768]{1,0:T(8,128)(2,1)S(1)}, bf16[256,768]{1,0:T(8,128)(2,1)}, u32[]{:S(2)}) copy-start(bf16[256,768]{1,0:T(8,128)(2,1)} %get-tuple-element.70.refs_3_) | copy-start | bytes 1179652
  107.9 5.1 %collective-permute-start.18 = (bf16[192,256]{1,0:T(8,128)(2,1)}, bf16[192,256]{1,0:T(8,128)(2,1)S(1)}, u32[]{:S(2)}, u32[]{:S(2)}) collective-permute-start(bf16[192,256]{1,0:T(8,128)(2,1)} %get-tuple-element.95), channel_id=1, source_target_pairs={{0,2},{2,0},{4,6},{6,4},{8,10},{10,8},{12,14},{14,12},{16,18},{18,... | collective-permute-start | bytes 294920 | tf_op jit(solution)/shard_map/ppermute | solution.py:633
  109.4 6.9 %collective-permute-start.19 = (bf16[192,256]{1,0:T(8,128)(2,1)}, bf16[192,256]{1,0:T(8,128)(2,1)S(1)}, u32[]{:S(2)}, u32[]{:S(2)}) collective-permute-start(bf16[192,256]{1,0:T(8,128)(2,1)} %get-tuple-element.96), channel_id=1, source_target_pairs={{0,4},{2,6},{4,0},{6,2},{8,12},{10,14},{12,8},{14,10},{16,20},{18,... | collective-permute-start | bytes 294920 | tf_op jit(solution)/shard_map/ppermute | solution.py:633
  109.5 6.9 %collective-permute-start.20 = (bf16[192,256]{1,0:T(8,128)(2,1)}, bf16[192,256]{1,0:T(8,128)(2,1)S(1)}, u32[]{:S(2)}, u32[]{:S(2)}) collective-permute-start(bf16[192,256]{1,0:T(8,128)(2,1)} %get-tuple-element.97), channel_id=1, source_target_pairs={{0,6},{2,4},{4,2},{6,0},{8,14},{10,12},{12,10},{14,8},{16,22},{18,... | collective-permute-start | bytes 294920 | tf_op jit(solution)/shard_map/ppermute | solution.py:633
  111.5 101.7 %collective-permute-start.51 = (bf16[768,1536]{1,0:T(8,128)(2,1)S(1)}, bf16[768,1536]{1,0:T(8,128)(2,1)}, u32[]{:S(2)}, u32[]{:S(2)}) collective-permute-start(bf16[768,1536]{1,0:T(8,128)(2,1)S(1)} %copy-done.3), channel_id=1, source_target_pairs={{0,1},{1,0},{2,3},{3,2},{4,5},{5,4},{6,7},{7,6},{8,9},{9,8},{10,11... | collective-permute-start | bytes 7077896 | tf_op jit(solution)/shard_map/ppermute | solution.py:630
  113.0 8.8 %collective-permute-start.36 = (bf16[288,256]{1,0:T(8,128)(2,1)S(1)}, bf16[288,256]{1,0:T(8,128)(2,1)S(1)}, u32[]{:S(2)}, u32[]{:S(2)}) collective-permute-start(bf16[288,256]{1,0:T(8,128)(2,1)S(1)} %copy-done.62), channel_id=1, source_target_pairs={{0,2},{2,0},{4,6},{6,4},{8,10},{10,8},{12,14},{14,12},{16,18},{18,... | collective-permute-start | bytes 442376 | tf_op jit(solution)/shard_map/ppermute | solution.py:633
  116.4 7.3 %collective-permute-start.37 = (bf16[288,256]{1,0:T(8,128)(2,1)S(1)}, bf16[288,256]{1,0:T(8,128)(2,1)S(1)}, u32[]{:S(2)}, u32[]{:S(2)}) collective-permute-start(bf16[288,256]{1,0:T(8,128)(2,1)S(1)} %copy-done.61), channel_id=1, source_target_pairs={{0,4},{2,6},{4,0},{6,2},{8,12},{10,14},{12,8},{14,10},{16,20},{18,... | collective-permute-start | bytes 442376 | tf_op jit(solution)/shard_map/ppermute | solution.py:633
  116.4 7.3 %collective-permute-start.38 = (bf16[288,256]{1,0:T(8,128)(2,1)S(1)}, bf16[288,256]{1,0:T(8,128)(2,1)S(1)}, u32[]{:S(2)}, u32[]{:S(2)}) collective-permute-start(bf16[288,256]{1,0:T(8,128)(2,1)S(1)} %copy-done.60), channel_id=1, source_target_pairs={{0,6},{2,4},{4,2},{6,0},{8,14},{10,12},{12,10},{14,8},{16,22},{18,... | collective-permute-start | bytes 442376 | tf_op jit(solution)/shard_map/ppermute | solution.py:633
  121.8 6.4 %collective-permute-start.11 = (f32[24,768]{1,0:T(8,128)S(1)}, f32[24,768]{1,0:T(8,128)S(1)}, u32[]{:S(2)}, u32[]{:S(2)}) collective-permute-start(f32[24,768]{1,0:T(8,128)S(1)} %copy-done.42), channel_id=1, source_target_pairs={{0,1},{1,0},{2,3},{3,2},{4,5},{5,4},{6,7},{7,6},{8,9},{9,8},{10,11... | collective-permute-start | bytes 221192 | tf_op jit(solution)/shard_map/ppermute | solution.py:630
  123.7 8.4 %collective-permute-start.24 = (bf16[48,768]{1,0:T(8,128)(2,1)}, bf16[48,768]{1,0:T(8,128)(2,1)S(1)}, u32[]{:S(2)}, u32[]{:S(2)}) collective-permute-start(bf16[48,768]{1,0:T(8,128)(2,1)} %get-tuple-element.99), channel_id=1, source_target_pairs={{0,8},{2,10},{4,12},{6,14},{8,0},{10,2},{12,4},{14,6},{16,24},{18,... | collective-permute-start | bytes 221192 | tf_op jit(solution)/shard_map/ppermute | solution.py:633
  123.7 8.4 %collective-permute-start.25 = (bf16[48,768]{1,0:T(8,128)(2,1)}, bf16[48,768]{1,0:T(8,128)(2,1)S(1)}, u32[]{:S(2)}, u32[]{:S(2)}) collective-permute-start(bf16[48,768]{1,0:T(8,128)(2,1)} %get-tuple-element.100), channel_id=1, source_target_pairs={{0,16},{2,18},{4,20},{6,22},{8,24},{10,26},{12,28},{14,30},{16,0},... | collective-permute-start | bytes 221192 | tf_op jit(solution)/shard_map/ppermute | solution.py:633
  128.8 6.4 %collective-permute-start.26 = (bf16[48,768]{1,0:T(8,128)(2,1)S(1)}, bf16[48,768]{1,0:T(8,128)(2,1)S(1)}, u32[]{:S(2)}, u32[]{:S(2)}) collective-permute-start(bf16[48,768]{1,0:T(8,128)(2,1)S(1)} %copy-done.63), channel_id=1, source_target_pairs={{0,24},{2,26},{4,28},{6,30},{8,16},{10,18},{12,20},{14,22},{16,8},... | collective-permute-start | bytes 221192 | tf_op jit(solution)/shard_map/ppermute | solution.py:633
  132.0 4.6 %collective-permute-start.39 = (bf16[48,768]{1,0:T(8,128)(2,1)}, bf16[48,768]{1,0:T(8,128)(2,1)S(1)}, u32[]{:S(2)}, u32[]{:S(2)}) collective-permute-start(bf16[48,768]{1,0:T(8,128)(2,1)} %get-tuple-element.109), channel_id=1, source_target_pairs={{0,8},{2,10},{4,12},{6,14},{8,0},{10,2},{12,4},{14,6},{16,24},{18,... | collective-permute-start | bytes 221192 | tf_op jit(solution)/shard_map/ppermute | solution.py:633
  132.1 36.1 %collective-permute-start.10 = (bf16[256,768]{1,0:T(8,128)(2,1)}, bf16[256,768]{1,0:T(8,128)(2,1)}, u32[]{:S(2)}, u32[]{:S(2)}) collective-permute-start(bf16[256,768]{1,0:T(8,128)(2,1)} %get-tuple-element.89.refs_2_), channel_id=1, source_target_pairs={{0,1},{1,0},{2,3},{3,2},{4,5},{5,4},{6,7},{7,6},{8,9},{9,8},{10,11... | collective-permute-start | bytes 1179656 | tf_op jit(solution)/shard_map/ppermute | solution.py:630
  135.3 7.9 %collective-permute-start.40 = (bf16[48,768]{1,0:T(8,128)(2,1)}, bf16[48,768]{1,0:T(8,128)(2,1)S(1)}, u32[]{:S(2)}, u32[]{:S(2)}) collective-permute-start(bf16[48,768]{1,0:T(8,128)(2,1)} %get-tuple-element.110), channel_id=1, source_target_pairs={{0,16},{2,18},{4,20},{6,22},{8,24},{10,26},{12,28},{14,30},{16,0},... | collective-permute-start | bytes 221192 | tf_op jit(solution)/shard_map/ppermute | solution.py:633
  136.6 21.0 %copy-start.47 = (bf16[48,768]{1,0:T(8,128)(2,1)}, bf16[48,768]{1,0:T(8,128)(2,1)S(1)}, u32[]{:S(2)}) copy-start(bf16[48,768]{1,0:T(8,128)(2,1)S(1)} %collective-permute-done.39.refs_1_) | copy-start | bytes 221188
  136.6 9.2 %collective-permute-start.41 = (bf16[48,768]{1,0:T(8,128)(2,1)}, bf16[48,768]{1,0:T(8,128)(2,1)S(1)}, u32[]{:S(2)}, u32[]{:S(2)}) collective-permute-start(bf16[48,768]{1,0:T(8,128)(2,1)} %get-tuple-element.111), channel_id=1, source_target_pairs={{0,24},{2,26},{4,28},{6,30},{8,16},{10,18},{12,20},{14,22},{16,8},... | collective-permute-start | bytes 221192 | tf_op jit(solution)/shard_map/ppermute | solution.py:633
  143.1 6.5 %collective-permute-start.32 = (bf16[48,768]{1,0:T(8,128)(2,1)}, bf16[48,768]{1,0:T(8,128)(2,1)}, u32[]{:S(2)}, u32[]{:S(2)}) collective-permute-start(bf16[48,768]{1,0:T(8,128)(2,1)} %shard_map.242.refs_0_), channel_id=1, source_target_pairs={{0,24},{2,26},{4,28},{6,30},{8,16},{10,18},{12,20},{14,22},{16,8},... | collective-permute-start | bytes 221192 | tf_op jit(solution)/shard_map/ppermute | solution.py:633
  145.8 6.4 %collective-permute-start.31 = (bf16[48,768]{1,0:T(8,128)(2,1)}, bf16[48,768]{1,0:T(8,128)(2,1)}, u32[]{:S(2)}, u32[]{:S(2)}) collective-permute-start(bf16[48,768]{1,0:T(8,128)(2,1)} %shard_map.242.refs_0_), channel_id=1, source_target_pairs={{0,16},{2,18},{4,20},{6,22},{8,24},{10,26},{12,28},{14,30},{16,0},... | collective-permute-start | bytes 221192 | tf_op jit(solution)/shard_map/ppermute | solution.py:633
  149.6 9.7 %collective-permute-start.30 = (bf16[48,768]{1,0:T(8,128)(2,1)}, bf16[48,768]{1,0:T(8,128)(2,1)}, u32[]{:S(2)}, u32[]{:S(2)}) collective-permute-start(bf16[48,768]{1,0:T(8,128)(2,1)} %shard_map.242.refs_0_), channel_id=1, source_target_pairs={{0,8},{2,10},{4,12},{6,14},{8,0},{10,2},{12,4},{14,6},{16,24},{18,... | collective-permute-start | bytes 221192 | tf_op jit(solution)/shard_map/ppermute | solution.py:633
  152.1 9.1 %collective-permute-start.29 = (bf16[48,768]{1,0:T(8,128)(2,1)}, bf16[48,768]{1,0:T(8,128)(2,1)}, u32[]{:S(2)}, u32[]{:S(2)}) collective-permute-start(bf16[48,768]{1,0:T(8,128)(2,1)} %shard_map.242.refs_0_), channel_id=1, source_target_pairs={{0,6},{2,4},{4,2},{6,0},{8,14},{10,12},{12,10},{14,8},{16,22},{18,... | collective-permute-start | bytes 221192 | tf_op jit(solution)/shard_map/ppermute | solution.py:633
  152.6 51.2 %all-to-all-start.3 = ((bf16[16,16,768]{2,1,0:T(8,128)(2,1)}), bf16[16,16,768]{2,1,0:T(8,128)(2,1)}, u32[]{:S(2)}, u32[]{:S(2)}) async-start(bf16[16,16,768]{2,1,0:T(8,128)(2,1)} %bitcast.8), calls=%async_computation.3 | async-start | bytes 786432 | tf_op jit(solution)/shard_map/all_to_all | solution.py:640
  159.3 44.5 %copy-start.12 = (f32[128,768]{1,0:T(8,128)S(1)}, f32[128,768]{1,0:T(8,128)}, u32[]{:S(2)}) copy-start(f32[128,768]{1,0:T(8,128)} %get-tuple-element.68.refs_2_) | copy-start | bytes 1179652
  159.3 5.1 %collective-permute-start.28 = (bf16[48,768]{1,0:T(8,128)(2,1)}, bf16[48,768]{1,0:T(8,128)(2,1)S(1)}, u32[]{:S(2)}, u32[]{:S(2)}) collective-permute-start(bf16[48,768]{1,0:T(8,128)(2,1)} %shard_map.242.refs_0_), channel_id=1, source_target_pairs={{0,4},{2,6},{4,0},{6,2},{8,12},{10,14},{12,8},{14,10},{16,20},{18,... | collective-permute-start | bytes 221192 | tf_op jit(solution)/shard_map/ppermute | solution.py:633
  161.2 6.4 %collective-permute-start.27 = (bf16[48,768]{1,0:T(8,128)(2,1)}, bf16[48,768]{1,0:T(8,128)(2,1)S(1)}, u32[]{:S(2)}, u32[]{:S(2)}) collective-permute-start(bf16[48,768]{1,0:T(8,128)(2,1)} %shard_map.242.refs_0_), channel_id=1, source_target_pairs={{0,2},{2,0},{4,6},{6,4},{8,10},{10,8},{12,14},{14,12},{16,18},{18,... | collective-permute-start | bytes 221192 | tf_op jit(solution)/shard_map/ppermute | solution.py:633
  164.4 26.8 %copy-start.44 = (bf16[48,768]{1,0:T(8,128)(2,1)}, bf16[48,768]{1,0:T(8,128)(2,1)S(1)}, u32[]{:S(2)}) copy-start(bf16[48,768]{1,0:T(8,128)(2,1)S(1)} %collective-permute-done.28.refs_2_) | copy-start | bytes 221188
  164.4 9.3 %collective-permute-start.47 = (bf16[48,768]{1,0:T(8,128)(2,1)}, bf16[48,768]{1,0:T(8,128)(2,1)S(1)}, u32[]{:S(2)}, u32[]{:S(2)}) collective-permute-start(bf16[48,768]{1,0:T(8,128)(2,1)} %shard_map.245.refs_0_), channel_id=1, source_target_pairs={{0,24},{2,26},{4,28},{6,30},{8,16},{10,18},{12,20},{14,22},{16,8},... | collective-permute-start | bytes 221192 | tf_op jit(solution)/shard_map/ppermute | solution.py:633
  167.6 23.7 %copy-start.45 = (bf16[48,768]{1,0:T(8,128)(2,1)}, bf16[48,768]{1,0:T(8,128)(2,1)S(1)}, u32[]{:S(2)}) copy-start(bf16[48,768]{1,0:T(8,128)(2,1)S(1)} %collective-permute-done.27.refs_1_) | copy-start | bytes 221188
  167.6 8.1 %collective-permute-start.46 = (bf16[48,768]{1,0:T(8,128)(2,1)}, bf16[48,768]{1,0:T(8,128)(2,1)S(1)}, u32[]{:S(2)}, u32[]{:S(2)}) collective-permute-start(bf16[48,768]{1,0:T(8,128)(2,1)} %shard_map.245.refs_0_), channel_id=1, source_target_pairs={{0,16},{2,18},{4,20},{6,22},{8,24},{10,26},{12,28},{14,30},{16,0},... | collective-permute-start | bytes 221192 | tf_op jit(solution)/shard_map/ppermute | solution.py:633
  168.1 7.6 %collective-permute-start.45 = (bf16[48,768]{1,0:T(8,128)(2,1)}, bf16[48,768]{1,0:T(8,128)(2,1)S(1)}, u32[]{:S(2)}, u32[]{:S(2)}) collective-permute-start(bf16[48,768]{1,0:T(8,128)(2,1)} %shard_map.245.refs_0_), channel_id=1, source_target_pairs={{0,8},{2,10},{4,12},{6,14},{8,0},{10,2},{12,4},{14,6},{16,24},{18,... | collective-permute-start | bytes 221192 | tf_op jit(solution)/shard_map/ppermute | solution.py:633
  173.7 6.1 %collective-permute-start.14 = (bf16[32,768]{1,0:T(8,128)(2,1)}, bf16[32,768]{1,0:T(8,128)(2,1)S(1)}, u32[]{:S(2)}, u32[]{:S(2)}) collective-permute-start(bf16[32,768]{1,0:T(8,128)(2,1)} %get-tuple-element.93.refs_0_), channel_id=1, source_target_pairs={{0,24},{2,26},{4,28},{6,30},{8,16},{10,18},{12,20},{14,22},{16,8},... | collective-permute-start | bytes 147464 | tf_op jit(solution)/shard_map/ppermute | solution.py:633
  175.7 5.5 %collective-permute-start.13 = (bf16[32,768]{1,0:T(8,128)(2,1)}, bf16[32,768]{1,0:T(8,128)(2,1)S(1)}, u32[]{:S(2)}, u32[]{:S(2)}) collective-permute-start(bf16[32,768]{1,0:T(8,128)(2,1)} %get-tuple-element.93.refs_0_), channel_id=1, source_target_pairs={{0,16},{2,18},{4,20},{6,22},{8,24},{10,26},{12,28},{14,30},{16,0},... | collective-permute-start | bytes 147464 | tf_op jit(solution)/shard_map/ppermute | solution.py:633
  175.7 6.7 %collective-permute-start.12 = (bf16[32,768]{1,0:T(8,128)(2,1)}, bf16[32,768]{1,0:T(8,128)(2,1)S(1)}, u32[]{:S(2)}, u32[]{:S(2)}) collective-permute-start(bf16[32,768]{1,0:T(8,128)(2,1)} %get-tuple-element.93.refs_0_), channel_id=1, source_target_pairs={{0,8},{2,10},{4,12},{6,14},{8,0},{10,2},{12,4},{14,6},{16,24},{18,... | collective-permute-start | bytes 147464 | tf_op jit(solution)/shard_map/ppermute | solution.py:633
  179.8 7.0 %collective-permute-start.35 = (bf16[144,768]{1,0:T(8,128)(2,1)S(1)}, bf16[144,768]{1,0:T(8,128)(2,1)S(1)}, u32[]{:S(2)}, u32[]{:S(2)}) collective-permute-start(bf16[144,768]{1,0:T(8,128)(2,1)S(1)} %constant_dynamic-update-slice_fusion.refs_4_), channel_id=1, source_target_pairs={{0,6},{2,4},{4,2},{6,0},{8,14},{10,12},{12,10},{14,8},{16,22},{18,... | collective-permute-start | bytes 663560 | tf_op jit(solution)/shard_map/ppermute | solution.py:633
  181.2 7.9 %collective-permute-start.34 = (bf16[144,768]{1,0:T(8,128)(2,1)S(1)}, bf16[144,768]{1,0:T(8,128)(2,1)S(1)}, u32[]{:S(2)}, u32[]{:S(2)}) collective-permute-start(bf16[144,768]{1,0:T(8,128)(2,1)S(1)} %constant_dynamic-update-slice_fusion.refs_4_), channel_id=1, source_target_pairs={{0,4},{2,6},{4,0},{6,2},{8,12},{10,14},{12,8},{14,10},{16,20},{18,... | collective-permute-start | bytes 663560 | tf_op jit(solution)/shard_map/ppermute | solution.py:633
  182.4 7.7 %collective-permute-start.33 = (bf16[144,768]{1,0:T(8,128)(2,1)S(1)}, bf16[144,768]{1,0:T(8,128)(2,1)S(1)}, u32[]{:S(2)}, u32[]{:S(2)}) collective-permute-start(bf16[144,768]{1,0:T(8,128)(2,1)S(1)} %constant_dynamic-update-slice_fusion.refs_4_), channel_id=1, source_target_pairs={{0,2},{2,0},{4,6},{6,4},{8,10},{10,8},{12,14},{14,12},{16,18},{18,... | collective-permute-start | bytes 663560 | tf_op jit(solution)/shard_map/ppermute | solution.py:633
  186.8 7.8 %collective-permute-start.17 = (bf16[32,768]{1,0:T(8,128)(2,1)S(1)}, bf16[32,768]{1,0:T(8,128)(2,1)S(1)}, u32[]{:S(2)}, u32[]{:S(2)}) collective-permute-start(bf16[32,768]{1,0:T(8,128)(2,1)S(1)} %convert_element_type.21.refs_0_), channel_id=1, source_target_pairs={{0,6},{2,4},{4,2},{6,0},{8,14},{10,12},{12,10},{14,8},{16,22},{18,... | collective-permute-start | bytes 147464 | tf_op jit(solution)/shard_map/ppermute | solution.py:633
  189.1 7.0 %collective-permute-start.16 = (bf16[32,768]{1,0:T(8,128)(2,1)S(1)}, bf16[32,768]{1,0:T(8,128)(2,1)S(1)}, u32[]{:S(2)}, u32[]{:S(2)}) collective-permute-start(bf16[32,768]{1,0:T(8,128)(2,1)S(1)} %convert_element_type.21.refs_0_), channel_id=1, source_target_pairs={{0,4},{2,6},{4,0},{6,2},{8,12},{10,14},{12,8},{14,10},{16,20},{18,... | collective-permute-start | bytes 147464 | tf_op jit(solution)/shard_map/ppermute | solution.py:633
  190.1 7.0 %collective-permute-start.15 = (bf16[32,768]{1,0:T(8,128)(2,1)S(1)}, bf16[32,768]{1,0:T(8,128)(2,1)S(1)}, u32[]{:S(2)}, u32[]{:S(2)}) collective-permute-start(bf16[32,768]{1,0:T(8,128)(2,1)S(1)} %convert_element_type.21.refs_0_), channel_id=1, source_target_pairs={{0,2},{2,0},{4,6},{6,4},{8,10},{10,8},{12,14},{14,12},{16,18},{18,... | collective-permute-start | bytes 147464 | tf_op jit(solution)/shard_map/ppermute | solution.py:633
  194.6 17.5 %collective-permute-start.44 = (bf16[48,768]{1,0:T(8,128)(2,1)}, bf16[48,768]{1,0:T(8,128)(2,1)}, u32[]{:S(2)}, u32[]{:S(2)}) collective-permute-start(bf16[48,768]{1,0:T(8,128)(2,1)} %shard_map.245.refs_0_), channel_id=1, source_target_pairs={{0,6},{2,4},{4,2},{6,0},{8,14},{10,12},{12,10},{14,8},{16,22},{18,... | collective-permute-start | bytes 221192 | tf_op jit(solution)/shard_map/ppermute | solution.py:633
  196.1 22.8 %collective-permute-start.43 = (bf16[48,768]{1,0:T(8,128)(2,1)}, bf16[48,768]{1,0:T(8,128)(2,1)}, u32[]{:S(2)}, u32[]{:S(2)}) collective-permute-start(bf16[48,768]{1,0:T(8,128)(2,1)} %shard_map.245.refs_0_), channel_id=1, source_target_pairs={{0,4},{2,6},{4,0},{6,2},{8,12},{10,14},{12,8},{14,10},{16,20},{18,... | collective-permute-start | bytes 221192 | tf_op jit(solution)/shard_map/ppermute | solution.py:633
  197.1 21.8 %collective-permute-start.42 = (bf16[48,768]{1,0:T(8,128)(2,1)}, bf16[48,768]{1,0:T(8,128)(2,1)}, u32[]{:S(2)}, u32[]{:S(2)}) collective-permute-start(bf16[48,768]{1,0:T(8,128)(2,1)} %shard_map.245.refs_0_), channel_id=1, source_target_pairs={{0,2},{2,0},{4,6},{6,4},{8,10},{10,8},{12,14},{14,12},{16,18},{18,... | collective-permute-start | bytes 221192 | tf_op jit(solution)/shard_map/ppermute | solution.py:633
  205.8 13.2 %collective-permute-start.50 = (bf16[144,768]{1,0:T(8,128)(2,1)}, bf16[144,768]{1,0:T(8,128)(2,1)S(1)}, u32[]{:S(2)}, u32[]{:S(2)}) collective-permute-start(bf16[144,768]{1,0:T(8,128)(2,1)} %copy-done.27), channel_id=1, source_target_pairs={{0,6},{2,4},{4,2},{6,0},{8,14},{10,12},{12,10},{14,8},{16,22},{18,... | collective-permute-start | bytes 663560 | tf_op jit(solution)/shard_map/ppermute | solution.py:633
  212.2 6.8 %collective-permute-start.49 = (bf16[144,768]{1,0:T(8,128)(2,1)S(1)}, bf16[144,768]{1,0:T(8,128)(2,1)S(1)}, u32[]{:S(2)}, u32[]{:S(2)}) collective-permute-start(bf16[144,768]{1,0:T(8,128)(2,1)S(1)} %copy-done.28), channel_id=1, source_target_pairs={{0,4},{2,6},{4,0},{6,2},{8,12},{10,14},{12,8},{14,10},{16,20},{18,... | collective-permute-start | bytes 663560 | tf_op jit(solution)/shard_map/ppermute | solution.py:633
  213.2 5.9 %collective-permute-start.48 = (bf16[144,768]{1,0:T(8,128)(2,1)S(1)}, bf16[144,768]{1,0:T(8,128)(2,1)S(1)}, u32[]{:S(2)}, u32[]{:S(2)}) collective-permute-start(bf16[144,768]{1,0:T(8,128)(2,1)S(1)} %copy-done.28), channel_id=1, source_target_pairs={{0,2},{2,0},{4,6},{6,4},{8,10},{10,8},{12,14},{14,12},{16,18},{18,... | collective-permute-start | bytes 663560 | tf_op jit(solution)/shard_map/ppermute | solution.py:633
  (57 other events, 277.3 us)
where the time goes:
time: 225 us; the launch traced here: 224 us
  starting transfers between devices  76.6 us (34%)
  Pallas kernels  64.5 us (29%)
  waiting for transfers between devices  44.7 us (20%)
  local copies, waits for them, and re-layouts  19.7 us (9%)
  matrix products  16 us (7%)
    pallas_call x17, Pallas kernels, run(): pl.pallas_call(body, out_shape=[jax.ShapeDtypeStruct(shape, dtype) for sh...  52.3 us
    ppermute x42, starting transfers between devices, hop(): lax.ppermute(item, 'expert', [(at, at ^ distance) for at in range(sources)])  51.7 us
    ppermute x42, waiting for transfers between devices, hop(): lax.ppermute(item, 'expert', [(at, at ^ distance) for at in range(sources)])  23.8 us
    all_to_all x4, starting transfers between devices, exchange(): lax.all_to_all(parts, 'expert', split_axis=0, concat_axis=0, tiled=True)  23.1 us
    all_to_all x4, waiting for transfers between devices, exchange(): lax.all_to_all(parts, 'expert', split_axis=0, concat_axis=0, tiled=True)  19.1 us
    dot_general x4, matrix products, product(): lax.dot_general(left, right, (((left_dim,), (right_dim,)), ((), ())), pre...  14.1 us
    pallas_call x1, Pallas kernels, apply_expert(): pl.pallas_call(functools.partial(expert_kernel, steps=steps), grid=(steps...  12.2 us
    unnamed x135, local copies, waits for them, and re-layouts  12.1 us
  transfers between devices with their start and end apart: 57, of which 19 were waited for; matrix products, arithmetic and copies ran while one was open for 13% of the time, Pallas kernels for 23%

commit v1 on v0

v1 whole, which is shorter than its diff:
```python
import functools

import jax
import jax.numpy as jnp
from jax import lax
from jax.experimental import pallas as pl
from jax.experimental.pallas import tpu as pltpu
from jax.sharding import PartitionSpec as P

EPSILON = 1e-06
BORDERS = (12, 16, 23, 32, 46, 64, 91)
HIGHEST = lax.Precision.HIGHEST
EXCLUDED = -1e30
PLANE = 4
LINE = 4
LOW = jnp.bfloat16
FULL = jnp.float32
GRANT = 56 * 1024 * 1024
LITTLE = 4 * 1024 * 1024


def inverse_rms(rows):
    return lax.rsqrt(jnp.mean(rows * rows, axis=-1, keepdims=True) + EPSILON)


def norm_back(rows, scale_rows, gain, grad_normed):
    scaled = grad_normed * gain
    grad_rows = scale_rows * scaled - rows * scale_rows**3 * jnp.mean(
        scaled * rows, axis=-1, keepdims=True
    )
    grad_gain = jnp.sum(grad_normed * rows * scale_rows, axis=0, keepdims=True)
    return (grad_rows, grad_gain)


def product(left, right, left_dim=1, right_dim=0, precision=None):
    return lax.dot_general(
        left,
        right,
        (((left_dim,), (right_dim,)), ((), ())),
        precision=precision,
        preferred_element_type=FULL,
    )


def wrapped_buckets(bucket_total, columns):
    column = lax.broadcasted_iota(jnp.int32, (bucket_total, columns), 1)
    offset = jnp.where(column < columns // 2, column, column - columns)
    magnitude = jnp.abs(offset)
    bucket = jnp.minimum(magnitude, 8)
    for border in BORDERS:
        bucket = bucket + (magnitude >= border).astype(jnp.int32)
    bucket = bucket + 16 * (offset > 0).astype(jnp.int32)
    rows = lax.broadcasted_iota(jnp.int32, (bucket_total, columns), 0)
    return (bucket == rows).astype(FULL)


class Fetched:
    def __init__(self, ref, copy):
        self.ref = ref
        self.copy = copy
        self.shape = ref.shape

    def ready(self):
        if self.copy is not None:
            self.copy.wait()
            self.copy = None

    def __getitem__(self, index):
        self.ready()
        return self.ref[index]


class Sent:
    def __init__(self, ref, copy):
        self.ref = ref
        self.copy = copy
        self.shape = ref.shape
        self.dtype = ref.dtype
        self.started = False

    def __getitem__(self, index):
        return self.ref[index]

    def __setitem__(self, index, value):
        self.ref[index] = value

    def send(self):
        if not self.started:
            self.copy.start()
            self.started = True


def run(kernel, outs, operands, scratch=(), scalars=0, raw=(), after=(), near=False):
    count, results = len(operands), len(outs)
    brought = [] if near else [at for at in range(scalars, count) if at not in raw]

    def body(*refs):
        refs = list(refs)
        given = refs[:count]
        rest = refs[count + len(after) :]
        targets, rest = rest[:results], rest[results:]
        if near:
            kernel(*given, *targets, *rest)
            return
        own, rest = rest[: len(scratch)], rest[len(scratch) :]
        buffers, rest = rest[: len(brought)], rest[len(brought) :]
        built, (arrived, left) = rest[:results], rest[results:]
        for slot, (at, buffer) in enumerate(zip(brought, buffers)):
            copy = pltpu.make_async_copy(given[at], buffer, arrived.at[slot])
            copy.start()
            given[at] = Fetched(buffer, copy)
        sent = [
            Sent(buffer, pltpu.make_async_copy(buffer, target, left.at[slot]))
            for slot, (buffer, target) in enumerate(zip(built, targets))
        ]
        kernel(*given, *sent, *own)
        for at in brought:
            given[at].ready()
        for item in sent:
            item.send()
        for item in sent:
            item.copy.wait()

    anywhere = pl.BlockSpec(memory_space=pl.ANY)
    placed = pl.BlockSpec(memory_space=pltpu.VMEM) if near else anywhere
    in_specs = [pl.BlockSpec(memory_space=pltpu.SMEM)] * scalars
    in_specs += [placed] * (count - scalars) + [anywhere] * len(after)
    scratch_shapes = list(scratch)
    if not near:
        scratch_shapes += [pltpu.VMEM(operands[at].shape, operands[at].dtype) for at in brought]
        scratch_shapes += [pltpu.VMEM(shape, dtype) for shape, dtype in outs]
        scratch_shapes += [pltpu.SemaphoreType.DMA((len(brought),))]
        scratch_shapes += [pltpu.SemaphoreType.DMA((results,))]
    return pl.pallas_call(
        body,
        out_shape=[jax.ShapeDtypeStruct(shape, dtype) for shape, dtype in outs],
        in_specs=in_specs,
        out_specs=[placed] * results,
        scratch_shapes=scratch_shapes,
        compiler_params=pltpu.CompilerParams(vmem_limit_bytes=LITTLE if near else GRANT),
        cost_estimate=pl.CostEstimate(flops=0, bytes_accessed=0, transcendentals=0),
    )(*operands, *after)


def placed_rows(chosen, experts, capacity, slots):
    own_rows = chosen.shape[1]
    picked = chosen == lax.broadcasted_iota(jnp.int32, (experts, own_rows), 0)
    picked_float = picked.astype(FULL)
    earlier = lax.broadcasted_iota(jnp.int32, (own_rows, own_rows), 0) < lax.broadcasted_iota(
        jnp.int32, (own_rows, own_rows), 1
    )
    ranks = product(picked_float.astype(LOW), earlier.astype(FULL).astype(LOW))
    rank = jnp.sum(ranks * picked_float, axis=0, keepdims=True)
    target = chosen * capacity + rank.astype(jnp.int32)
    place = target == lax.broadcasted_iota(jnp.int32, (slots, own_rows), 0)
    return place.astype(FULL).astype(LOW)


def forward_kernel(
    lengths_ref,
    tokens_ref,
    gain_ref,
    query_ref,
    key_ref,
    value_ref,
    table_ref,
    output_ref,
    own_ref,
    other_ref,
    qkv_ref,
    probs_ref,
    normed_turned_ref,
    mixed_ref,
    whole_ref,
    *,
    head_size,
):
    group_rows = tokens_ref.shape[0]
    own_rows = own_ref.shape[0]
    heads, buckets = table_ref.shape
    columns = heads * head_size
    scale = head_size ** (-0.5)
    half = lax.axis_index("shard")
    own_at = pl.multiple_of(half * own_rows, own_rows)
    other_at = pl.multiple_of((1 - half) * own_rows, own_rows)
    inputs = tokens_ref[...].astype(FULL)
    normed = inputs * inverse_rms(inputs) * gain_ref[...].reshape(1, -1)
    whole_ref[...] = normed
    normed_turned_ref[0:own_rows, :] = whole_ref[pl.ds(own_at, own_rows), :].astype(LOW)
    normed_turned_ref[own_rows:, :] = whole_ref[pl.ds(other_at, own_rows), :].astype(LOW)
    normed = normed.astype(LOW)
    queries = product(normed, query_ref[...]).astype(LOW)
    keys = product(normed, key_ref[...]).astype(LOW)
    values = product(normed, value_ref[...]).astype(LOW)
    qkv_ref[:, 0:columns] = queries
    qkv_ref[:, columns : 2 * columns] = keys
    qkv_ref[:, 2 * columns : 3 * columns] = values
    qkv_ref.send()
    normed_turned_ref.send()
    per_offset = product(
        table_ref[...], wrapped_buckets(buckets, group_rows), 1, 0, HIGHEST
    )
    row_at = lax.broadcasted_iota(jnp.int32, (group_rows, group_rows), 0)
    column_at = lax.broadcasted_iota(jnp.int32, (group_rows, group_rows), 1)
    row_part = jnp.zeros((group_rows, group_rows), jnp.int32)
    column_part = jnp.zeros((group_rows, group_rows), jnp.int32)
    end = 0
    for part in range(lengths_ref.shape[1] - 1):
        end = end + lengths_ref[0, part]
        row_part = row_part + (row_at >= end).astype(jnp.int32)
        column_part = column_part + (column_at >= end).astype(jnp.int32)
    same = row_part == column_part
    mixed_parts = []
    for head in range(heads):
        here = slice(head * head_size, (head + 1) * head_size)
        bias = pltpu.roll(
            jnp.broadcast_to(per_offset[head : head + 1, :], (group_rows, group_rows)),
            0,
            1,
            stride=1,
            stride_axis=0,
        )
        scores = product(queries[:, here], keys[:, here], 1, 1)
        scores = jnp.where(same, scores * scale + bias, EXCLUDED)
        raised = jnp.exp(scores - jnp.max(scores, axis=-1, keepdims=True))
        probs = raised * (1.0 / jnp.sum(raised, axis=-1, keepdims=True))
        probs = probs.astype(LOW)
        probs_ref[head] = probs
        mixed_parts.append(product(probs, values[:, here]))
    probs_ref.send()
    mixed = jnp.concatenate(mixed_parts, axis=1).astype(LOW)
    mixed_ref[...] = mixed
    mixed_ref.send()
    whole_ref[...] = product(mixed, output_ref[...])
    own_ref[...] = whole_ref[pl.ds(own_at, own_rows), :]
    other_ref[...] = whole_ref[pl.ds(other_at, own_rows), :]


def hidden_kernel(
    routes_ref,
    cotangent_ref,
    tokens_ref,
    own_ref,
    gain_ref,
    normed_ref,
    came_ref,
    place_ref,
    hidden_ref,
    sent_ref,
    normed_own_ref,
    *,
    experts,
    capacity,
):
    own_rows, width = own_ref.shape
    slots = place_ref.shape[0]
    place = placed_rows(routes_ref[...], experts, capacity, slots)
    place_ref[...] = place
    place_ref.send()
    sent_ref[:, width:] = product(place, cotangent_ref[...]).astype(LOW)
    own_at = pl.multiple_of(lax.axis_index("shard") * own_rows, own_rows)
    inputs = tokens_ref[pl.ds(own_at, own_rows), :].astype(FULL)
    hidden = inputs + (own_ref[...] + came_ref[...])
    normed = (hidden * inverse_rms(hidden) * gain_ref[...].reshape(1, -1)).astype(LOW)
    sent_ref[:, 0:width] = product(place, normed).astype(LOW)
    sent_ref.send()
    hidden_ref[...] = hidden
    normed_own_ref[...] = normed_ref[0:own_rows, :]


def expert_kernel(
    arrived_ref,
    router_ref,
    in_own_ref,
    out_own_ref,
    in_came_ref,
    out_came_ref,
    back_ref,
    grad_back_ref,
    grad_router_ref,
    rows_ref,
    grad_produced_ref,
    active_own_ref,
    active_came_ref,
    grad_pre_own_ref,
    grad_pre_came_ref,
    in_held_ref,
    out_held_ref,
    arrived,
):
    width, units = in_own_ref.shape
    copies = [
        pltpu.make_async_copy(source, target, arrived.at[at])
        for at, (source, target) in enumerate(
            (
                (in_own_ref, in_held_ref.at[0]),
                (out_own_ref, out_held_ref.at[0]),
                (in_came_ref, in_held_ref.at[1]),
                (out_came_ref, out_held_ref.at[1]),
            )
        )
    ]
    for copy in copies:
        copy.start()
    rows = arrived_ref[:, 0:width]
    grads = arrived_ref[:, width:].astype(FULL)
    rows_ref[...] = rows
    rows_ref.send()
    logits = product(rows, router_ref[...], 1, 1)
    raised = jnp.exp(logits - jnp.max(logits, axis=-1, keepdims=True))
    chances = raised * (1.0 / jnp.sum(raised, axis=-1, keepdims=True))
    chosen = lax.broadcasted_iota(jnp.int32, chances.shape, 1) == lax.axis_index("expert")
    gate = jnp.sum(jnp.where(chosen, chances, 0.0), axis=1, keepdims=True)
    grad_produced = (gate * grads).astype(LOW)
    grad_produced_ref[...] = grad_produced
    grad_produced_ref.send()
    produced = 0.0
    grad_rows = 0.0
    block = 512
    for source in range(2):
        copies[2 * source].wait()
        copies[2 * source + 1].wait()
        active_ref = (active_own_ref, active_came_ref)[source]
        grad_pre_ref = (grad_pre_own_ref, grad_pre_came_ref)[source]
        for first in range(0, units, block):
            here = slice(first, first + block)
            in_block = in_held_ref[source, :, here]
            out_block = out_held_ref[source, here, :]
            pre = product(rows, in_block)
            grad_active = product(grad_produced, out_block, 1, 1)
            steep = 1.0 / (1.0 + 0.2316419 * jnp.abs(pre))
            density = jnp.exp(-0.5 * pre * pre) * 0.3989422804014327
            tail = 1.330274429
            for factor in (-1.821255978, 1.781477937, -0.356563782, 0.319381530):
                tail = tail * steep + factor
            tail = tail * steep * density
            cumulative = jnp.where(pre >= 0.0, 1.0 - tail, tail)
            active = (pre * cumulative).astype(LOW)
            grad_pre = (grad_active * (cumulative + pre * density)).astype(LOW)
            active_ref[:, here] = active
            grad_pre_ref[:, here] = grad_pre
            produced = produced + product(active, out_block)
            grad_rows = grad_rows + product(grad_pre, in_block, 1, 1)
        active_ref.send()
        grad_pre_ref.send()
    produced = produced.astype(LOW).astype(FULL)
    grad_gate = jnp.sum(grads * produced, axis=1, keepdims=True)
    grad_logits = (grad_gate * chances * (chosen.astype(FULL) - gate)).astype(LOW)
    grad_back_ref[...] = (grad_rows + product(grad_logits, router_ref[...])).astype(LOW)
    grad_back_ref.send()
    back_ref[...] = (gate * produced).astype(LOW)
    grad_router_ref[...] = product(grad_logits, rows, 0, 0)


def grad_hidden_kernel(
    place_ref,
    returned_ref,
    hidden_ref,
    gain_ref,
    cotangent_ref,
    grad_router_ref,
    attention_ref,
    small_ref,
):
    experts = grad_router_ref.shape[0]
    width = hidden_ref.shape[1]
    hidden = hidden_ref[...]
    grad_normed = product(place_ref[...], returned_ref[...], 0, 0)
    grad_rows, grad_gain = norm_back(hidden, inverse_rms(hidden), gain_ref[...].reshape(1, -1), grad_normed)
    attention_ref[...] = (cotangent_ref[...].astype(FULL) + grad_rows).astype(LOW)
    small_ref[0:experts, :] = grad_router_ref[...]
    small_ref[experts:, :] = jnp.concatenate(
        [grad_gain, jnp.zeros((small_ref.shape[0] - experts - 1, width), FULL)], axis=0
    )


def halves(own_rows):
    half = lax.axis_index("shard")
    own_at = pl.multiple_of(half * own_rows, own_rows)
    other_at = pl.multiple_of((1 - half) * own_rows, own_rows)
    return (own_at, other_at)


def attention_back_kernel(
    attention_own_ref,
    attention_came_ref,
    output_ref,
    mixed_ref,
    qkv_ref,
    probs_ref,
    query_ref,
    key_ref,
    value_ref,
    back_ref,
    grad_normed_ref,
    grad_table_ref,
    back_out_ref,
    part_ref,
    part_one_ref,
    part_two_ref,
    part_three_ref,
    attention_ref,
    grads_ref,
    turned_ref,
    output_grad_ref,
    *,
    head_size,
    bucket_total,
):
    own_rows, width = attention_own_ref.shape
    group_rows = 2 * own_rows
    heads = probs_ref.shape[0]
    columns = heads * head_size
    scale = head_size ** (-0.5)
    own_at, other_at = halves(own_rows)
    attention_ref[pl.ds(own_at, own_rows), :] = attention_own_ref[...]
    attention_ref[pl.ds(other_at, own_rows), :] = attention_came_ref[...]
    grad_mixed = product(attention_ref[...], output_ref[...], 1, 1).astype(LOW)
    output_grad_ref[...] = product(mixed_ref[...], attention_ref[...], 0, 0)
    reversal = (
        lax.broadcasted_iota(jnp.int32, (group_rows, group_rows), 0)
        + lax.broadcasted_iota(jnp.int32, (group_rows, group_rows), 1)
        == group_rows - 1
    )
    reversal = reversal.astype(FULL).astype(LOW)
    grad_queries, grad_keys, grad_values, sums = [], [], [], []
    for head in range(heads):
        first = head * head_size
        queries = qkv_ref[:, first : first + head_size]
        keys = qkv_ref[:, columns + first : columns + first + head_size]
        values = qkv_ref[:, 2 * columns + first : 2 * columns + first + head_size]
        probs = probs_ref[head].astype(FULL)
        grad_head = grad_mixed[:, first : first + head_size]
        grad_probs = product(grad_head, values, 1, 1)
        inner = jnp.sum(probs * grad_probs, axis=-1, keepdims=True)
        grad_scores = probs * (grad_probs - inner)
        upper = grad_scores.astype(LOW)
        rest = (grad_scores - upper.astype(FULL)).astype(LOW)
        backwards = product(reversal, upper) + product(reversal, rest)
        aligned = pltpu.roll(backwards, 1, 1, stride=1, stride_axis=0)
        sums.append(jnp.sum(aligned, axis=0, keepdims=True))
        grad_queries.append(product(upper, keys) * scale)
        grad_keys.append(product(upper, queries, 0, 0) * scale)
        grad_values.append(product(probs_ref[head], grad_head, 0, 0))
    grad_table_ref[...] = product(
        jnp.concatenate(sums, axis=0), wrapped_buckets(bucket_total, group_rows), 1, 1, HIGHEST
    )
    grad_queries = jnp.concatenate(grad_queries, axis=1)
    grad_keys = jnp.concatenate(grad_keys, axis=1)
    grad_values = jnp.concatenate(grad_values, axis=1)
    grads_ref[:, 0:columns] = grad_values
    grads_ref[:, columns : 2 * columns] = grad_queries
    grads_ref[:, 2 * columns : 3 * columns] = grad_keys
    turned_ref[:, 0:own_rows] = grads_ref[pl.ds(own_at, own_rows), :].T
    turned_ref[:, own_rows:] = grads_ref[pl.ds(other_at, own_rows), :].T
    mine = lax.rem(lax.axis_index("expert"), PLANE)
    rows = columns // PLANE
    refs = (part_ref, part_one_ref, part_two_ref, part_three_ref)
    for other, ref in enumerate(refs):
        for weight in range(3):
            at = pl.multiple_of((mine ^ other) * rows + weight * columns, 16)
            ref[weight * rows : (weight + 1) * rows, :] = turned_ref[pl.ds(at, rows), :].astype(
                LOW
            )
        at = pl.multiple_of((mine ^ other) * rows, 16)
        quarter = output_grad_ref[pl.ds(at, rows), :].astype(LOW)
        for piece in range(width // group_rows):
            ref[(3 + piece) * rows : (4 + piece) * rows, :] = quarter[
                :, piece * group_rows : (piece + 1) * group_rows
            ]
        ref.send()
    back_out_ref[...] = back_ref[...]
    back_out_ref.send()
    grad_normed = product(grad_queries.astype(LOW), query_ref[...], 1, 1)
    grad_normed = grad_normed + product(grad_keys.astype(LOW), key_ref[...], 1, 1)
    grad_normed = grad_normed + product(grad_values.astype(LOW), value_ref[...], 1, 1)
    grad_normed_ref[...] = grad_normed.astype(LOW)


def grad_tokens_kernel(
    tokens_ref,
    gain_ref,
    normed_own_ref,
    normed_came_ref,
    attention_own_ref,
    attention_came_ref,
    small_own_ref,
    small_came_ref,
    table_ref,
    grad_tokens_ref,
    small_ref,
):
    own_rows = attention_own_ref.shape[0]
    width = tokens_ref.shape[1]
    heads, buckets = table_ref.shape
    half = lax.axis_index("shard")
    own_at = pl.multiple_of(half * own_rows, own_rows)
    other_at = pl.multiple_of((1 - half) * own_rows, own_rows)
    inputs = tokens_ref[...].astype(FULL)
    grad_normed = normed_own_ref[...].astype(FULL) + normed_came_ref[...].astype(FULL)
    grad_rows, grad_gain = norm_back(inputs, inverse_rms(inputs), gain_ref[...].reshape(1, -1), grad_normed)
    grad_tokens_ref[...] = grad_rows
    grad_tokens_ref[pl.ds(own_at, own_rows), :] += attention_own_ref[...].astype(FULL)
    grad_tokens_ref[pl.ds(other_at, own_rows), :] += attention_came_ref[...].astype(FULL)
    summed = small_own_ref[...] + small_came_ref[...]
    table = jnp.concatenate([table_ref[...], jnp.zeros((heads, width - buckets), FULL)], axis=1)
    more = small_ref.shape[0] - summed.shape[0] - heads - 1
    small_ref[...] = jnp.concatenate(
        [summed, grad_gain, table, jnp.zeros((more, width), FULL)], axis=0
    ).astype(small_ref.dtype)


def line_chunks(totals, refs, total_refs, shared=()):
    mine = lax.rem(lax.axis_index("expert") // PLANE, LINE)
    for total, total_ref in zip(totals, total_refs):
        total_ref[...] = total
    for other, ref in enumerate(refs):
        chunks = []
        for total_ref in total_refs:
            rows = total_ref.shape[0] // LINE
            at = pl.multiple_of((mine ^ other) * rows, 8)
            chunks.append(total_ref[pl.ds(at, rows), :])
        ref[...] = jnp.concatenate(chunks + list(shared), axis=0).astype(ref.dtype)
        ref.send()


def sums_kernel(*refs):
    parts, nears, fars, normed_ref, small_ref = refs[0:4], refs[4:7], refs[7:10], *refs[10:12]
    outs, total_refs = refs[12:16], refs[16:20]
    own_rows = normed_ref.shape[0] // 2
    rows = total_refs[0].shape[0]
    pieces = normed_ref.shape[1] // parts[0].shape[1]
    output = 0.0
    weights = 0.0
    for at, part in enumerate(parts):
        output = output + jnp.concatenate(
            [part[(3 + piece) * rows : (4 + piece) * rows, :] for piece in range(pieces)], axis=1
        ).astype(FULL)
        near = nears[at - 1][...] if at else normed_ref[0:own_rows]
        far = fars[at - 1][...] if at else normed_ref[own_rows:]
        weights = weights + product(part[0 : 3 * rows, 0:own_rows], near)
        weights = weights + product(part[0 : 3 * rows, own_rows:], far)
    totals = (weights[0:rows], weights[rows : 2 * rows], weights[2 * rows :], output)
    line_chunks(totals, outs, total_refs, (small_ref[...].astype(FULL),))


def summed(refs, rows=slice(None)):
    near = refs[0][rows, :].astype(FULL) + refs[1][rows, :].astype(FULL)
    far = refs[2][rows, :].astype(FULL) + refs[3][rows, :].astype(FULL)
    return near + far


def line_sum_kernel(*refs):
    total = summed(refs[0:LINE])
    for out_ref in refs[LINE:]:
        out_ref[...] = total[0 : out_ref.shape[0]].astype(out_ref.dtype)


def assemble_kernel(*refs):
    chunk_refs = refs[0 : PLANE * LINE]
    value_ref, query_ref, key_ref, output_ref, router_ref, ffn_ref, attn_ref, table_ref = refs[
        PLANE * LINE : -3
    ]
    totals = refs[-3:] + (output_ref.ref,)
    member = lax.rem(lax.axis_index("expert"), PLANE)
    floor = lax.rem(lax.axis_index("expert") // PLANE, LINE)
    rows = output_ref.shape[0] // PLANE // LINE
    for along in range(LINE):
        for across in range(PLANE):
            chunk = chunk_refs[along * PLANE + across][0 : 4 * rows, :].astype(FULL)
            at = pl.multiple_of(((member ^ across) * LINE + (floor ^ along)) * rows, 8)
            for weight, total_ref in enumerate(totals):
                total_ref[pl.ds(at, rows), :] = chunk[weight * rows : (weight + 1) * rows]
    output_ref.send()
    for total_ref, ref in zip(totals, (value_ref, query_ref, key_ref)):
        ref[...] = total_ref[...].T
        ref.send()
    small = summed(chunk_refs[0:PLANE], slice(4 * rows, None))
    experts = router_ref.shape[0]
    heads, buckets = table_ref.shape
    late = -(-(experts + 1) // 8) * 8
    router_ref[...] = small[0:experts]
    ffn_ref[...] = small[experts : experts + 1].reshape(-1)
    attn_ref[...] = small[late : late + 1].reshape(-1)
    table_ref[...] = small[late + 1 : late + 1 + heads, 0:buckets]


def expert_grads_kernel(
    rows_ref,
    rows_far_ref,
    grad_produced_ref,
    grad_produced_far_ref,
    active_ref,
    active_far_ref,
    grad_pre_ref,
    grad_pre_far_ref,
    grad_in_ref,
    grad_out_ref,
    done_ref,
):
    done_ref[...] = jnp.zeros_like(done_ref)
    grad_in_ref[...] = product(rows_ref[...], grad_pre_ref[...], 0, 0) + product(
        rows_far_ref[...], grad_pre_far_ref[...], 0, 0
    )
    grad_out_ref[...] = product(active_ref[...], grad_produced_ref[...], 0, 0) + product(
        active_far_ref[...], grad_produced_far_ref[...], 0, 0
    )


def expert_grads(rows, rows_far, grad_produced, grad_produced_far, *wide):
    slots, width = rows.shape
    units = wide[0].shape[1]
    block = 768
    fixed = pl.BlockSpec((slots, width), lambda step: (0, 0))
    moving = pl.BlockSpec((slots, block), lambda step: (0, step))
    return pl.pallas_call(
        expert_grads_kernel,
        grid=(units // block,),
        out_shape=[
            jax.ShapeDtypeStruct((width, units), FULL),
            jax.ShapeDtypeStruct((units, width), FULL),
            jax.ShapeDtypeStruct((8, 128), FULL),
        ],
        in_specs=[fixed] * 4 + [moving] * 4,
        out_specs=[
            pl.BlockSpec((width, block), lambda step: (0, step)),
            pl.BlockSpec((block, width), lambda step: (step, 0)),
            pl.BlockSpec((8, 128), lambda step: (0, 0)),
        ],
        compiler_params=pltpu.CompilerParams(vmem_limit_bytes=GRANT),
        cost_estimate=pl.CostEstimate(flops=0, bytes_accessed=0, transcendentals=0),
    )(rows, rows_far, grad_produced, grad_produced_far, *wide)


def block_out_kernel(place_ref, returned_ref, hidden_ref, out_ref):
    out_ref[...] = (
        hidden_ref[...] + product(place_ref[...], returned_ref[...], 0, 0)
    ).astype(LOW)


def shards(
    tokens,
    attn_gain,
    query_weight,
    key_weight,
    value_weight,
    output_weight,
    bias_table,
    ffn_gain,
    router_weight,
    expert_in,
    expert_out,
    routes,
    lengths,
    cotangent,
):
    group_rows, width = tokens.shape
    own_rows = cotangent.shape[0]
    heads = bias_table.shape[1]
    buckets = bias_table.shape[0]
    columns = query_weight.shape[1]
    head_size = columns // heads
    sources = lax.axis_size("expert")
    experts = router_weight.shape[1]
    capacity = 2 * own_rows // experts
    slots = experts * capacity
    beyond = sources // (PLANE * LINE)
    router_rows = router_weight.T

    def swap(item):
        return lax.ppermute(item, "shard", [(0, 1), (1, 0)])

    def hop(item, distance):
        return lax.ppermute(item, "expert", [(at, at ^ distance) for at in range(sources)])

    def around(items, stride):
        return tuple(hop(item, stride * (step + 1)) for step, item in enumerate(items))

    def exchange(rows):
        parts = rows.reshape(sources, slots // sources, rows.shape[1])
        came = lax.all_to_all(parts, "expert", split_axis=0, concat_axis=0, tiled=True)
        return came.reshape(rows.shape)

    def beyond_sum(item):
        if beyond == 1:
            return item
        groups = [
            [near + PLANE * LINE * far for far in range(beyond)] for near in range(PLANE * LINE)
        ]
        return lax.psum(item, "expert", axis_index_groups=groups)

    in_own, out_own = expert_in[0], expert_out[0]
    in_came, out_came = swap(in_own), swap(out_own)
    own, other, qkv, probs, normed, mixed = run(
        functools.partial(forward_kernel, head_size=head_size),
        [
            ((own_rows, width), FULL),
            ((own_rows, width), FULL),
            ((group_rows, 3 * columns), LOW),
            ((heads, group_rows, group_rows), LOW),
            ((group_rows, width), LOW),
            ((group_rows, columns), LOW),
        ],
        (
            lengths,
            tokens,
            attn_gain,
            query_weight,
            key_weight,
            value_weight,
            bias_table.T,
            output_weight,
        ),
        scratch=(pltpu.VMEM((group_rows, width), FULL),),
        scalars=1,
    )
    place, hidden, sent, normed_own = run(
        functools.partial(hidden_kernel, experts=experts, capacity=capacity),
        [
            ((slots, own_rows), LOW),
            ((own_rows, width), FULL),
            ((slots, 2 * width), LOW),
            ((own_rows, width), LOW),
        ],
        (routes.reshape(1, own_rows), cotangent, tokens, own, ffn_gain, normed, swap(other)),
    )
    normed_near = around((normed_own,) * 3, 1)
    (
        back,
        grad_back,
        grad_router,
        rows,
        grad_produced,
        active_own,
        active_came,
        grad_pre_own,
        grad_pre_came,
    ) = run(
        expert_kernel,
        [
            ((slots, width), LOW),
            ((slots, width), LOW),
            ((experts, width), FULL),
            ((slots, width), LOW),
            ((slots, width), LOW),
        ]
        + [((slots, in_own.shape[1]), LOW)] * 4,
        (exchange(sent), router_rows, in_own, out_own, in_came, out_came),
        scratch=(
            pltpu.VMEM((2, *in_own.shape), LOW),
            pltpu.VMEM((2, *out_own.shape), LOW),
            pltpu.SemaphoreType.DMA((4,)),
        ),
        raw=(2, 3, 4, 5),
        after=normed_near,
    )
    returned_grads = exchange(grad_back)
    rows_far, grad_produced_far = swap(rows), swap(grad_produced)
    active_far, grad_pre_far = swap(active_came), swap(grad_pre_came)
    small_rows = -(-(experts + 1) // 8) * 8
    attention_own, small_own = run(
        grad_hidden_kernel,
        [((own_rows, width), LOW), ((small_rows, width), FULL)],
        (place, returned_grads, hidden, ffn_gain, cotangent, grad_router),
        after=(rows_far, grad_produced_far, active_far, grad_pre_far),
    )
    attention_came = swap(attention_own)
    part_rows = columns // PLANE
    grad_normed_own, grad_table, back, *parts = run(
        functools.partial(attention_back_kernel, head_size=head_size, bucket_total=buckets),
        [((group_rows, width), LOW), ((heads, buckets), FULL), ((slots, width), LOW)]
        + [((part_rows * (3 + width // group_rows), group_rows), LOW)] * PLANE,
        (
            attention_own,
            attention_came,
            output_weight,
            mixed,
            qkv,
            probs,
            query_weight,
            key_weight,
            value_weight,
            back,
        ),
        scratch=(
            pltpu.VMEM((group_rows, width), LOW),
            pltpu.VMEM((group_rows, 3 * columns), FULL),
            pltpu.VMEM((3 * columns, group_rows), FULL),
            pltpu.VMEM((columns, width), FULL),
        ),
    )
    parts = (parts[0],) + around(parts[1:], 1)
    grad_normed_came = swap(grad_normed_own)
    small_came = swap(small_own)
    normed_far = tuple(swap(item) for item in normed_near)
    late_rows = -(-(heads + 1) // 8) * 8
    grad_tokens, small = run(
        grad_tokens_kernel,
        [((group_rows, width), FULL), ((small_rows + late_rows, width), LOW)],
        (
            tokens,
            attn_gain,
            grad_normed_own,
            grad_normed_came,
            attention_own,
            attention_came,
            small_own,
            small_came,
            grad_table,
        ),
    )
    returned = exchange(back)
    grad_expert_in, grad_expert_out, done = expert_grads(
        rows,
        rows_far,
        grad_produced,
        grad_produced_far,
        active_own,
        active_far,
        grad_pre_own,
        grad_pre_far,
    )
    chunk_rows = 4 * part_rows // LINE
    all_rows = chunk_rows + small_rows + late_rows
    chunks = run(
        sums_kernel,
        [((all_rows, width), LOW)] * LINE,
        parts + normed_near + normed_far + (normed, small),
        scratch=(pltpu.VMEM((part_rows, width), FULL),) * 4,
        after=(returned,),
    )
    (block_out,) = run(
        block_out_kernel, [((own_rows, width), LOW)], (place, returned, hidden)
    )
    chunks = (chunks[0],) + around(chunks[1:], PLANE)
    if beyond == 1:
        whole, chunk = run(
            line_sum_kernel,
            [((all_rows, width), LOW), ((chunk_rows, width), LOW)],
            chunks,
            near=True,
            after=(done,),
        )
    else:
        (whole,) = run(line_sum_kernel, [((all_rows, width), FULL)], chunks)
        whole = beyond_sum(whole).astype(LOW)
        chunk = whole[0:chunk_rows]
    gathered = (whole,) + around((whole,) * 3, 1)
    for item in around((chunk,) * 3, PLANE):
        gathered += (item,) + around((item,) * 3, 1)
    (
        grad_value,
        grad_query,
        grad_key,
        grad_output,
        grad_router,
        grad_ffn_gain,
        grad_attn_gain,
        grad_table,
    ) = run(
        assemble_kernel,
        [((width, columns), FULL)] * 3
        + [((columns, width), FULL), ((experts, width), FULL), ((width,), FULL), ((width,), FULL)]
        + [((heads, buckets), FULL)],
        gathered,
        scratch=(pltpu.VMEM((columns, width), FULL),) * 3,
    )
    grad_router = grad_router.T
    grad_table = grad_table.T
    return (
        block_out,
        grad_tokens,
        grad_attn_gain,
        grad_query,
        grad_key,
        grad_value,
        grad_output,
        grad_table,
        grad_ffn_gain,
        grad_router,
        grad_expert_in[None],
        grad_expert_out[None],
    )


def solution(mesh):
    return jax.shard_map(
        shards,
        mesh=mesh,
        in_specs=(
            P("expert", None),
            P(),
            P(None, "shard"),
            P(None, "shard"),
            P(None, "shard"),
            P("shard", None),
            P(None, "shard"),
            P(),
            P(),
            P("expert", None, "shard"),
            P("expert", "shard", None),
            P(("expert", "shard"), None),
            P("expert", None),
            P(("expert", "shard"), None),
        ),
        out_specs=(
            P(("expert", "shard"), None),
            P("expert", None),
            P(),
            P(None, "shard"),
            P(None, "shard"),
            P(None, "shard"),
            P("shard", None),
            P(None, "shard"),
            P(),
            P(),
            P("expert", None, "shard"),
            P("expert", "shard", None),
        ),
        check_vma=False,
    )
```

time: 225 us -> 184 us (0.82)
  starting transfers between devices: 76.6 us -> 57.8 us
  waiting for transfers between devices: 44.7 us -> 62.5 us
  matrix products: 16 us -> 0 us
  local copies, waits for them, and re-layouts: 19.7 us -> 7.04 us
  Pallas kernels: 64.5 us -> 55 us
    ppermute x42 -> x24, waiting for transfers between devices: 23.8 us -> 45.7 us  [hop(): lax.ppermute(item, 'expert', [(at, at ^ distance) for at in range(sources)])]
    ppermute x42 -> x24, starting transfers between devices: 51.7 us -> 35.5 us  [hop(): lax.ppermute(item, 'expert', [(at, at ^ distance) for at in range(sources)])]
    dot_general x5 -> x0, matrix products: 16 us -> none  [the longest x4 14.1 us: product(): lax.dot_general(left, right, (((left_dim,), (right_dim,)), ((), ())), pre...]
    all_to_all x4 -> x3, waiting for transfers between devices: 19.1 us -> 10.3 us  [exchange(): lax.all_to_all(parts, 'expert', split_axis=0, concat_axis=0, tiled=True)]
    pallas_call x1, Pallas kernels: 12.2 us -> 6.68 us  [expert_grads(): pl.pallas_call(expert_grads_kernel, grid=(units // block,), out_shape=[ja...]
    unnamed x135 -> x82, local copies, waits for them, and re-layouts: 12.1 us -> 7.04 us
    ppermute x11 -> x13, waiting for transfers between devices: 1.91 us -> 6.46 us  [swap(): return lax.ppermute(item, 'shard', [(0, 1), (1, 0)])]
    all_to_all x4 -> x3, starting transfers between devices: 23.1 us -> 18.8 us  [exchange(): lax.all_to_all(parts, 'expert', split_axis=0, concat_axis=0, tiled=True)]
  transfers between devices with their start and end apart: 57 -> 40, of which waited for: 19 -> 18; matrix products, arithmetic and copies ran while one was open for 13% -> 0% of each run, Pallas kernels for 23% -> 12%
where the time goes in v1:
time: 184 us
  waiting for transfers between devices  62.5 us (34%)
  starting transfers between devices  57.8 us (31%)
  Pallas kernels  55 us (30%)
  local copies, waits for them, and re-layouts  7.04 us (4%)
    pallas_call x10, Pallas kernels, run(): pl.pallas_call(body, out_shape=[jax.ShapeDtypeStruct(shape, dtype) for sh...  48.3 us
    ppermute x24, waiting for transfers between devices, hop(): lax.ppermute(item, 'expert', [(at, at ^ distance) for at in range(sources)])  45.7 us
    ppermute x24, starting transfers between devices, hop(): lax.ppermute(item, 'expert', [(at, at ^ distance) for at in range(sources)])  35.5 us
    all_to_all x3, starting transfers between devices, exchange(): lax.all_to_all(parts, 'expert', split_axis=0, concat_axis=0, tiled=True)  18.8 us
    all_to_all x3, waiting for transfers between devices, exchange(): lax.all_to_all(parts, 'expert', split_axis=0, concat_axis=0, tiled=True)  10.3 us
    unnamed x82, local copies, waits for them, and re-layouts  7.04 us
    pallas_call x1, Pallas kernels, expert_grads(): pl.pallas_call(expert_grads_kernel, grid=(units // block,), out_shape=[ja...  6.68 us
    ppermute x13, waiting for transfers between devices, swap(): return lax.ppermute(item, 'shard', [(0, 1), (1, 0)])  6.46 us
  transfers between devices with their start and end apart: 40, of which 18 were waited for; matrix products, arithmetic and copies ran while one was open for 0% of the time, Pallas kernels for 12%

profile of v1, /device:TPU:0, one launch (start us, length us, event | category | flops | bytes accessed | tf_op | source)
XLA Modules:
  0.0 183.6 jit_solution(12565273312722627017)
XLA Ops:
  0.6 0.5 collective-permute-start.1
  1.2 7.0 %shard_map.229 = (f32[128,768]{1,0:T(8,128)}, f32[128,768]{1,0:T(8,128)}, bf16[256,1152]{1,0:T(8,128)(2,1)}, bf16[6,256,256]{2,1,0:T(8,128)(2,1)}, bf16[256,768]{1,0:T(8,128)(2,1)}, /*index=5*/bf16[256,384]{1,0:T(8,128)(2,1)}) custom-call(s32[1,4]{1,0:T(1,128)} %refs_0_.2, bf16[256,768]{1,0:T(8,128)(2,1)} %refs_0_.3, f32[768]{0:T(1024)} %refs_1_.5, ...), custom_call_target="tpu_custom_call" | custom-call | tf_op jit(solution)/shard_map/pallas_call | solution.py:134
  8.2 0.5 collective-permute-start
  8.7 1.6 collective-permute-done.refs_6_
  10.3 0.7 copy-done.17
  11.0 3.1 %shard_map.230 = (bf16[256,128]{1,0:T(8,128)(2,1)}, f32[128,768]{1,0:T(8,128)}, bf16[256,1536]{1,0:T(8,128)(2,1)}, bf16[128,768]{1,0:T(8,128)(2,1)}) custom-call(s32[1,128]{1,0:T(1,128)} %bitcast.28, bf16[128,768]{1,0:T(8,128)(2,1)} %refs_4_.5, bf16[256,768]{1,0:T(8,128)(2,1)} %refs_0_.3, f32[128,768]{1,0:T(8,128)} %get-tuple-element.59.refs_3_, ...), custom_call_target="tpu_custom_call" | custom-call | tf_op jit(solution)/shard_map/pallas_call | solution.py:134
  14.1 8.2 %all-to-all-start = ((bf16[16,16,1536]{2,1,0:T(8,128)(2,1)}), bf16[16,16,1536]{2,1,0:T(8,128)(2,1)S(1)}, u32[]{:S(2)}, u32[]{:S(2)}) async-start(bf16[16,16,1536]{2,1,0:T(8,128)(2,1)} %bitcast.23), calls=%async_computation | async-start | bytes 1572864 | tf_op jit(solution)/shard_map/all_to_all | solution.py:681
  22.4 2.8 %collective-permute-start.5 = (bf16[128,768]{1,0:T(8,128)(2,1)}, bf16[128,768]{1,0:T(8,128)(2,1)S(1)}, u32[]{:S(2)}, u32[]{:S(2)}) collective-permute-start(bf16[128,768]{1,0:T(8,128)(2,1)} %get-tuple-element.64), channel_id=1, source_target_pairs={{0,6},{2,4},{4,2},{6,0},{8,14},{10,12},{12,10},{14,8},{16,22},{18,... | collective-permute-start | bytes 589832 | tf_op jit(solution)/shard_map/ppermute | solution.py:674
  25.2 0.6 collective-permute-start.4
  25.9 12.3 %collective-permute-done.5.refs_8_.refs_6_ = bf16[128,768]{1,0:T(8,128)(2,1)S(1)} collective-permute-done((bf16[128,768]{1,0:T(8,128)(2,1)}, bf16[128,768]{1,0:T(8,128)(2,1)S(1)}, u32[]{:S(2)}, u32[]{:S(2)}) %collective-permute-start.5) | collective-permute-done | bytes 196640 | tf_op jit(solution)/shard_map/ppermute | solution.py:674
  38.3 3.6 %collective-permute-done.4.refs_7_.refs_5_ = bf16[128,768]{1,0:T(8,128)(2,1)S(1)} collective-permute-done((bf16[128,768]{1,0:T(8,128)(2,1)}, bf16[128,768]{1,0:T(8,128)(2,1)S(1)}, u32[]{:S(2)}, u32[]{:S(2)}) %collective-permute-start.4) | collective-permute-done | bytes 196640 | tf_op jit(solution)/shard_map/ppermute | solution.py:674
  41.9 0.6 collective-permute-done.3.refs_6_.refs_4_
  42.6 0.8 copy-done.4
  43.4 0.8 copy-done.7
  44.2 11.6 %shard_map.231 = (bf16[256,768]{1,0:T(8,128)(2,1)}, bf16[256,768]{1,0:T(8,128)(2,1)}, f32[16,768]{1,0:T(8,128)}, bf16[256,768]{1,0:T(8,128)(2,1)}, bf16[256,768]...) custom-call(bf16[256,1536]{1,0:T(8,128)(2,1)} %bitcast.17, ...), custom_call_target="tpu_custom_call" | custom-call | tf_op jit(solution)/shard_map/pallas_call | solution.py:134
  55.9 0.5 collective-permute-start.9
  56.4 6.8 %all-to-all-start.1 = ((bf16[16,16,768]{2,1,0:T(8,128)(2,1)}), bf16[16,16,768]{2,1,0:T(8,128)(2,1)S(1)}, u32[]{:S(2)}, u32[]{:S(2)}) async-start(bf16[16,16,768]{2,1,0:T(8,128)(2,1)} %bitcast.25), calls=%async_computation.1 | async-start | bytes 786432 | tf_op jit(solution)/shard_map/all_to_all | solution.py:681
  63.3 0.5 collective-permute-start.7
  63.7 1.4 collective-permute-done.6.refs_6_.rows_far_ref
  65.2 0.6 collective-permute-done.7.refs_7_.grad_produced_far_ref
  65.7 10.3 %all-to-all-done.1 = bf16[16,16,768]{2,1,0:T(8,128)(2,1)S(1)} async-done(((bf16[16,16,768]{2,1,0:T(8,128)(2,1)}), bf16[16,16,768]{2,1,0:T(8,128)(2,1)S(1)}, u32[]{:S(2)}, u32[]{:S(2)}) %all-to-all-start.1) | async-done | bytes 393248 | tf_op jit(solution)/shard_map/all_to_all | solution.py:681
  76.1 0.7 copy-done.10
  77.3 2.4 %shard_map.232 = (bf16[128,768]{1,0:T(8,128)(2,1)}, f32[24,768]{1,0:T(8,128)}) custom-call(bf16[256,128]{1,0:T(8,128)(2,1)} %get-tuple-element.62.refs_0_, bf16[256,768]{1,0:T(8,128)(2,1)} %bitcast.22, f32[128,768]{1,0:T(8,128)} %get-tuple-element.66.refs_2_, f32[768]{0:T(1024)} %refs_3_.3, bf16[128,768]{1,0:T(8,128)(2,1)} %refs_4_.5, ...), custom_call_target="tpu_custom_call" | custom-call | tf_op jit(solution)/shard_map/pallas_call | solution.py:134
  79.8 1.6 collective-permute-done.10.refs_1_.refs_5_
  81.4 0.7 copy-done.11
  82.1 9.3 %shard_map.233 = (bf16[256,768]{1,0:T(8,128)(2,1)}, f32[6,32]{1,0:T(8,128)}, bf16[256,768]{1,0:T(8,128)(2,1)}, bf16[576,256]{1,0:T(8,128)(2,1)}, bf16[576,256]{1...) custom-call(bf16[128,768]{1,0:T(8,128)(2,1)} %get-tuple-element.72.refs_0_.refs_4_, ...), custom_call_target="tpu_custom_call" | custom-call | tf_op jit(solution)/shard_map/pallas_call | solution.py:134
  91.4 3.8 %all-to-all-start.2 = ((bf16[16,16,768]{2,1,0:T(8,128)(2,1)}), bf16[16,16,768]{2,1,0:T(8,128)(2,1)S(1)}, u32[]{:S(2)}, u32[]{:S(2)}) async-start(bf16[16,16,768]{2,1,0:T(8,128)(2,1)} %bitcast.24), calls=%async_computation.2 | async-start | bytes 786432 | tf_op jit(solution)/shard_map/all_to_all | solution.py:681
  95.4 0.4 collective-permute-start.18
  95.8 1.8 collective-permute-start.13
  97.6 1.5 collective-permute-start.14
  99.4 1.3 collective-permute-done.12.refs_7_
  100.8 0.4 collective-permute-start.16
  101.6 2.9 %shard_map.235 = (f32[256,768]{1,0:T(8,128)}, bf16[32,768]{1,0:T(8,128)(2,1)}) custom-call(bf16[256,768]{1,0:T(8,128)(2,1)} %refs_0_.3, f32[768]{0:T(1024)} %refs_1_.5, bf16[256,768]{1,0:T(8,128)(2,1)} %get-tuple-element.78.refs_2_, bf16[256,768]{1,0:T(8,128)(2,1)} %copy-done.16, bf16[128,768]{1,0:T(8,128)(2,1)} %get-tuple-element.72.refs_0_.refs_4_, ...), custom_call_target="tpu_custom_call" | custom-call | tf_op jit(solution)/shard_map/pallas_call | solution.py:134
  104.5 4.7 %collective-permute-done.13.refs_1_ = bf16[576,256]{1,0:T(8,128)(2,1)S(1)} collective-permute-done((bf16[576,256]{1,0:T(8,128)(2,1)}, bf16[576,256]{1,0:T(8,128)(2,1)S(1)}, u32[]{:S(2)}, u32[]{:S(2)}) %collective-permute-start.13) | collective-permute-done | bytes 294944 | tf_op jit(solution)/shard_map/ppermute | solution.py:674
  109.3 6.7 %collective-permute-done.15.refs_3_ = bf16[576,256]{1,0:T(8,128)(2,1)S(1)} collective-permute-done((bf16[576,256]{1,0:T(8,128)(2,1)}, bf16[576,256]{1,0:T(8,128)(2,1)S(1)}, u32[]{:S(2)}, u32[]{:S(2)}) %collective-permute-start.15) | collective-permute-done | bytes 294944 | tf_op jit(solution)/shard_map/ppermute | solution.py:674
  116.0 0.7 copy-done.20
  116.8 4.6 %shard_map.236 = (bf16[128,768]{1,0:T(8,128)(2,1)}, bf16[128,768]{1,0:T(8,128)(2,1)}, bf16[128,768]{1,0:T(8,128)(2,1)}, bf16[128,768]{1,0:T(8,128)(2,1)}) custom-call(bf16[576,256]{1,0:T(8,128)(2,1)} %get-tuple-element.82.refs_0_, bf16[576,256]{1,0:T(8,128)(2,1)} %copy-done.18, bf16[576,256]{1,0:T(8,128)(2,1)} %copy-done.19, bf16[576,256]{1,0:T(8,128)(2,1)} %copy-done.20, ...), custom_call_target="tpu_custom_call" | custom-call | tf_op jit(solution)/shard_map/pallas_call | solution.py:134
  121.5 1.5 collective-permute-start.19
  123.0 2.0 %collective-permute-start.20 = (bf16[128,768]{1,0:T(8,128)(2,1)}, bf16[128,768]{1,0:T(8,128)(2,1)S(1)}, u32[]{:S(2)}, u32[]{:S(2)}) collective-permute-start(bf16[128,768]{1,0:T(8,128)(2,1)} %get-tuple-element.89), channel_id=1, source_target_pairs={{0,16},{2,18},{4,20},{6,22},{8,24},{10,26},{12,28},{14,30},{16,0},... | collective-permute-start | bytes 589832 | tf_op jit(solution)/shard_map/ppermute | solution.py:674
  124.9 1.0 collective-permute-start.21
  125.9 6.7 %shard_map.237 = (f32[768,1536]{1,0:T(8,128)}, f32[1536,768]{1,0:T(8,128)}, f32[8,128]{1,0:T(8,128)}) custom-call(bf16[256,768]{1,0:T(8,128)(2,1)} %get-tuple-element.68.rows_ref, bf16[256,768]{1,0:T(8,128)(2,1)} %copy-done.8, bf16[256,768]{1,0:T(8,128)(2,1)} %get-tuple-element.69.grad_produced_ref, bf16[256,768]{1,0:T(8,128)(2,1)} %copy-done.9, ...), custom_call_target="tpu_custom_call" | custom-call | tf_op jit(solution)/shard_map/pallas_call | solution.py:616
  132.6 7.8 %collective-permute-done.20.refs_2_ = bf16[128,768]{1,0:T(8,128)(2,1)S(1)} collective-permute-done((bf16[128,768]{1,0:T(8,128)(2,1)}, bf16[128,768]{1,0:T(8,128)(2,1)S(1)}, u32[]{:S(2)}, u32[]{:S(2)}) %collective-permute-start.20) | collective-permute-done | bytes 196640 | tf_op jit(solution)/shard_map/ppermute | solution.py:674
  140.4 0.7 copy-done.2
  141.2 2.4 %collective-permute-start.33 = (bf16[96,768]{1,0:T(8,128)(2,1)S(1)}, bf16[96,768]{1,0:T(8,128)(2,1)S(1)}, u32[]{:S(2)}, u32[]{:S(2)}) collective-permute-start(bf16[96,768]{1,0:T(8,128)(2,1)S(1)} %get-tuple-element.95), channel_id=1, source_target_pairs={{0,24},{2,26},{4,28},{6,30},{8,16},{10,18},{12,20},{14,22},{16,8},... | collective-permute-start | bytes 442376 | tf_op jit(solution)/shard_map/ppermute | solution.py:674
  143.6 1.0 collective-permute-start.24
  144.6 1.4 collective-permute-start.23
  146.0 3.7 %collective-permute-start.29 = (bf16[96,768]{1,0:T(8,128)(2,1)S(1)}, bf16[96,768]{1,0:T(8,128)(2,1)S(1)}, u32[]{:S(2)}, u32[]{:S(2)}) collective-permute-start(bf16[96,768]{1,0:T(8,128)(2,1)S(1)} %get-tuple-element.95), channel_id=1, source_target_pairs={{0,16},{2,18},{4,20},{6,22},{8,24},{10,26},{12,28},{14,30},{16,0},... | collective-permute-start | bytes 442376 | tf_op jit(solution)/shard_map/ppermute | solution.py:674
  149.9 1.2 collective-permute-start.22
  151.1 5.1 %collective-permute-done.29.refs_8_ = bf16[96,768]{1,0:T(8,128)(2,1)S(1)} collective-permute-done((bf16[96,768]{1,0:T(8,128)(2,1)S(1)}, bf16[96,768]{1,0:T(8,128)(2,1)S(1)}, u32[]{:S(2)}, u32[]{:S(2)}) %collective-permute-start.29) | collective-permute-done | bytes 147488 | tf_op jit(solution)/shard_map/ppermute | solution.py:674
  156.2 1.0 collective-permute-start.36
  157.3 2.6 %collective-permute-start.35 = (bf16[96,768]{1,0:T(8,128)(2,1)S(1)}, bf16[96,768]{1,0:T(8,128)(2,1)S(1)}, u32[]{:S(2)}, u32[]{:S(2)}) collective-permute-start(bf16[96,768]{1,0:T(8,128)(2,1)S(1)} %collective-permute-done.33.refs_12_), channel_id=1, source_target_pairs={{0,4},{2,6},{4,0},{6,2},{8,12},{10,14},{12,8},{14,10},{16,20},{18,... | collective-permute-start | bytes 442376 | tf_op jit(solution)/shard_map/ppermute | solution.py:674
  159.9 1.5 collective-permute-start.32
  161.4 1.9 %collective-permute-start.31 = (bf16[96,768]{1,0:T(8,128)(2,1)S(1)}, bf16[96,768]{1,0:T(8,128)(2,1)S(1)}, u32[]{:S(2)}, u32[]{:S(2)}) collective-permute-start(bf16[96,768]{1,0:T(8,128)(2,1)S(1)} %collective-permute-done.29.refs_8_), channel_id=1, source_target_pairs={{0,4},{2,6},{4,0},{6,2},{8,12},{10,14},{12,8},{14,10},{16,20},{18,... | collective-permute-start | bytes 442376 | tf_op jit(solution)/shard_map/ppermute | solution.py:674
  163.3 0.3 collective-permute-done.36.refs_15_
  163.7 2.4 %collective-permute-start.30 = (bf16[96,768]{1,0:T(8,128)(2,1)S(1)}, bf16[96,768]{1,0:T(8,128)(2,1)S(1)}, u32[]{:S(2)}, u32[]{:S(2)}) collective-permute-start(bf16[96,768]{1,0:T(8,128)(2,1)S(1)} %collective-permute-done.29.refs_8_), channel_id=1, source_target_pairs={{0,2},{2,0},{4,6},{6,4},{8,10},{10,8},{12,14},{14,12},{16,18},{18,... | collective-permute-start | bytes 442376 | tf_op jit(solution)/shard_map/ppermute | solution.py:674
  166.1 1.7 collective-permute-done.35.refs_14_
  167.9 2.7 %collective-permute-start.27 = (bf16[96,768]{1,0:T(8,128)(2,1)S(1)}, bf16[96,768]{1,0:T(8,128)(2,1)S(1)}, u32[]{:S(2)}, u32[]{:S(2)}) collective-permute-start(bf16[96,768]{1,0:T(8,128)(2,1)S(1)} %collective-permute-done.25.refs_4_), channel_id=1, source_target_pairs={{0,4},{2,6},{4,0},{6,2},{8,12},{10,14},{12,8},{14,10},{16,20},{18,... | collective-permute-start | bytes 442376 | tf_op jit(solution)/shard_map/ppermute | solution.py:674
  170.6 1.8 collective-permute-start.26
  172.4 2.1 %shard_map.234 = bf16[128,768]{1,0:T(8,128)(2,1)} custom-call(bf16[256,128]{1,0:T(8,128)(2,1)} %get-tuple-element.62.refs_0_, bf16[256,768]{1,0:T(8,128)(2,1)} %bitcast.16, f32[128,768]{1,0:T(8,128)} %get-tuple-element.66.refs_2_), custom_call_target="tpu_custom_call" | custom-call | tf_op jit(solution)/shard_map/pallas_call | solution.py:134
  174.6 1.7 collective-permute-done.28.refs_7_
  176.3 0.7 collective-permute-done.27.refs_6_
  177.0 0.4 collective-permute-done.26.refs_5_
  177.7 0.6 copy-done.38
  178.3 5.1 %shard_map.239 = (f32[768,384]{1,0:T(8,128)}, f32[768,384]{1,0:T(8,128)}, f32[768,384]{1,0:T(8,128)}, f32[384,768]{1,0:T(8,128)}, f32[16,768]{1,0:T(8,128)}, /*i...) custom-call(bf16[128,768]{1,0:T(8,128)(2,1)} %copy-done, bf16[128,768]{1,0:T(8,128)(2,1)} %copy-done.23, ...), custom_call_target="tpu_custom_call" | custom-call | tf_op jit(solution)/shard_map/pallas_call | solution.py:134
  (109 shorter events, 3.0 us)
Async XLA Ops:
  0.6 41.9 %collective-permute-start.1 = (bf16[768,1536]{1,0:T(8,128)(2,1)}, bf16[768,1536]{1,0:T(8,128)(2,1)S(1)}, u32[]{:S(2)}, u32[]{:S(2)}) collective-permute-start(bf16[768,1536]{1,0:T(8,128)(2,1)} %bitcast.18), channel_id=1, source_target_pairs={{0,1},{1,0},{2,3},{3,2},{4,5},{5,4},{6,7},{7,6},{8,9},{9,8},{10,11... | collective-permute-start | bytes 7077896 | tf_op jit(solution)/shard_map/ppermute | solution.py:671
  1.2 41.4 %collective-permute-start.2 = (bf16[1536,768]{1,0:T(8,128)(2,1)}, bf16[1536,768]{1,0:T(8,128)(2,1)}, u32[]{:S(2)}, u32[]{:S(2)}) collective-permute-start(bf16[1536,768]{1,0:T(8,128)(2,1)} %bitcast.20), channel_id=1, source_target_pairs={{0,1},{1,0},{2,3},{3,2},{4,5},{5,4},{6,7},{7,6},{8,9},{9,8},{10,11... | collective-permute-start | bytes 7077896 | tf_op jit(solution)/shard_map/ppermute | solution.py:671
  8.2 2.1 %collective-permute-start = (f32[128,768]{1,0:T(8,128)}, f32[128,768]{1,0:T(8,128)S(1)}, u32[]{:S(2)}, u32[]{:S(2)}) collective-permute-start(f32[128,768]{1,0:T(8,128)} %get-tuple-element.61), channel_id=1, source_target_pairs={{0,1},{1,0},{2,3},{3,2},{4,5},{5,4},{6,7},{7,6},{8,9},{9,8},{10,11... | collective-permute-start | bytes 1179656 | tf_op jit(solution)/shard_map/ppermute | solution.py:671
  14.1 28.4 %all-to-all-start = ((bf16[16,16,1536]{2,1,0:T(8,128)(2,1)}), bf16[16,16,1536]{2,1,0:T(8,128)(2,1)S(1)}, u32[]{:S(2)}, u32[]{:S(2)}) async-start(bf16[16,16,1536]{2,1,0:T(8,128)(2,1)} %bitcast.23), calls=%async_computation | async-start | bytes 1572864 | tf_op jit(solution)/shard_map/all_to_all | solution.py:681
  22.4 15.9 %collective-permute-start.5 = (bf16[128,768]{1,0:T(8,128)(2,1)}, bf16[128,768]{1,0:T(8,128)(2,1)S(1)}, u32[]{:S(2)}, u32[]{:S(2)}) collective-permute-start(bf16[128,768]{1,0:T(8,128)(2,1)} %get-tuple-element.64), channel_id=1, source_target_pairs={{0,6},{2,4},{4,2},{6,0},{8,14},{10,12},{12,10},{14,8},{16,22},{18,... | collective-permute-start | bytes 589832 | tf_op jit(solution)/shard_map/ppermute | solution.py:674
  25.2 16.7 %collective-permute-start.4 = (bf16[128,768]{1,0:T(8,128)(2,1)}, bf16[128,768]{1,0:T(8,128)(2,1)S(1)}, u32[]{:S(2)}, u32[]{:S(2)}) collective-permute-start(bf16[128,768]{1,0:T(8,128)(2,1)} %get-tuple-element.64), channel_id=1, source_target_pairs={{0,4},{2,6},{4,0},{6,2},{8,12},{10,14},{12,8},{14,10},{16,20},{18,... | collective-permute-start | bytes 589832 | tf_op jit(solution)/shard_map/ppermute | solution.py:674
  25.8 16.7 %collective-permute-start.3 = (bf16[128,768]{1,0:T(8,128)(2,1)}, bf16[128,768]{1,0:T(8,128)(2,1)}, u32[]{:S(2)}, u32[]{:S(2)}) collective-permute-start(bf16[128,768]{1,0:T(8,128)(2,1)} %get-tuple-element.64), channel_id=1, source_target_pairs={{0,2},{2,0},{4,6},{6,4},{8,10},{10,8},{12,14},{14,12},{16,18},{18,... | collective-permute-start | bytes 589832 | tf_op jit(solution)/shard_map/ppermute | solution.py:674
  38.3 4.3 %copy-start.12 = (bf16[128,768]{1,0:T(8,128)(2,1)}, bf16[128,768]{1,0:T(8,128)(2,1)S(1)}, u32[]{:S(2)}) copy-start(bf16[128,768]{1,0:T(8,128)(2,1)S(1)} %collective-permute-done.5.refs_8_.refs_6_) | copy-start | bytes 589828
  55.8 20.2 %collective-permute-start.8 = (bf16[256,1536]{1,0:T(8,128)(2,1)}, bf16[256,1536]{1,0:T(8,128)(2,1)S(1)}, u32[]{:S(2)}, u32[]{:S(2)}) collective-permute-start(bf16[256,1536]{1,0:T(8,128)(2,1)} %get-tuple-element.70), channel_id=1, source_target_pairs={{0,1},{1,0},{2,3},{3,2},{4,5},{5,4},{6,7},{7,6},{8,9},{9,8},{10,11... | collective-permute-start | bytes 2359304 | tf_op jit(solution)/shard_map/ppermute | solution.py:671
  55.9 20.1 %collective-permute-start.9 = (bf16[256,1536]{1,0:T(8,128)(2,1)}, bf16[256,1536]{1,0:T(8,128)(2,1)S(1)}, u32[]{:S(2)}, u32[]{:S(2)}) collective-permute-start(bf16[256,1536]{1,0:T(8,128)(2,1)} %get-tuple-element.71), channel_id=1, source_target_pairs={{0,1},{1,0},{2,3},{3,2},{4,5},{5,4},{6,7},{7,6},{8,9},{9,8},{10,11... | collective-permute-start | bytes 2359304 | tf_op jit(solution)/shard_map/ppermute | solution.py:671
  56.4 19.6 %all-to-all-start.1 = ((bf16[16,16,768]{2,1,0:T(8,128)(2,1)}), bf16[16,16,768]{2,1,0:T(8,128)(2,1)S(1)}, u32[]{:S(2)}, u32[]{:S(2)}) async-start(bf16[16,16,768]{2,1,0:T(8,128)(2,1)} %bitcast.25), calls=%async_computation.1 | async-start | bytes 786432 | tf_op jit(solution)/shard_map/all_to_all | solution.py:681
  63.2 2.0 %collective-permute-start.6 = (bf16[256,768]{1,0:T(8,128)(2,1)}, bf16[256,768]{1,0:T(8,128)(2,1)S(1)}, u32[]{:S(2)}, u32[]{:S(2)}) collective-permute-start(bf16[256,768]{1,0:T(8,128)(2,1)} %get-tuple-element.68.rows_ref), channel_id=1, source_target_pairs={{0,1},{1,0},{2,3},{3,2},{4,5},{5,4},{6,7},{7,6},{8,9},{9,8},{10,11... | collective-permute-start | bytes 1179656 | tf_op jit(solution)/shard_map/ppermute | solution.py:671
  63.3 2.5 %collective-permute-start.7 = (bf16[256,768]{1,0:T(8,128)(2,1)}, bf16[256,768]{1,0:T(8,128)(2,1)S(1)}, u32[]{:S(2)}, u32[]{:S(2)}) collective-permute-start(bf16[256,768]{1,0:T(8,128)(2,1)} %get-tuple-element.69.grad_produced_ref), channel_id=1, source_target_pairs={{0,1},{1,0},{2,3},{3,2},{4,5},{5,4},{6,7},{7,6},{8,9},{9,8},{10,11... | collective-permute-start | bytes 1179656 | tf_op jit(solution)/shard_map/ppermute | solution.py:671
  65.2 10.9 %copy-start.8 = (bf16[256,768]{1,0:T(8,128)(2,1)}, bf16[256,768]{1,0:T(8,128)(2,1)S(1)}, u32[]{:S(2)}) copy-start(bf16[256,768]{1,0:T(8,128)(2,1)S(1)} %collective-permute-done.6.refs_6_.rows_far_ref) | copy-start | bytes 1179652
  65.7 10.3 %copy-start.9 = (bf16[256,768]{1,0:T(8,128)(2,1)}, bf16[256,768]{1,0:T(8,128)(2,1)S(1)}, u32[]{:S(2)}) copy-start(bf16[256,768]{1,0:T(8,128)(2,1)S(1)} %collective-permute-done.7.refs_7_.grad_produced_far_ref) | copy-start | bytes 1179652
  79.7 1.7 collective-permute-start.10
  82.1 13.3 %copy-start.13 = (bf16[128,768]{1,0:T(8,128)(2,1)S(1)}, bf16[128,768]{1,0:T(8,128)(2,1)}, u32[]{:S(2)}) copy-start(bf16[128,768]{1,0:T(8,128)(2,1)} %copy-done.12) | copy-start | bytes 589828
  82.1 17.2 %copy-start.39 = (f32[24,768]{1,0:T(8,128)S(1)}, f32[24,768]{1,0:T(8,128)}, u32[]{:S(2)}) copy-start(f32[24,768]{1,0:T(8,128)} %get-tuple-element.79.refs_6_) | copy-start | bytes 221188
  82.1 18.5 %copy-start.15 = (bf16[128,768]{1,0:T(8,128)(2,1)S(1)}, bf16[128,768]{1,0:T(8,128)(2,1)}, u32[]{:S(2)}) copy-start(bf16[128,768]{1,0:T(8,128)(2,1)} %copy-done.14) | copy-start | bytes 589828
  91.4 24.6 %all-to-all-start.2 = ((bf16[16,16,768]{2,1,0:T(8,128)(2,1)}), bf16[16,16,768]{2,1,0:T(8,128)(2,1)S(1)}, u32[]{:S(2)}, u32[]{:S(2)}) async-start(bf16[16,16,768]{2,1,0:T(8,128)(2,1)} %bitcast.24), calls=%async_computation.2 | async-start | bytes 786432 | tf_op jit(solution)/shard_map/all_to_all | solution.py:681
  95.2 5.6 %collective-permute-start.11 = (bf16[256,768]{1,0:T(8,128)(2,1)}, bf16[256,768]{1,0:T(8,128)(2,1)S(1)}, u32[]{:S(2)}, u32[]{:S(2)}) collective-permute-start(bf16[256,768]{1,0:T(8,128)(2,1)} %get-tuple-element.78.refs_2_), channel_id=1, source_target_pairs={{0,1},{1,0},{2,3},{3,2},{4,5},{5,4},{6,7},{7,6},{8,9},{9,8},{10,11... | collective-permute-start | bytes 1179656 | tf_op jit(solution)/shard_map/ppermute | solution.py:671
  95.4 3.9 %collective-permute-start.18 = (bf16[128,768]{1,0:T(8,128)(2,1)S(1)}, bf16[128,768]{1,0:T(8,128)(2,1)S(1)}, u32[]{:S(2)}, u32[]{:S(2)}) collective-permute-start(bf16[128,768]{1,0:T(8,128)(2,1)S(1)} %copy-done.13), channel_id=1, source_target_pairs={{0,1},{1,0},{2,3},{3,2},{4,5},{5,4},{6,7},{7,6},{8,9},{9,8},{10,11... | collective-permute-start | bytes 589832 | tf_op jit(solution)/shard_map/ppermute | solution.py:671
  95.8 13.5 %collective-permute-start.13 = (bf16[576,256]{1,0:T(8,128)(2,1)}, bf16[576,256]{1,0:T(8,128)(2,1)S(1)}, u32[]{:S(2)}, u32[]{:S(2)}) collective-permute-start(bf16[576,256]{1,0:T(8,128)(2,1)} %get-tuple-element.83), channel_id=1, source_target_pairs={{0,2},{2,0},{4,6},{6,4},{8,10},{10,8},{12,14},{14,12},{16,18},{18,... | collective-permute-start | bytes 884744 | tf_op jit(solution)/shard_map/ppermute | solution.py:674
  97.6 11.7 %collective-permute-start.14 = (bf16[576,256]{1,0:T(8,128)(2,1)}, bf16[576,256]{1,0:T(8,128)(2,1)S(1)}, u32[]{:S(2)}, u32[]{:S(2)}) collective-permute-start(bf16[576,256]{1,0:T(8,128)(2,1)} %get-tuple-element.84), channel_id=1, source_target_pairs={{0,4},{2,6},{4,0},{6,2},{8,12},{10,14},{12,8},{14,10},{16,20},{18,... | collective-permute-start | bytes 884744 | tf_op jit(solution)/shard_map/ppermute | solution.py:674
  99.0 16.9 %collective-permute-start.15 = (bf16[576,256]{1,0:T(8,128)(2,1)}, bf16[576,256]{1,0:T(8,128)(2,1)S(1)}, u32[]{:S(2)}, u32[]{:S(2)}) collective-permute-start(bf16[576,256]{1,0:T(8,128)(2,1)} %get-tuple-element.85), channel_id=1, source_target_pairs={{0,6},{2,4},{4,2},{6,0},{8,14},{10,12},{12,10},{14,8},{16,22},{18,... | collective-permute-start | bytes 884744 | tf_op jit(solution)/shard_map/ppermute | solution.py:674
  99.3 16.7 %copy-start.24 = (bf16[128,768]{1,0:T(8,128)(2,1)}, bf16[128,768]{1,0:T(8,128)(2,1)S(1)}, u32[]{:S(2)}) copy-start(bf16[128,768]{1,0:T(8,128)(2,1)S(1)} %collective-permute-done.18.refs_9_) | copy-start | bytes 589828
  99.3 1.3 collective-permute-start.12
  100.6 3.9 %collective-permute-start.17 = (bf16[128,768]{1,0:T(8,128)(2,1)S(1)}, bf16[128,768]{1,0:T(8,128)(2,1)S(1)}, u32[]{:S(2)}, u32[]{:S(2)}) collective-permute-start(bf16[128,768]{1,0:T(8,128)(2,1)S(1)} %copy-done.15), channel_id=1, source_target_pairs={{0,1},{1,0},{2,3},{3,2},{4,5},{5,4},{6,7},{7,6},{8,9},{9,8},{10,11... | collective-permute-start | bytes 589832 | tf_op jit(solution)/shard_map/ppermute | solution.py:671
  100.8 3.7 %collective-permute-start.16 = (bf16[128,768]{1,0:T(8,128)(2,1)}, bf16[128,768]{1,0:T(8,128)(2,1)S(1)}, u32[]{:S(2)}, u32[]{:S(2)}) collective-permute-start(bf16[128,768]{1,0:T(8,128)(2,1)} %collective-permute-done.3.refs_6_.refs_4_), channel_id=1, source_target_pairs={{0,1},{1,0},{2,3},{3,2},{4,5},{5,4},{6,7},{7,6},{8,9},{9,8},{10,11... | collective-permute-start | bytes 589832 | tf_op jit(solution)/shard_map/ppermute | solution.py:671
  104.5 11.5 %copy-start.25 = (bf16[128,768]{1,0:T(8,128)(2,1)}, bf16[128,768]{1,0:T(8,128)(2,1)S(1)}, u32[]{:S(2)}) copy-start(bf16[128,768]{1,0:T(8,128)(2,1)S(1)} %collective-permute-done.17.refs_8_) | copy-start | bytes 589828
  104.5 11.5 %copy-start.26 = (bf16[128,768]{1,0:T(8,128)(2,1)}, bf16[128,768]{1,0:T(8,128)(2,1)S(1)}, u32[]{:S(2)}) copy-start(bf16[128,768]{1,0:T(8,128)(2,1)S(1)} %collective-permute-done.16.refs_7_) | copy-start | bytes 589828
  109.3 6.7 %copy-start.18 = (bf16[576,256]{1,0:T(8,128)(2,1)}, bf16[576,256]{1,0:T(8,128)(2,1)S(1)}, u32[]{:S(2)}) copy-start(bf16[576,256]{1,0:T(8,128)(2,1)S(1)} %collective-permute-done.13.refs_1_) | copy-start | bytes 884740
  109.3 6.7 %copy-start.19 = (bf16[576,256]{1,0:T(8,128)(2,1)}, bf16[576,256]{1,0:T(8,128)(2,1)S(1)}, u32[]{:S(2)}) copy-start(bf16[576,256]{1,0:T(8,128)(2,1)S(1)} %collective-permute-done.14.refs_2_) | copy-start | bytes 884740
  121.5 11.1 %collective-permute-start.19 = (bf16[128,768]{1,0:T(8,128)(2,1)}, bf16[128,768]{1,0:T(8,128)(2,1)S(1)}, u32[]{:S(2)}, u32[]{:S(2)}) collective-permute-start(bf16[128,768]{1,0:T(8,128)(2,1)} %get-tuple-element.88), channel_id=1, source_target_pairs={{0,8},{2,10},{4,12},{6,14},{8,0},{10,2},{12,4},{14,6},{16,24},{18,... | collective-permute-start | bytes 589832 | tf_op jit(solution)/shard_map/ppermute | solution.py:674
  123.0 17.4 %collective-permute-start.20 = (bf16[128,768]{1,0:T(8,128)(2,1)}, bf16[128,768]{1,0:T(8,128)(2,1)S(1)}, u32[]{:S(2)}, u32[]{:S(2)}) collective-permute-start(bf16[128,768]{1,0:T(8,128)(2,1)} %get-tuple-element.89), channel_id=1, source_target_pairs={{0,16},{2,18},{4,20},{6,22},{8,24},{10,26},{12,28},{14,30},{16,0},... | collective-permute-start | bytes 589832 | tf_op jit(solution)/shard_map/ppermute | solution.py:674
  124.9 15.4 %collective-permute-start.21 = (bf16[128,768]{1,0:T(8,128)(2,1)}, bf16[128,768]{1,0:T(8,128)(2,1)S(1)}, u32[]{:S(2)}, u32[]{:S(2)}) collective-permute-start(bf16[128,768]{1,0:T(8,128)(2,1)} %get-tuple-element.90), channel_id=1, source_target_pairs={{0,24},{2,26},{4,28},{6,30},{8,16},{10,18},{12,20},{14,22},{16,8},... | collective-permute-start | bytes 589832 | tf_op jit(solution)/shard_map/ppermute | solution.py:674
  125.9 14.5 %copy-start.1 = (bf16[128,768]{1,0:T(8,128)(2,1)S(1)}, bf16[128,768]{1,0:T(8,128)(2,1)}, u32[]{:S(2)}) copy-start(bf16[128,768]{1,0:T(8,128)(2,1)} %get-tuple-element.87.refs_0_) | copy-start | bytes 589828
  141.2 36.2 %copy-start = (bf16[128,768]{1,0:T(8,128)(2,1)}, bf16[128,768]{1,0:T(8,128)(2,1)S(1)}, u32[]{:S(2)}) copy-start(bf16[128,768]{1,0:T(8,128)(2,1)S(1)} %get-tuple-element.94.refs_0_) | copy-start | bytes 589828
  141.2 8.7 %collective-permute-start.33 = (bf16[96,768]{1,0:T(8,128)(2,1)S(1)}, bf16[96,768]{1,0:T(8,128)(2,1)S(1)}, u32[]{:S(2)}, u32[]{:S(2)}) collective-permute-start(bf16[96,768]{1,0:T(8,128)(2,1)S(1)} %get-tuple-element.95), channel_id=1, source_target_pairs={{0,24},{2,26},{4,28},{6,30},{8,16},{10,18},{12,20},{14,22},{16,8},... | collective-permute-start | bytes 442376 | tf_op jit(solution)/shard_map/ppermute | solution.py:674
  143.6 16.2 %collective-permute-start.24 = (bf16[128,768]{1,0:T(8,128)(2,1)S(1)}, bf16[128,768]{1,0:T(8,128)(2,1)S(1)}, u32[]{:S(2)}, u32[]{:S(2)}) collective-permute-start(bf16[128,768]{1,0:T(8,128)(2,1)S(1)} %get-tuple-element.94.refs_0_), channel_id=1, source_target_pairs={{0,6},{2,4},{4,2},{6,0},{8,14},{10,12},{12,10},{14,8},{16,22},{18,... | collective-permute-start | bytes 589832 | tf_op jit(solution)/shard_map/ppermute | solution.py:674
  144.6 15.2 %collective-permute-start.23 = (bf16[128,768]{1,0:T(8,128)(2,1)S(1)}, bf16[128,768]{1,0:T(8,128)(2,1)S(1)}, u32[]{:S(2)}, u32[]{:S(2)}) collective-permute-start(bf16[128,768]{1,0:T(8,128)(2,1)S(1)} %get-tuple-element.94.refs_0_), channel_id=1, source_target_pairs={{0,4},{2,6},{4,0},{6,2},{8,12},{10,14},{12,8},{14,10},{16,20},{18,... | collective-permute-start | bytes 589832 | tf_op jit(solution)/shard_map/ppermute | solution.py:674
  146.0 10.3 %collective-permute-start.29 = (bf16[96,768]{1,0:T(8,128)(2,1)S(1)}, bf16[96,768]{1,0:T(8,128)(2,1)S(1)}, u32[]{:S(2)}, u32[]{:S(2)}) collective-permute-start(bf16[96,768]{1,0:T(8,128)(2,1)S(1)} %get-tuple-element.95), channel_id=1, source_target_pairs={{0,16},{2,18},{4,20},{6,22},{8,24},{10,26},{12,28},{14,30},{16,0},... | collective-permute-start | bytes 442376 | tf_op jit(solution)/shard_map/ppermute | solution.py:674
  149.6 7.6 %collective-permute-start.25 = (bf16[96,768]{1,0:T(8,128)(2,1)S(1)}, bf16[96,768]{1,0:T(8,128)(2,1)S(1)}, u32[]{:S(2)}, u32[]{:S(2)}) collective-permute-start(bf16[96,768]{1,0:T(8,128)(2,1)S(1)} %get-tuple-element.95), channel_id=1, source_target_pairs={{0,8},{2,10},{4,12},{6,14},{8,0},{10,2},{12,4},{14,6},{16,24},{18,... | collective-permute-start | bytes 442376 | tf_op jit(solution)/shard_map/ppermute | solution.py:674
  149.9 27.5 %copy-start.27 = (bf16[96,768]{1,0:T(8,128)(2,1)}, bf16[96,768]{1,0:T(8,128)(2,1)S(1)}, u32[]{:S(2)}) copy-start(bf16[96,768]{1,0:T(8,128)(2,1)S(1)} %collective-permute-done.33.refs_12_) | copy-start | bytes 442372
  149.9 11.5 %collective-permute-start.22 = (bf16[128,768]{1,0:T(8,128)(2,1)S(1)}, bf16[128,768]{1,0:T(8,128)(2,1)S(1)}, u32[]{:S(2)}, u32[]{:S(2)}) collective-permute-start(bf16[128,768]{1,0:T(8,128)(2,1)S(1)} %get-tuple-element.94.refs_0_), channel_id=1, source_target_pairs={{0,2},{2,0},{4,6},{6,4},{8,10},{10,8},{12,14},{14,12},{16,18},{18,... | collective-permute-start | bytes 589832 | tf_op jit(solution)/shard_map/ppermute | solution.py:674
  156.2 21.2 %copy-start.28 = (bf16[96,768]{1,0:T(8,128)(2,1)}, bf16[96,768]{1,0:T(8,128)(2,1)S(1)}, u32[]{:S(2)}) copy-start(bf16[96,768]{1,0:T(8,128)(2,1)S(1)} %collective-permute-done.29.refs_8_) | copy-start | bytes 442372
  156.2 7.4 %collective-permute-start.36 = (bf16[96,768]{1,0:T(8,128)(2,1)S(1)}, bf16[96,768]{1,0:T(8,128)(2,1)S(1)}, u32[]{:S(2)}, u32[]{:S(2)}) collective-permute-start(bf16[96,768]{1,0:T(8,128)(2,1)S(1)} %collective-permute-done.33.refs_12_), channel_id=1, source_target_pairs={{0,6},{2,4},{4,2},{6,0},{8,14},{10,12},{12,10},{14,8},{16,22},{18,... | collective-permute-start | bytes 442376 | tf_op jit(solution)/shard_map/ppermute | solution.py:674
  157.3 20.1 %copy-start.29 = (bf16[96,768]{1,0:T(8,128)(2,1)}, bf16[96,768]{1,0:T(8,128)(2,1)S(1)}, u32[]{:S(2)}) copy-start(bf16[96,768]{1,0:T(8,128)(2,1)S(1)} %collective-permute-done.25.refs_4_) | copy-start | bytes 442372
  157.3 10.5 %collective-permute-start.35 = (bf16[96,768]{1,0:T(8,128)(2,1)S(1)}, bf16[96,768]{1,0:T(8,128)(2,1)S(1)}, u32[]{:S(2)}, u32[]{:S(2)}) collective-permute-start(bf16[96,768]{1,0:T(8,128)(2,1)S(1)} %collective-permute-done.33.refs_12_), channel_id=1, source_target_pairs={{0,4},{2,6},{4,0},{6,2},{8,12},{10,14},{12,8},{14,10},{16,20},{18,... | collective-permute-start | bytes 442376 | tf_op jit(solution)/shard_map/ppermute | solution.py:674
  159.8 17.6 %copy-start.21 = (bf16[128,768]{1,0:T(8,128)(2,1)}, bf16[128,768]{1,0:T(8,128)(2,1)S(1)}, u32[]{:S(2)}) copy-start(bf16[128,768]{1,0:T(8,128)(2,1)S(1)} %collective-permute-done.24.refs_3_) | copy-start | bytes 589828
  159.8 8.1 %collective-permute-start.34 = (bf16[96,768]{1,0:T(8,128)(2,1)S(1)}, bf16[96,768]{1,0:T(8,128)(2,1)S(1)}, u32[]{:S(2)}, u32[]{:S(2)}) collective-permute-start(bf16[96,768]{1,0:T(8,128)(2,1)S(1)} %collective-permute-done.33.refs_12_), channel_id=1, source_target_pairs={{0,2},{2,0},{4,6},{6,4},{8,10},{10,8},{12,14},{14,12},{16,18},{18,... | collective-permute-start | bytes 442376 | tf_op jit(solution)/shard_map/ppermute | solution.py:674
  159.9 17.6 %copy-start.22 = (bf16[128,768]{1,0:T(8,128)(2,1)}, bf16[128,768]{1,0:T(8,128)(2,1)S(1)}, u32[]{:S(2)}) copy-start(bf16[128,768]{1,0:T(8,128)(2,1)S(1)} %collective-permute-done.23.refs_2_) | copy-start | bytes 589828
  159.9 10.8 %collective-permute-start.32 = (bf16[96,768]{1,0:T(8,128)(2,1)S(1)}, bf16[96,768]{1,0:T(8,128)(2,1)S(1)}, u32[]{:S(2)}, u32[]{:S(2)}) collective-permute-start(bf16[96,768]{1,0:T(8,128)(2,1)S(1)} %collective-permute-done.29.refs_8_), channel_id=1, source_target_pairs={{0,6},{2,4},{4,2},{6,0},{8,14},{10,12},{12,10},{14,8},{16,22},{18,... | collective-permute-start | bytes 442376 | tf_op jit(solution)/shard_map/ppermute | solution.py:674
  161.4 16.1 %copy-start.23 = (bf16[128,768]{1,0:T(8,128)(2,1)}, bf16[128,768]{1,0:T(8,128)(2,1)S(1)}, u32[]{:S(2)}) copy-start(bf16[128,768]{1,0:T(8,128)(2,1)S(1)} %collective-permute-done.22.refs_1_) | copy-start | bytes 589828
  161.4 13.2 %collective-permute-start.31 = (bf16[96,768]{1,0:T(8,128)(2,1)S(1)}, bf16[96,768]{1,0:T(8,128)(2,1)S(1)}, u32[]{:S(2)}, u32[]{:S(2)}) collective-permute-start(bf16[96,768]{1,0:T(8,128)(2,1)S(1)} %collective-permute-done.29.refs_8_), channel_id=1, source_target_pairs={{0,4},{2,6},{4,0},{6,2},{8,12},{10,14},{12,8},{14,10},{16,20},{18,... | collective-permute-start | bytes 442376 | tf_op jit(solution)/shard_map/ppermute | solution.py:674
  163.7 13.8 %copy-start.30 = (bf16[96,768]{1,0:T(8,128)(2,1)}, bf16[96,768]{1,0:T(8,128)(2,1)S(1)}, u32[]{:S(2)}) copy-start(bf16[96,768]{1,0:T(8,128)(2,1)S(1)} %collective-permute-done.36.refs_15_) | copy-start | bytes 442372
  163.7 10.9 %collective-permute-start.30 = (bf16[96,768]{1,0:T(8,128)(2,1)S(1)}, bf16[96,768]{1,0:T(8,128)(2,1)S(1)}, u32[]{:S(2)}, u32[]{:S(2)}) collective-permute-start(bf16[96,768]{1,0:T(8,128)(2,1)S(1)} %collective-permute-done.29.refs_8_), channel_id=1, source_target_pairs={{0,2},{2,0},{4,6},{6,4},{8,10},{10,8},{12,14},{14,12},{16,18},{18,... | collective-permute-start | bytes 442376 | tf_op jit(solution)/shard_map/ppermute | solution.py:674
  167.8 9.7 %copy-start.31 = (bf16[96,768]{1,0:T(8,128)(2,1)}, bf16[96,768]{1,0:T(8,128)(2,1)S(1)}, u32[]{:S(2)}) copy-start(bf16[96,768]{1,0:T(8,128)(2,1)S(1)} %collective-permute-done.35.refs_14_) | copy-start | bytes 442372
  167.8 8.5 %collective-permute-start.28 = (bf16[96,768]{1,0:T(8,128)(2,1)S(1)}, bf16[96,768]{1,0:T(8,128)(2,1)S(1)}, u32[]{:S(2)}, u32[]{:S(2)}) collective-permute-start(bf16[96,768]{1,0:T(8,128)(2,1)S(1)} %collective-permute-done.25.refs_4_), channel_id=1, source_target_pairs={{0,6},{2,4},{4,2},{6,0},{8,14},{10,12},{12,10},{14,8},{16,22},{18,... | collective-permute-start | bytes 442376 | tf_op jit(solution)/shard_map/ppermute | solution.py:674
  167.9 9.5 %copy-start.32 = (bf16[96,768]{1,0:T(8,128)(2,1)}, bf16[96,768]{1,0:T(8,128)(2,1)S(1)}, u32[]{:S(2)}) copy-start(bf16[96,768]{1,0:T(8,128)(2,1)S(1)} %collective-permute-done.34.refs_13_) | copy-start | bytes 442372
  167.9 9.1 %collective-permute-start.27 = (bf16[96,768]{1,0:T(8,128)(2,1)S(1)}, bf16[96,768]{1,0:T(8,128)(2,1)S(1)}, u32[]{:S(2)}, u32[]{:S(2)}) collective-permute-start(bf16[96,768]{1,0:T(8,128)(2,1)S(1)} %collective-permute-done.25.refs_4_), channel_id=1, source_target_pairs={{0,4},{2,6},{4,0},{6,2},{8,12},{10,14},{12,8},{14,10},{16,20},{18,... | collective-permute-start | bytes 442376 | tf_op jit(solution)/shard_map/ppermute | solution.py:674
  170.6 6.9 %copy-start.33 = (bf16[96,768]{1,0:T(8,128)(2,1)}, bf16[96,768]{1,0:T(8,128)(2,1)S(1)}, u32[]{:S(2)}) copy-start(bf16[96,768]{1,0:T(8,128)(2,1)S(1)} %collective-permute-done.32.refs_11_) | copy-start | bytes 442372
  170.6 6.8 %collective-permute-start.26 = (bf16[96,768]{1,0:T(8,128)(2,1)S(1)}, bf16[96,768]{1,0:T(8,128)(2,1)S(1)}, u32[]{:S(2)}, u32[]{:S(2)}) collective-permute-start(bf16[96,768]{1,0:T(8,128)(2,1)S(1)} %collective-permute-done.25.refs_4_), channel_id=1, source_target_pairs={{0,2},{2,0},{4,6},{6,4},{8,10},{10,8},{12,14},{14,12},{16,18},{18,... | collective-permute-start | bytes 442376 | tf_op jit(solution)/shard_map/ppermute | solution.py:674
  174.6 2.9 %copy-start.34 = (bf16[96,768]{1,0:T(8,128)(2,1)}, bf16[96,768]{1,0:T(8,128)(2,1)S(1)}, u32[]{:S(2)}) copy-start(bf16[96,768]{1,0:T(8,128)(2,1)S(1)} %collective-permute-done.31.refs_10_) | copy-start | bytes 442372
  (17 other events, 16.7 us)

commit v2 on v1

--- a/solution.py
+++ b/solution.py
@@ -15,8 +15,7 @@
 LINE = 4
 LOW = jnp.bfloat16
 FULL = jnp.float32
-GRANT = 56 * 1024 * 1024
-LITTLE = 4 * 1024 * 1024
+MEGABYTE = 1024 * 1024
 
 
 def inverse_rms(rows):
@@ -137,7 +136,7 @@
         in_specs=in_specs,
         out_specs=[placed] * results,
         scratch_shapes=scratch_shapes,
-        compiler_params=pltpu.CompilerParams(vmem_limit_bytes=LITTLE if near else GRANT),
+        compiler_params=pltpu.CompilerParams(vmem_limit_bytes=(4 if near else 56) * MEGABYTE),
         cost_estimate=pl.CostEstimate(flops=0, bytes_accessed=0, transcendentals=0),
     )(*operands, *after)
 
@@ -352,28 +351,6 @@
     grad_router_ref[...] = product(grad_logits, rows, 0, 0)
 
 
-def grad_hidden_kernel(
-    place_ref,
-    returned_ref,
-    hidden_ref,
-    gain_ref,
-    cotangent_ref,
-    grad_router_ref,
-    attention_ref,
-    small_ref,
-):
-    experts = grad_router_ref.shape[0]
-    width = hidden_ref.shape[1]
-    hidden = hidden_ref[...]
-    grad_normed = product(place_ref[...], returned_ref[...], 0, 0)
-    grad_rows, grad_gain = norm_back(hidden, inverse_rms(hidden), gain_ref[...].reshape(1, -1), grad_normed)
-    attention_ref[...] = (cotangent_ref[...].astype(FULL) + grad_rows).astype(LOW)
-    small_ref[0:experts, :] = grad_router_ref[...]
-    small_ref[experts:, :] = jnp.concatenate(
-        [grad_gain, jnp.zeros((small_ref.shape[0] - experts - 1, width), FULL)], axis=0
-    )
-
-
 def halves(own_rows):
     half = lax.axis_index("shard")
     own_at = pl.multiple_of(half * own_rows, own_rows)
@@ -382,24 +359,27 @@
 
 
 def attention_back_kernel(
-    attention_own_ref,
-    attention_came_ref,
+    place_own_ref,
+    place_came_ref,
+    hidden_own_ref,
+    hidden_came_ref,
+    gain_ref,
+    cotangent_own_ref,
+    cotangent_came_ref,
+    returned_own_ref,
+    returned_came_ref,
     output_ref,
     mixed_ref,
     qkv_ref,
     probs_ref,
-    query_ref,
-    key_ref,
-    value_ref,
-    back_ref,
-    grad_normed_ref,
+    attention_ref,
+    grad_ffn_ref,
+    grad_low_ref,
     grad_table_ref,
-    back_out_ref,
     part_ref,
     part_one_ref,
     part_two_ref,
     part_three_ref,
-    attention_ref,
     grads_ref,
     turned_ref,
     output_grad_ref,
@@ -407,14 +387,26 @@
     head_size,
     bucket_total,
 ):
-    own_rows, width = attention_own_ref.shape
+    own_rows, width = hidden_own_ref.shape
     group_rows = 2 * own_rows
     heads = probs_ref.shape[0]
     columns = heads * head_size
     scale = head_size ** (-0.5)
     own_at, other_at = halves(own_rows)
-    attention_ref[pl.ds(own_at, own_rows), :] = attention_own_ref[...]
-    attention_ref[pl.ds(other_at, own_rows), :] = attention_came_ref[...]
+    gain = gain_ref[...].reshape(1, -1)
+    grad_gains = []
+    for at, place, rows, cotangent, returned in (
+        (own_at, place_own_ref, hidden_own_ref, cotangent_own_ref, returned_own_ref),
+        (other_at, place_came_ref, hidden_came_ref, cotangent_came_ref, returned_came_ref),
+    ):
+        hidden = rows[...]
+        grads = product(place[...], returned[...], 0, 0)
+        grad_rows, grad_gain = norm_back(hidden, inverse_rms(hidden), gain, grads)
+        grad_rows = cotangent[...].astype(FULL) + grad_rows
+        attention_ref[pl.ds(at, own_rows), :] = grad_rows.astype(LOW)
+        grad_gains.append(grad_gain)
+    grad_ffn_ref[...] = grad_gains[0] + grad_gains[1]
+    attention_ref.send()
     grad_mixed = product(attention_ref[...], output_ref[...], 1, 1).astype(LOW)
     output_grad_ref[...] = product(mixed_ref[...], attention_ref[...], 0, 0)
     reversal = (
@@ -451,6 +443,8 @@
     grads_ref[:, 0:columns] = grad_values
     grads_ref[:, columns : 2 * columns] = grad_queries
     grads_ref[:, 2 * columns : 3 * columns] = grad_keys
+    grad_low_ref[...] = grads_ref[...].astype(LOW)
+    grad_low_ref.send()
     turned_ref[:, 0:own_rows] = grads_ref[pl.ds(own_at, own_rows), :].T
     turned_ref[:, own_rows:] = grads_ref[pl.ds(other_at, own_rows), :].T
     mine = lax.rem(lax.axis_index("expert"), PLANE)
@@ -469,44 +463,62 @@
                 :, piece * group_rows : (piece + 1) * group_rows
             ]
         ref.send()
-    back_out_ref[...] = back_ref[...]
-    back_out_ref.send()
-    grad_normed = product(grad_queries.astype(LOW), query_ref[...], 1, 1)
-    grad_normed = grad_normed + product(grad_keys.astype(LOW), key_ref[...], 1, 1)
-    grad_normed = grad_normed + product(grad_values.astype(LOW), value_ref[...], 1, 1)
-    grad_normed_ref[...] = grad_normed.astype(LOW)
 
 
 def grad_tokens_kernel(
     tokens_ref,
     gain_ref,
-    normed_own_ref,
-    normed_came_ref,
-    attention_own_ref,
-    attention_came_ref,
-    small_own_ref,
-    small_came_ref,
+    attention_ref,
+    router_own_ref,
+    router_came_ref,
+    ffn_ref,
     table_ref,
+    back_ref,
+    grads_own_ref,
+    value_own_ref,
+    query_own_ref,
+    key_own_ref,
+    value_came_ref,
+    query_came_ref,
+    key_came_ref,
+    grads_came_ref,
     grad_tokens_ref,
     small_ref,
+    back_out_ref,
 ):
-    own_rows = attention_own_ref.shape[0]
-    width = tokens_ref.shape[1]
+    back_out_ref[...] = back_ref[...]
+    back_out_ref.send()
+    width, columns = value_own_ref.shape
+    experts = router_own_ref.shape[0]
     heads, buckets = table_ref.shape
-    half = lax.axis_index("shard")
-    own_at = pl.multiple_of(half * own_rows, own_rows)
-    other_at = pl.multiple_of((1 - half) * own_rows, own_rows)
+    sums = []
+    for grads, weights in (
+        (grads_own_ref, (value_own_ref, query_own_ref, key_own_ref)),
+        (grads_came_ref, (value_came_ref, query_came_ref, key_came_ref)),
+    ):
+        total = 0.0
+        for at, ref in enumerate(weights):
+            part = grads[:, at * columns : (at + 1) * columns]
+            total = total + product(part, ref[...], 1, 1)
+        sums.append(total)
+    grad_normed = sums[0] + sums[1]
     inputs = tokens_ref[...].astype(FULL)
-    grad_normed = normed_own_ref[...].astype(FULL) + normed_came_ref[...].astype(FULL)
-    grad_rows, grad_gain = norm_back(inputs, inverse_rms(inputs), gain_ref[...].reshape(1, -1), grad_normed)
-    grad_tokens_ref[...] = grad_rows
-    grad_tokens_ref[pl.ds(own_at, own_rows), :] += attention_own_ref[...].astype(FULL)
-    grad_tokens_ref[pl.ds(other_at, own_rows), :] += attention_came_ref[...].astype(FULL)
-    summed = small_own_ref[...] + small_came_ref[...]
+    grad_rows, grad_gain = norm_back(
+        inputs, inverse_rms(inputs), gain_ref[...].reshape(1, -1), grad_normed
+    )
+    grad_tokens_ref[...] = grad_rows + attention_ref[...].astype(FULL)
     table = jnp.concatenate([table_ref[...], jnp.zeros((heads, width - buckets), FULL)], axis=1)
-    more = small_ref.shape[0] - summed.shape[0] - heads - 1
+    early = -(-(experts + 1) // 8) * 8
     small_ref[...] = jnp.concatenate(
-        [summed, grad_gain, table, jnp.zeros((more, width), FULL)], axis=0
+        [
+            router_own_ref[...] + router_came_ref[...],
+            ffn_ref[...],
+            jnp.zeros((early - experts - 1, width), FULL),
+            grad_gain,
+            table,
+            jnp.zeros((small_ref.shape[0] - early - heads - 1, width), FULL),
+        ],
+        axis=0,
     ).astype(small_ref.dtype)
 
 
@@ -627,7 +639,7 @@
             pl.BlockSpec((block, width), lambda step: (step, 0)),
             pl.BlockSpec((8, 128), lambda step: (0, 0)),
         ],
-        compiler_params=pltpu.CompilerParams(vmem_limit_bytes=GRANT),
+        compiler_params=pltpu.CompilerParams(vmem_limit_bytes=56 * MEGABYTE),
         cost_estimate=pl.CostEstimate(flops=0, bytes_accessed=0, transcendentals=0),
     )(rows, rows_far, grad_produced, grad_produced_far, *wide)
 
@@ -757,56 +769,73 @@
     returned_grads = exchange(grad_back)
     rows_far, grad_produced_far = swap(rows), swap(grad_produced)
     active_far, grad_pre_far = swap(active_came), swap(grad_pre_came)
+    grad_router_came = swap(grad_router)
+    place_came, hidden_came, cotangent_came = swap(place), swap(hidden), swap(cotangent)
     small_rows = -(-(experts + 1) // 8) * 8
-    attention_own, small_own = run(
-        grad_hidden_kernel,
-        [((own_rows, width), LOW), ((small_rows, width), FULL)],
-        (place, returned_grads, hidden, ffn_gain, cotangent, grad_router),
-        after=(rows_far, grad_produced_far, active_far, grad_pre_far),
-    )
-    attention_came = swap(attention_own)
     part_rows = columns // PLANE
-    grad_normed_own, grad_table, back, *parts = run(
+    attention, grad_ffn, grads_low, grad_table, *parts = run(
         functools.partial(attention_back_kernel, head_size=head_size, bucket_total=buckets),
-        [((group_rows, width), LOW), ((heads, buckets), FULL), ((slots, width), LOW)]
+        [
+            ((group_rows, width), LOW),
+            ((1, width), FULL),
+            ((group_rows, 3 * columns), LOW),
+            ((heads, buckets), FULL),
+        ]
         + [((part_rows * (3 + width // group_rows), group_rows), LOW)] * PLANE,
         (
-            attention_own,
-            attention_came,
+            place,
+            place_came,
+            hidden,
+            hidden_came,
+            ffn_gain,
+            cotangent,
+            cotangent_came,
+            returned_grads,
+            swap(returned_grads),
             output_weight,
             mixed,
             qkv,
             probs,
-            query_weight,
-            key_weight,
-            value_weight,
-            back,
         ),
         scratch=(
-            pltpu.VMEM((group_rows, width), LOW),
             pltpu.VMEM((group_rows, 3 * columns), FULL),
             pltpu.VMEM((3 * columns, group_rows), FULL),
             pltpu.VMEM((columns, width), FULL),
         ),
+        after=(
+            rows_far,
+            grad_produced_far,
+            active_far,
+            grad_pre_far,
+            grad_router_came,
+        ),
     )
     parts = (parts[0],) + around(parts[1:], 1)
-    grad_normed_came = swap(grad_normed_own)
-    small_came = swap(small_own)
+    grads_came = swap(grads_low)
+    weights = (value_weight, query_weight, key_weight)
+    weights_came = tuple(swap(item) for item in weights)
     normed_far = tuple(swap(item) for item in normed_near)
     late_rows = -(-(heads + 1) // 8) * 8
-    grad_tokens, small = run(
+    grad_tokens, small, back = run(
         grad_tokens_kernel,
-        [((group_rows, width), FULL), ((small_rows + late_rows, width), LOW)],
+        [
+            ((group_rows, width), FULL),
+            ((small_rows + late_rows, width), LOW),
+            ((slots, width), LOW),
+        ],
         (
             tokens,
             attn_gain,
-            grad_normed_own,
-            grad_normed_came,
-            attention_own,
-            attention_came,
-            small_own,
-            small_came,
+            attention,
+            grad_router,
+            grad_router_came,
+            grad_ffn,
             grad_table,
+            back,
+            grads_low,
+            *weights,
+            *weights_came,
+            grads_came,
         ),
     )
     returned = exchange(back)
@@ -827,7 +856,6 @@
         [((all_rows, width), LOW)] * LINE,
         parts + normed_near + normed_far + (normed, small),
         scratch=(pltpu.VMEM((part_rows, width), FULL),) * 4,
-        after=(returned,),
     )
     (block_out,) = run(
         block_out_kernel, [((own_rows, width), LOW)], (place, returned, hidden)
@@ -864,6 +892,7 @@
         + [((heads, buckets), FULL)],
         gathered,
         scratch=(pltpu.VMEM((columns, width), FULL),) * 3,
+        after=(block_out,),
     )
     grad_router = grad_router.T
     grad_table = grad_table.T

time: 184 us -> 174 us (0.946)
  waiting for transfers between devices: 62.5 us -> 52.6 us
    ppermute x24, waiting for transfers between devices: 45.7 us -> 39.8 us  [hop(): lax.ppermute(item, 'expert', [(at, at ^ distance) for at in range(sources)])]
    all_to_all x3, waiting for transfers between devices: 10.3 us -> 5.66 us  [exchange(): lax.all_to_all(parts, 'expert', split_axis=0, concat_axis=0, tiled=True)]
    ppermute x24, starting transfers between devices: 35.5 us -> 33.3 us  [hop(): lax.ppermute(item, 'expert', [(at, at ^ distance) for at in range(sources)])]
    ppermute x13 -> x19, starting transfers between devices: 3.45 us -> 5.04 us  [swap(): return lax.ppermute(item, 'shard', [(0, 1), (1, 0)])]
    pallas_call x10 -> x9, Pallas kernels: 48.3 us -> 49 us  [run(): pl.pallas_call(body, out_shape=[jax.ShapeDtypeStruct(shape, dtype) for sh...]
    ppermute x13 -> x19, waiting for transfers between devices: 6.46 us -> 7.12 us  [swap(): return lax.ppermute(item, 'shard', [(0, 1), (1, 0)])]
    unnamed x82 -> x88, local copies, waits for them, and re-layouts: 7.04 us -> 6.47 us
  transfers between devices with their start and end apart: 40 -> 46, of which waited for: 18 -> 17; matrix products, arithmetic and copies ran while one was open for 0% -> 0% of each run, Pallas kernels for 12% -> 22%
where the time goes in v2:
time: 174 us; the launch traced here: 173 us
  starting transfers between devices  57.3 us (33%)
  Pallas kernels  55.7 us (32%)
  waiting for transfers between devices  52.6 us (30%)
  local copies, waits for them, and re-layouts  6.47 us (4%)
    pallas_call x9, Pallas kernels, run(): pl.pallas_call(body, out_shape=[jax.ShapeDtypeStruct(shape, dtype) for sh...  49 us
    ppermute x24, waiting for transfers between devices, hop(): lax.ppermute(item, 'expert', [(at, at ^ distance) for at in range(sources)])  39.8 us
    ppermute x24, starting transfers between devices, hop(): lax.ppermute(item, 'expert', [(at, at ^ distance) for at in range(sources)])  33.3 us
    all_to_all x3, starting transfers between devices, exchange(): lax.all_to_all(parts, 'expert', split_axis=0, concat_axis=0, tiled=True)  18.9 us
    ppermute x19, waiting for transfers between devices, swap(): return lax.ppermute(item, 'shard', [(0, 1), (1, 0)])  7.12 us
    pallas_call x1, Pallas kernels, expert_grads(): pl.pallas_call(expert_grads_kernel, grid=(units // block,), out_shape=[ja...  6.68 us
    unnamed x88, local copies, waits for them, and re-layouts  6.47 us
    all_to_all x3, waiting for transfers between devices, exchange(): lax.all_to_all(parts, 'expert', split_axis=0, concat_axis=0, tiled=True)  5.66 us
  transfers between devices with their start and end apart: 46, of which 17 were waited for; matrix products, arithmetic and copies ran while one was open for 0% of the time, Pallas kernels for 22%

profile of v2, /device:TPU:0, one launch (start us, length us, event | category | flops | bytes accessed | tf_op | source)
XLA Modules:
  0.0 173.3 jit_solution(9939723250937225328)
XLA Ops:
  0.6 0.5 collective-permute-start.4
  1.2 7.0 %shard_map.229 = (f32[128,768]{1,0:T(8,128)}, f32[128,768]{1,0:T(8,128)}, bf16[256,1152]{1,0:T(8,128)(2,1)}, bf16[6,256,256]{2,1,0:T(8,128)(2,1)}, bf16[256,768]{1,0:T(8,128)(2,1)}, /*index=5*/bf16[256,384]{1,0:T(8,128)(2,1)}) custom-call(s32[1,4]{1,0:T(1,128)} %refs_0_.2, bf16[256,768]{1,0:T(8,128)(2,1)} %refs_0_.3, f32[768]{0:T(1024)} %refs_1_.5, ...), custom_call_target="tpu_custom_call" | custom-call | tf_op jit(solution)/shard_map/pallas_call | solution.py:133
  8.2 0.5 collective-permute-start
  8.7 1.6 collective-permute-done.refs_6_
  10.3 0.7 copy-done.19
  11.0 3.1 %shard_map.230 = (bf16[256,128]{1,0:T(8,128)(2,1)}, f32[128,768]{1,0:T(8,128)}, bf16[256,1536]{1,0:T(8,128)(2,1)}, bf16[128,768]{1,0:T(8,128)(2,1)}) custom-call(s32[1,128]{1,0:T(1,128)} %bitcast.26, bf16[128,768]{1,0:T(8,128)(2,1)} %refs_5_.3, bf16[256,768]{1,0:T(8,128)(2,1)} %refs_0_.3, f32[128,768]{1,0:T(8,128)} %get-tuple-element.59.refs_3_, ...), custom_call_target="tpu_custom_call" | custom-call | tf_op jit(solution)/shard_map/pallas_call | solution.py:133
  14.1 8.2 %all-to-all-start = ((bf16[16,16,1536]{2,1,0:T(8,128)(2,1)}), bf16[16,16,1536]{2,1,0:T(8,128)(2,1)S(1)}, u32[]{:S(2)}, u32[]{:S(2)}) async-start(bf16[16,16,1536]{2,1,0:T(8,128)(2,1)} %bitcast.21), calls=%async_computation | async-start | bytes 1572864 | tf_op jit(solution)/shard_map/all_to_all | solution.py:693
  22.4 2.8 %collective-permute-start.8 = (bf16[128,768]{1,0:T(8,128)(2,1)}, bf16[128,768]{1,0:T(8,128)(2,1)S(1)}, u32[]{:S(2)}, u32[]{:S(2)}) collective-permute-start(bf16[128,768]{1,0:T(8,128)(2,1)} %get-tuple-element.65), channel_id=1, source_target_pairs={{0,6},{2,4},{4,2},{6,0},{8,14},{10,12},{12,10},{14,8},{16,22},{18,... | collective-permute-start | bytes 589832 | tf_op jit(solution)/shard_map/ppermute | solution.py:686
  25.2 0.6 collective-permute-start.7
  25.9 12.3 %collective-permute-done.8.refs_8_.refs_6_ = bf16[128,768]{1,0:T(8,128)(2,1)S(1)} collective-permute-done((bf16[128,768]{1,0:T(8,128)(2,1)}, bf16[128,768]{1,0:T(8,128)(2,1)S(1)}, u32[]{:S(2)}, u32[]{:S(2)}) %collective-permute-start.8) | collective-permute-done | bytes 196640 | tf_op jit(solution)/shard_map/ppermute | solution.py:686
  38.3 3.8 %collective-permute-done.7.refs_7_.refs_5_ = bf16[128,768]{1,0:T(8,128)(2,1)} collective-permute-done((bf16[128,768]{1,0:T(8,128)(2,1)}, bf16[128,768]{1,0:T(8,128)(2,1)}, u32[]{:S(2)}, u32[]{:S(2)}) %collective-permute-start.7) | collective-permute-done | bytes 196640 | tf_op jit(solution)/shard_map/ppermute | solution.py:686
  42.0 0.5 collective-permute-done.6.refs_6_.refs_4_
  42.5 1.4 copy-done.9
  44.2 11.8 %shard_map.231 = (bf16[256,768]{1,0:T(8,128)(2,1)}, bf16[256,768]{1,0:T(8,128)(2,1)}, f32[16,768]{1,0:T(8,128)}, bf16[256,768]{1,0:T(8,128)(2,1)}, bf16[256,768]...) custom-call(bf16[256,1536]{1,0:T(8,128)(2,1)} %bitcast.15, ...), custom_call_target="tpu_custom_call" | custom-call | tf_op jit(solution)/shard_map/pallas_call | solution.py:133
  56.0 6.8 %all-to-all-start.1 = ((bf16[16,16,768]{2,1,0:T(8,128)(2,1)}), bf16[16,16,768]{2,1,0:T(8,128)(2,1)}, u32[]{:S(2)}, u32[]{:S(2)}) async-start(bf16[16,16,768]{2,1,0:T(8,128)(2,1)} %bitcast.23), calls=%async_computation.1 | async-start | bytes 786432 | tf_op jit(solution)/shard_map/all_to_all | solution.py:693
  62.9 0.5 collective-permute-start.2
  63.5 0.4 collective-permute-start.3
  64.0 2.3 %collective-permute-done.3.refs_6_ = bf16[128,768]{1,0:T(8,128)(2,1)S(1)} collective-permute-done((bf16[128,768]{1,0:T(8,128)(2,1)S(1)}, bf16[128,768]{1,0:T(8,128)(2,1)S(1)}, u32[]{:S(2)}, u32[]{:S(2)}) %collective-permute-start.3) | collective-permute-done | bytes 196640 | tf_op jit(solution)/shard_map/ppermute | solution.py:683
  66.5 1.0 collective-permute-done.1.refs_1_
  67.6 0.4 collective-permute-start.14
  68.1 1.4 collective-permute-done.14.refs_17_.refs_4_
  69.5 5.7 %all-to-all-done.1 = bf16[16,16,768]{2,1,0:T(8,128)(2,1)} async-done(((bf16[16,16,768]{2,1,0:T(8,128)(2,1)}), bf16[16,16,768]{2,1,0:T(8,128)(2,1)}, u32[]{:S(2)}, u32[]{:S(2)}) %all-to-all-start.1) | async-done | bytes 393248 | tf_op jit(solution)/shard_map/all_to_all | solution.py:693
  75.2 0.5 collective-permute-start.16
  75.8 0.5 collective-permute-start.15
  76.3 0.8 collective-permute-done.9.refs_8_
  77.1 0.7 copy-done.18
  77.8 9.5 %shard_map.232 = (bf16[256,768]{1,0:T(8,128)(2,1)}, f32[1,768]{1,0:T(1,128)}, bf16[256,1152]{1,0:T(8,128)(2,1)}, f32[6,32]{1,0:T(8,128)}, bf16[576,256]{1,0:T(8,...) custom-call(bf16[256,128]{1,0:T(8,128)(2,1)} %get-tuple-element.62.refs_0_, ...), custom_call_target="tpu_custom_call" | custom-call | tf_op jit(solution)/shard_map/pallas_call | solution.py:133
  87.5 0.4 collective-permute-start.24
  87.9 0.6 collective-permute-start.19
  88.5 0.9 collective-permute-start.20
  89.4 2.1 %collective-permute-start.21 = (bf16[576,256]{1,0:T(8,128)(2,1)}, bf16[576,256]{1,0:T(8,128)(2,1)S(1)}, u32[]{:S(2)}, u32[]{:S(2)}) collective-permute-start(bf16[576,256]{1,0:T(8,128)(2,1)} %get-tuple-element.85), channel_id=1, source_target_pairs={{0,6},{2,4},{4,2},{6,0},{8,14},{10,12},{12,10},{14,8},{16,22},{18,... | collective-permute-start | bytes 884744 | tf_op jit(solution)/shard_map/ppermute | solution.py:686
  91.4 0.5 collective-permute-start.22
  92.3 5.7 %shard_map.233 = (f32[256,768]{1,0:T(8,128)}, bf16[32,768]{1,0:T(8,128)(2,1)}, bf16[256,768]{1,0:T(8,128)(2,1)}) custom-call(bf16[256,768]{1,0:T(8,128)(2,1)} %refs_0_.3, f32[768]{0:T(1024)} %refs_1_.5, bf16[256,768]{1,0:T(8,128)(2,1)} %get-tuple-element.75.refs_2_, f32[16,768]{1,0:T(8,128)} %get-tuple-element.74.refs_3_, f32[16,768]{1,0:T(8,128)} %copy-done.23, ...), custom_call_target="tpu_custom_call" | custom-call | tf_op jit(solution)/shard_map/pallas_call | solution.py:133
  98.0 3.8 %all-to-all-start.2 = ((bf16[16,16,768]{2,1,0:T(8,128)(2,1)}), bf16[16,16,768]{2,1,0:T(8,128)(2,1)S(1)}, u32[]{:S(2)}, u32[]{:S(2)}) async-start(bf16[16,16,768]{2,1,0:T(8,128)(2,1)} %bitcast.22), calls=%async_computation.2 | async-start | bytes 786432 | tf_op jit(solution)/shard_map/all_to_all | solution.py:693
  101.9 1.9 %collective-permute-done.21.refs_3_ = bf16[576,256]{1,0:T(8,128)(2,1)S(1)} collective-permute-done((bf16[576,256]{1,0:T(8,128)(2,1)}, bf16[576,256]{1,0:T(8,128)(2,1)S(1)}, u32[]{:S(2)}, u32[]{:S(2)}) %collective-permute-start.21) | collective-permute-done | bytes 294944 | tf_op jit(solution)/shard_map/ppermute | solution.py:686
  103.8 0.7 copy-done.22
  104.5 4.7 %shard_map.235 = (bf16[128,768]{1,0:T(8,128)(2,1)}, bf16[128,768]{1,0:T(8,128)(2,1)}, bf16[128,768]{1,0:T(8,128)(2,1)}, bf16[128,768]{1,0:T(8,128)(2,1)}) custom-call(bf16[576,256]{1,0:T(8,128)(2,1)} %get-tuple-element.82.refs_0_, bf16[576,256]{1,0:T(8,128)(2,1)} %copy-done.20, bf16[576,256]{1,0:T(8,128)(2,1)} %copy-done.21, bf16[576,256]{1,0:T(8,128)(2,1)} %copy-done.22, ...), custom_call_target="tpu_custom_call" | custom-call | tf_op jit(solution)/shard_map/pallas_call | solution.py:133
  109.2 1.2 collective-permute-start.25
  110.4 1.4 collective-permute-start.26
  111.8 1.9 %collective-permute-start.27 = (bf16[128,768]{1,0:T(8,128)(2,1)}, bf16[128,768]{1,0:T(8,128)(2,1)S(1)}, u32[]{:S(2)}, u32[]{:S(2)}) collective-permute-start(bf16[128,768]{1,0:T(8,128)(2,1)} %get-tuple-element.90), channel_id=1, source_target_pairs={{0,24},{2,26},{4,28},{6,30},{8,16},{10,18},{12,20},{14,22},{16,8},... | collective-permute-start | bytes 589832 | tf_op jit(solution)/shard_map/ppermute | solution.py:686
  113.7 6.7 %shard_map.236 = (f32[768,1536]{1,0:T(8,128)}, f32[1536,768]{1,0:T(8,128)}, f32[8,128]{1,0:T(8,128)}) custom-call(bf16[256,768]{1,0:T(8,128)(2,1)} %get-tuple-element.70.rows_ref, bf16[256,768]{1,0:T(8,128)(2,1)} %collective-permute-done.10.refs_13_.rows_far_ref, bf16[256,768]{1,0:T(8,128)(2,1)} %get-tuple-element.71.grad_produced_ref, ...), custom_call_target="tpu_custom_call" | custom-call | tf_op jit(solution)/shard_map/pallas_call | solution.py:628
  120.3 7.4 %collective-permute-done.26.refs_2_ = bf16[128,768]{1,0:T(8,128)(2,1)S(1)} collective-permute-done((bf16[128,768]{1,0:T(8,128)(2,1)}, bf16[128,768]{1,0:T(8,128)(2,1)S(1)}, u32[]{:S(2)}, u32[]{:S(2)}) %collective-permute-start.26) | collective-permute-done | bytes 196640 | tf_op jit(solution)/shard_map/ppermute | solution.py:686
  127.7 0.7 copy-done.2
  128.5 1.8 %collective-permute-start.39 = (bf16[96,768]{1,0:T(8,128)(2,1)S(1)}, bf16[96,768]{1,0:T(8,128)(2,1)S(1)}, u32[]{:S(2)}, u32[]{:S(2)}) collective-permute-start(bf16[96,768]{1,0:T(8,128)(2,1)S(1)} %get-tuple-element.95), channel_id=1, source_target_pairs={{0,24},{2,26},{4,28},{6,30},{8,16},{10,18},{12,20},{14,22},{16,8},... | collective-permute-start | bytes 442376 | tf_op jit(solution)/shard_map/ppermute | solution.py:686
  130.4 1.9 %collective-permute-start.30 = (bf16[128,768]{1,0:T(8,128)(2,1)S(1)}, bf16[128,768]{1,0:T(8,128)(2,1)S(1)}, u32[]{:S(2)}, u32[]{:S(2)}) collective-permute-start(bf16[128,768]{1,0:T(8,128)(2,1)S(1)} %get-tuple-element.94.refs_0_), channel_id=1, source_target_pairs={{0,6},{2,4},{4,2},{6,0},{8,14},{10,12},{12,10},{14,8},{16,22},{18,... | collective-permute-start | bytes 589832 | tf_op jit(solution)/shard_map/ppermute | solution.py:686
  132.3 0.4 collective-permute-start.29
  132.7 5.5 %collective-permute-start.35 = (bf16[96,768]{1,0:T(8,128)(2,1)S(1)}, bf16[96,768]{1,0:T(8,128)(2,1)S(1)}, u32[]{:S(2)}, u32[]{:S(2)}) collective-permute-start(bf16[96,768]{1,0:T(8,128)(2,1)S(1)} %get-tuple-element.95), channel_id=1, source_target_pairs={{0,16},{2,18},{4,20},{6,22},{8,24},{10,26},{12,28},{14,30},{16,0},... | collective-permute-start | bytes 442376 | tf_op jit(solution)/shard_map/ppermute | solution.py:686
  138.2 0.6 collective-permute-start.28
  138.9 5.7 %collective-permute-done.35.refs_8_ = bf16[96,768]{1,0:T(8,128)(2,1)S(1)} collective-permute-done((bf16[96,768]{1,0:T(8,128)(2,1)S(1)}, bf16[96,768]{1,0:T(8,128)(2,1)S(1)}, u32[]{:S(2)}, u32[]{:S(2)}) %collective-permute-start.35) | collective-permute-done | bytes 147488 | tf_op jit(solution)/shard_map/ppermute | solution.py:686
  144.6 2.3 %collective-permute-start.42 = (bf16[96,768]{1,0:T(8,128)(2,1)S(1)}, bf16[96,768]{1,0:T(8,128)(2,1)S(1)}, u32[]{:S(2)}, u32[]{:S(2)}) collective-permute-start(bf16[96,768]{1,0:T(8,128)(2,1)S(1)} %collective-permute-done.39.refs_12_), channel_id=1, source_target_pairs={{0,6},{2,4},{4,2},{6,0},{8,14},{10,12},{12,10},{14,8},{16,22},{18,... | collective-permute-start | bytes 442376 | tf_op jit(solution)/shard_map/ppermute | solution.py:686
  147.2 0.9 collective-permute-start.40
  148.1 2.3 %collective-permute-start.38 = (bf16[96,768]{1,0:T(8,128)(2,1)S(1)}, bf16[96,768]{1,0:T(8,128)(2,1)S(1)}, u32[]{:S(2)}, u32[]{:S(2)}) collective-permute-start(bf16[96,768]{1,0:T(8,128)(2,1)S(1)} %collective-permute-done.35.refs_8_), channel_id=1, source_target_pairs={{0,6},{2,4},{4,2},{6,0},{8,14},{10,12},{12,10},{14,8},{16,22},{18,... | collective-permute-start | bytes 442376 | tf_op jit(solution)/shard_map/ppermute | solution.py:686
  150.7 0.6 collective-permute-done.42.refs_15_
  151.3 1.2 collective-permute-start.36
  152.5 2.8 %collective-permute-done.41.refs_14_ = bf16[96,768]{1,0:T(8,128)(2,1)S(1)} collective-permute-done((bf16[96,768]{1,0:T(8,128)(2,1)S(1)}, bf16[96,768]{1,0:T(8,128)(2,1)S(1)}, u32[]{:S(2)}, u32[]{:S(2)}) %collective-permute-start.41) | collective-permute-done | bytes 147488 | tf_op jit(solution)/shard_map/ppermute | solution.py:686
  155.3 3.6 %collective-permute-start.34 = (bf16[96,768]{1,0:T(8,128)(2,1)S(1)}, bf16[96,768]{1,0:T(8,128)(2,1)S(1)}, u32[]{:S(2)}, u32[]{:S(2)}) collective-permute-start(bf16[96,768]{1,0:T(8,128)(2,1)S(1)} %collective-permute-done.31.refs_4_), channel_id=1, source_target_pairs={{0,6},{2,4},{4,2},{6,0},{8,14},{10,12},{12,10},{14,8},{16,22},{18,... | collective-permute-start | bytes 442376 | tf_op jit(solution)/shard_map/ppermute | solution.py:686
  158.9 0.6 collective-permute-start.32
  159.6 0.7 copy-done.10
  160.3 2.1 %shard_map.234.refs_16_ = bf16[128,768]{1,0:T(8,128)(2,1)} custom-call(bf16[256,128]{1,0:T(8,128)(2,1)} %get-tuple-element.62.refs_0_, bf16[256,768]{1,0:T(8,128)(2,1)} %bitcast.20, f32[128,768]{1,0:T(8,128)} %get-tuple-element.63.refs_2_), custom_call_target="tpu_custom_call" | custom-call | tf_op jit(solution)/shard_map/pallas_call | solution.py:133
  162.5 2.2 %collective-permute-done.34.refs_7_ = bf16[96,768]{1,0:T(8,128)(2,1)S(1)} collective-permute-done((bf16[96,768]{1,0:T(8,128)(2,1)S(1)}, bf16[96,768]{1,0:T(8,128)(2,1)S(1)}, u32[]{:S(2)}, u32[]{:S(2)}) %collective-permute-start.34) | collective-permute-done | bytes 147488 | tf_op jit(solution)/shard_map/ppermute | solution.py:686
  164.7 2.0 %collective-permute-done.33.refs_6_ = bf16[96,768]{1,0:T(8,128)(2,1)S(1)} collective-permute-done((bf16[96,768]{1,0:T(8,128)(2,1)S(1)}, bf16[96,768]{1,0:T(8,128)(2,1)S(1)}, u32[]{:S(2)}, u32[]{:S(2)}) %collective-permute-start.33) | collective-permute-done | bytes 147488 | tf_op jit(solution)/shard_map/ppermute | solution.py:686
  166.6 0.7 collective-permute-done.32.refs_5_
  167.4 0.7 copy-done.42
  168.1 5.1 %shard_map.238 = (f32[768,384]{1,0:T(8,128)}, f32[768,384]{1,0:T(8,128)}, f32[768,384]{1,0:T(8,128)}, f32[384,768]{1,0:T(8,128)}, f32[16,768]{1,0:T(8,128)}, /*i...) custom-call(bf16[128,768]{1,0:T(8,128)(2,1)} %copy-done.1, bf16[128,768]{1,0:T(8,128)(2,1)} %copy-done.27, ...), custom_call_target="tpu_custom_call" | custom-call | tf_op jit(solution)/shard_map/pallas_call | solution.py:133
  (126 shorter events, 2.7 us)
Async XLA Ops:
  0.6 41.9 %collective-permute-start.4 = (bf16[768,1536]{1,0:T(8,128)(2,1)}, bf16[768,1536]{1,0:T(8,128)(2,1)S(1)}, u32[]{:S(2)}, u32[]{:S(2)}) collective-permute-start(bf16[768,1536]{1,0:T(8,128)(2,1)} %bitcast.16), channel_id=1, source_target_pairs={{0,1},{1,0},{2,3},{3,2},{4,5},{5,4},{6,7},{7,6},{8,9},{9,8},{10,11... | collective-permute-start | bytes 7077896 | tf_op jit(solution)/shard_map/ppermute | solution.py:683
  1.2 41.4 %collective-permute-start.5 = (bf16[1536,768]{1,0:T(8,128)(2,1)}, bf16[1536,768]{1,0:T(8,128)(2,1)}, u32[]{:S(2)}, u32[]{:S(2)}) collective-permute-start(bf16[1536,768]{1,0:T(8,128)(2,1)} %bitcast.18), channel_id=1, source_target_pairs={{0,1},{1,0},{2,3},{3,2},{4,5},{5,4},{6,7},{7,6},{8,9},{9,8},{10,11... | collective-permute-start | bytes 7077896 | tf_op jit(solution)/shard_map/ppermute | solution.py:683
  8.2 2.1 %collective-permute-start = (f32[128,768]{1,0:T(8,128)}, f32[128,768]{1,0:T(8,128)S(1)}, u32[]{:S(2)}, u32[]{:S(2)}) collective-permute-start(f32[128,768]{1,0:T(8,128)} %get-tuple-element.61), channel_id=1, source_target_pairs={{0,1},{1,0},{2,3},{3,2},{4,5},{5,4},{6,7},{7,6},{8,9},{9,8},{10,11... | collective-permute-start | bytes 1179656 | tf_op jit(solution)/shard_map/ppermute | solution.py:683
  14.1 28.4 %all-to-all-start = ((bf16[16,16,1536]{2,1,0:T(8,128)(2,1)}), bf16[16,16,1536]{2,1,0:T(8,128)(2,1)S(1)}, u32[]{:S(2)}, u32[]{:S(2)}) async-start(bf16[16,16,1536]{2,1,0:T(8,128)(2,1)} %bitcast.21), calls=%async_computation | async-start | bytes 1572864 | tf_op jit(solution)/shard_map/all_to_all | solution.py:693
  22.4 15.9 %collective-permute-start.8 = (bf16[128,768]{1,0:T(8,128)(2,1)}, bf16[128,768]{1,0:T(8,128)(2,1)S(1)}, u32[]{:S(2)}, u32[]{:S(2)}) collective-permute-start(bf16[128,768]{1,0:T(8,128)(2,1)} %get-tuple-element.65), channel_id=1, source_target_pairs={{0,6},{2,4},{4,2},{6,0},{8,14},{10,12},{12,10},{14,8},{16,22},{18,... | collective-permute-start | bytes 589832 | tf_op jit(solution)/shard_map/ppermute | solution.py:686
  25.2 16.8 %collective-permute-start.7 = (bf16[128,768]{1,0:T(8,128)(2,1)}, bf16[128,768]{1,0:T(8,128)(2,1)}, u32[]{:S(2)}, u32[]{:S(2)}) collective-permute-start(bf16[128,768]{1,0:T(8,128)(2,1)} %get-tuple-element.65), channel_id=1, source_target_pairs={{0,4},{2,6},{4,0},{6,2},{8,12},{10,14},{12,8},{14,10},{16,20},{18,... | collective-permute-start | bytes 589832 | tf_op jit(solution)/shard_map/ppermute | solution.py:686
  25.8 16.7 %collective-permute-start.6 = (bf16[128,768]{1,0:T(8,128)(2,1)}, bf16[128,768]{1,0:T(8,128)(2,1)}, u32[]{:S(2)}, u32[]{:S(2)}) collective-permute-start(bf16[128,768]{1,0:T(8,128)(2,1)} %get-tuple-element.65), channel_id=1, source_target_pairs={{0,2},{2,0},{4,6},{6,4},{8,10},{10,8},{12,14},{14,12},{16,18},{18,... | collective-permute-start | bytes 589832 | tf_op jit(solution)/shard_map/ppermute | solution.py:686
  44.2 19.4 %copy-start.11 = (bf16[128,768]{1,0:T(8,128)(2,1)S(1)}, bf16[128,768]{1,0:T(8,128)(2,1)}, u32[]{:S(2)}) copy-start(bf16[128,768]{1,0:T(8,128)(2,1)} %refs_5_.3) | copy-start | bytes 589828
  44.2 31.0 %copy-start.6 = (bf16[768,384]{1,0:T(8,128)(2,1)S(1)}, bf16[768,384]{1,0:T(8,128)(2,1)}, u32[]{:S(2)}) copy-start(bf16[768,384]{1,0:T(8,128)(2,1)} %refs_10_.1) | copy-start | bytes 1769476
  44.2 31.5 %copy-start.7 = (bf16[768,384]{1,0:T(8,128)(2,1)S(1)}, bf16[768,384]{1,0:T(8,128)(2,1)}, u32[]{:S(2)}) copy-start(bf16[768,384]{1,0:T(8,128)(2,1)} %refs_11_.1) | copy-start | bytes 1769476
  44.2 31.6 %copy-start.8 = (bf16[768,384]{1,0:T(8,128)(2,1)S(1)}, bf16[768,384]{1,0:T(8,128)(2,1)}, u32[]{:S(2)}) copy-start(bf16[768,384]{1,0:T(8,128)(2,1)} %refs_9_.3) | copy-start | bytes 1769476
  56.0 19.1 %all-to-all-start.1 = ((bf16[16,16,768]{2,1,0:T(8,128)(2,1)}), bf16[16,16,768]{2,1,0:T(8,128)(2,1)}, u32[]{:S(2)}, u32[]{:S(2)}) async-start(bf16[16,16,768]{2,1,0:T(8,128)(2,1)} %bitcast.23), calls=%async_computation.1 | async-start | bytes 786432 | tf_op jit(solution)/shard_map/all_to_all | solution.py:693
  62.9 12.9 %collective-permute-start.12 = (bf16[256,1536]{1,0:T(8,128)(2,1)}, bf16[256,1536]{1,0:T(8,128)(2,1)S(1)}, u32[]{:S(2)}, u32[]{:S(2)}) collective-permute-start(bf16[256,1536]{1,0:T(8,128)(2,1)} %get-tuple-element.72), channel_id=1, source_target_pairs={{0,1},{1,0},{2,3},{3,2},{4,5},{5,4},{6,7},{7,6},{8,9},{9,8},{10,11... | collective-permute-start | bytes 2359304 | tf_op jit(solution)/shard_map/ppermute | solution.py:683
  62.9 4.7 %collective-permute-start.2 = (f32[128,768]{1,0:T(8,128)}, f32[128,768]{1,0:T(8,128)}, u32[]{:S(2)}, u32[]{:S(2)}) collective-permute-start(f32[128,768]{1,0:T(8,128)} %get-tuple-element.63.refs_2_), channel_id=1, source_target_pairs={{0,1},{1,0},{2,3},{3,2},{4,5},{5,4},{6,7},{7,6},{8,9},{9,8},{10,11... | collective-permute-start | bytes 1179656 | tf_op jit(solution)/shard_map/ppermute | solution.py:683
  63.4 12.8 %collective-permute-start.13 = (bf16[256,1536]{1,0:T(8,128)(2,1)}, bf16[256,1536]{1,0:T(8,128)(2,1)S(1)}, u32[]{:S(2)}, u32[]{:S(2)}) collective-permute-start(bf16[256,1536]{1,0:T(8,128)(2,1)} %get-tuple-element.73), channel_id=1, source_target_pairs={{0,1},{1,0},{2,3},{3,2},{4,5},{5,4},{6,7},{7,6},{8,9},{9,8},{10,11... | collective-permute-start | bytes 2359304 | tf_op jit(solution)/shard_map/ppermute | solution.py:683
  63.5 2.8 %collective-permute-start.3 = (bf16[128,768]{1,0:T(8,128)(2,1)S(1)}, bf16[128,768]{1,0:T(8,128)(2,1)S(1)}, u32[]{:S(2)}, u32[]{:S(2)}) collective-permute-start(bf16[128,768]{1,0:T(8,128)(2,1)S(1)} %copy-done.11), channel_id=1, source_target_pairs={{0,1},{1,0},{2,3},{3,2},{4,5},{5,4},{6,7},{7,6},{8,9},{9,8},{10,11... | collective-permute-start | bytes 589832 | tf_op jit(solution)/shard_map/ppermute | solution.py:683
  63.9 3.5 %collective-permute-start.1 = (bf16[256,128]{1,0:T(8,128)(2,1)}, bf16[256,128]{1,0:T(8,128)(2,1)S(1)}, u32[]{:S(2)}, u32[]{:S(2)}) collective-permute-start(bf16[256,128]{1,0:T(8,128)(2,1)} %get-tuple-element.62.refs_0_), channel_id=1, source_target_pairs={{0,1},{1,0},{2,3},{3,2},{4,5},{5,4},{6,7},{7,6},{8,9},{9,8},{10,11... | collective-permute-start | bytes 196616 | tf_op jit(solution)/shard_map/ppermute | solution.py:683
  66.3 8.8 %collective-permute-start.10 = (bf16[256,768]{1,0:T(8,128)(2,1)}, bf16[256,768]{1,0:T(8,128)(2,1)}, u32[]{:S(2)}, u32[]{:S(2)}) collective-permute-start(bf16[256,768]{1,0:T(8,128)(2,1)} %get-tuple-element.70.rows_ref), channel_id=1, source_target_pairs={{0,1},{1,0},{2,3},{3,2},{4,5},{5,4},{6,7},{7,6},{8,9},{9,8},{10,11... | collective-permute-start | bytes 1179656 | tf_op jit(solution)/shard_map/ppermute | solution.py:683
  67.5 8.2 %collective-permute-start.11 = (bf16[256,768]{1,0:T(8,128)(2,1)}, bf16[256,768]{1,0:T(8,128)(2,1)}, u32[]{:S(2)}, u32[]{:S(2)}) collective-permute-start(bf16[256,768]{1,0:T(8,128)(2,1)} %get-tuple-element.71.grad_produced_ref), channel_id=1, source_target_pairs={{0,1},{1,0},{2,3},{3,2},{4,5},{5,4},{6,7},{7,6},{8,9},{9,8},{10,11... | collective-permute-start | bytes 1179656 | tf_op jit(solution)/shard_map/ppermute | solution.py:683
  67.6 1.9 %collective-permute-start.14 = (f32[16,768]{1,0:T(8,128)}, f32[16,768]{1,0:T(8,128)S(1)}, u32[]{:S(2)}, u32[]{:S(2)}) collective-permute-start(f32[16,768]{1,0:T(8,128)} %get-tuple-element.74.refs_3_), channel_id=1, source_target_pairs={{0,1},{1,0},{2,3},{3,2},{4,5},{5,4},{6,7},{7,6},{8,9},{9,8},{10,11... | collective-permute-start | bytes 147464 | tf_op jit(solution)/shard_map/ppermute | solution.py:683
  75.1 1.9 %collective-permute-start.9 = (bf16[256,768]{1,0:T(8,128)(2,1)}, bf16[256,768]{1,0:T(8,128)(2,1)S(1)}, u32[]{:S(2)}, u32[]{:S(2)}) collective-permute-start(bf16[256,768]{1,0:T(8,128)(2,1)} %bitcast.8.refs_7_), channel_id=1, source_target_pairs={{0,1},{1,0},{2,3},{3,2},{4,5},{5,4},{6,7},{7,6},{8,9},{9,8},{10,11... | collective-permute-start | bytes 1179656 | tf_op jit(solution)/shard_map/ppermute | solution.py:683
  75.2 12.7 %collective-permute-start.16 = (bf16[768,384]{1,0:T(8,128)(2,1)S(1)}, bf16[768,384]{1,0:T(8,128)(2,1)S(1)}, u32[]{:S(2)}, u32[]{:S(2)}) collective-permute-start(bf16[768,384]{1,0:T(8,128)(2,1)S(1)} %copy-done.6), channel_id=1, source_target_pairs={{0,1},{1,0},{2,3},{3,2},{4,5},{5,4},{6,7},{7,6},{8,9},{9,8},{10,11... | collective-permute-start | bytes 1769480 | tf_op jit(solution)/shard_map/ppermute | solution.py:683
  75.7 12.8 %collective-permute-start.17 = (bf16[768,384]{1,0:T(8,128)(2,1)S(1)}, bf16[768,384]{1,0:T(8,128)(2,1)S(1)}, u32[]{:S(2)}, u32[]{:S(2)}) collective-permute-start(bf16[768,384]{1,0:T(8,128)(2,1)S(1)} %copy-done.7), channel_id=1, source_target_pairs={{0,1},{1,0},{2,3},{3,2},{4,5},{5,4},{6,7},{7,6},{8,9},{9,8},{10,11... | collective-permute-start | bytes 1769480 | tf_op jit(solution)/shard_map/ppermute | solution.py:683
  75.8 13.6 %collective-permute-start.15 = (bf16[768,384]{1,0:T(8,128)(2,1)S(1)}, bf16[768,384]{1,0:T(8,128)(2,1)S(1)}, u32[]{:S(2)}, u32[]{:S(2)}) collective-permute-start(bf16[768,384]{1,0:T(8,128)(2,1)S(1)} %copy-done.8), channel_id=1, source_target_pairs={{0,1},{1,0},{2,3},{3,2},{4,5},{5,4},{6,7},{7,6},{8,9},{9,8},{10,11... | collective-permute-start | bytes 1769480 | tf_op jit(solution)/shard_map/ppermute | solution.py:683
  77.8 9.7 %copy-start.13 = (bf16[128,768]{1,0:T(8,128)(2,1)S(1)}, bf16[128,768]{1,0:T(8,128)(2,1)}, u32[]{:S(2)}) copy-start(bf16[128,768]{1,0:T(8,128)(2,1)} %copy-done.12) | copy-start | bytes 589828
  87.3 4.1 %collective-permute-start.18 = (bf16[256,1152]{1,0:T(8,128)(2,1)}, bf16[256,1152]{1,0:T(8,128)(2,1)S(1)}, u32[]{:S(2)}, u32[]{:S(2)}) collective-permute-start(bf16[256,1152]{1,0:T(8,128)(2,1)} %get-tuple-element.79.refs_8_), channel_id=1, source_target_pairs={{0,1},{1,0},{2,3},{3,2},{4,5},{5,4},{6,7},{7,6},{8,9},{9,8},{10,11... | collective-permute-start | bytes 1769480 | tf_op jit(solution)/shard_map/ppermute | solution.py:683
  87.5 3.9 %collective-permute-start.24 = (bf16[128,768]{1,0:T(8,128)(2,1)S(1)}, bf16[128,768]{1,0:T(8,128)(2,1)S(1)}, u32[]{:S(2)}, u32[]{:S(2)}) collective-permute-start(bf16[128,768]{1,0:T(8,128)(2,1)S(1)} %copy-done.13), channel_id=1, source_target_pairs={{0,1},{1,0},{2,3},{3,2},{4,5},{5,4},{6,7},{7,6},{8,9},{9,8},{10,11... | collective-permute-start | bytes 589832 | tf_op jit(solution)/shard_map/ppermute | solution.py:683
  87.9 13.9 %collective-permute-start.19 = (bf16[576,256]{1,0:T(8,128)(2,1)}, bf16[576,256]{1,0:T(8,128)(2,1)S(1)}, u32[]{:S(2)}, u32[]{:S(2)}) collective-permute-start(bf16[576,256]{1,0:T(8,128)(2,1)} %get-tuple-element.83), channel_id=1, source_target_pairs={{0,2},{2,0},{4,6},{6,4},{8,10},{10,8},{12,14},{14,12},{16,18},{18,... | collective-permute-start | bytes 884744 | tf_op jit(solution)/shard_map/ppermute | solution.py:686
  88.5 13.4 %collective-permute-start.20 = (bf16[576,256]{1,0:T(8,128)(2,1)}, bf16[576,256]{1,0:T(8,128)(2,1)S(1)}, u32[]{:S(2)}, u32[]{:S(2)}) collective-permute-start(bf16[576,256]{1,0:T(8,128)(2,1)} %get-tuple-element.84), channel_id=1, source_target_pairs={{0,4},{2,6},{4,0},{6,2},{8,12},{10,14},{12,8},{14,10},{16,20},{18,... | collective-permute-start | bytes 884744 | tf_op jit(solution)/shard_map/ppermute | solution.py:686
  89.4 14.4 %collective-permute-start.21 = (bf16[576,256]{1,0:T(8,128)(2,1)}, bf16[576,256]{1,0:T(8,128)(2,1)S(1)}, u32[]{:S(2)}, u32[]{:S(2)}) collective-permute-start(bf16[576,256]{1,0:T(8,128)(2,1)} %get-tuple-element.85), channel_id=1, source_target_pairs={{0,6},{2,4},{4,2},{6,0},{8,14},{10,12},{12,10},{14,8},{16,22},{18,... | collective-permute-start | bytes 884744 | tf_op jit(solution)/shard_map/ppermute | solution.py:686
  91.4 12.4 %copy-start.28 = (bf16[128,768]{1,0:T(8,128)(2,1)}, bf16[128,768]{1,0:T(8,128)(2,1)S(1)}, u32[]{:S(2)}) copy-start(bf16[128,768]{1,0:T(8,128)(2,1)S(1)} %collective-permute-done.24.refs_9_) | copy-start | bytes 589828
  91.4 10.4 %collective-permute-start.23 = (bf16[128,768]{1,0:T(8,128)(2,1)}, bf16[128,768]{1,0:T(8,128)(2,1)S(1)}, u32[]{:S(2)}, u32[]{:S(2)}) collective-permute-start(bf16[128,768]{1,0:T(8,128)(2,1)} %collective-permute-done.7.refs_7_.refs_5_), channel_id=1, source_target_pairs={{0,1},{1,0},{2,3},{3,2},{4,5},{5,4},{6,7},{7,6},{8,9},{9,8},{10,11... | collective-permute-start | bytes 589832 | tf_op jit(solution)/shard_map/ppermute | solution.py:683
  91.4 10.4 %collective-permute-start.22 = (bf16[128,768]{1,0:T(8,128)(2,1)}, bf16[128,768]{1,0:T(8,128)(2,1)S(1)}, u32[]{:S(2)}, u32[]{:S(2)}) collective-permute-start(bf16[128,768]{1,0:T(8,128)(2,1)} %collective-permute-done.6.refs_6_.refs_4_), channel_id=1, source_target_pairs={{0,1},{1,0},{2,3},{3,2},{4,5},{5,4},{6,7},{7,6},{8,9},{9,8},{10,11... | collective-permute-start | bytes 589832 | tf_op jit(solution)/shard_map/ppermute | solution.py:683
  98.0 61.6 %all-to-all-start.2 = ((bf16[16,16,768]{2,1,0:T(8,128)(2,1)}), bf16[16,16,768]{2,1,0:T(8,128)(2,1)S(1)}, u32[]{:S(2)}, u32[]{:S(2)}) async-start(bf16[16,16,768]{2,1,0:T(8,128)(2,1)} %bitcast.22), calls=%async_computation.2 | async-start | bytes 786432 | tf_op jit(solution)/shard_map/all_to_all | solution.py:693
  109.2 11.1 %collective-permute-start.25 = (bf16[128,768]{1,0:T(8,128)(2,1)}, bf16[128,768]{1,0:T(8,128)(2,1)S(1)}, u32[]{:S(2)}, u32[]{:S(2)}) collective-permute-start(bf16[128,768]{1,0:T(8,128)(2,1)} %get-tuple-element.88), channel_id=1, source_target_pairs={{0,8},{2,10},{4,12},{6,14},{8,0},{10,2},{12,4},{14,6},{16,24},{18,... | collective-permute-start | bytes 589832 | tf_op jit(solution)/shard_map/ppermute | solution.py:686
  110.4 17.4 %collective-permute-start.26 = (bf16[128,768]{1,0:T(8,128)(2,1)}, bf16[128,768]{1,0:T(8,128)(2,1)S(1)}, u32[]{:S(2)}, u32[]{:S(2)}) collective-permute-start(bf16[128,768]{1,0:T(8,128)(2,1)} %get-tuple-element.89), channel_id=1, source_target_pairs={{0,16},{2,18},{4,20},{6,22},{8,24},{10,26},{12,28},{14,30},{16,0},... | collective-permute-start | bytes 589832 | tf_op jit(solution)/shard_map/ppermute | solution.py:686
  111.8 16.0 %collective-permute-start.27 = (bf16[128,768]{1,0:T(8,128)(2,1)}, bf16[128,768]{1,0:T(8,128)(2,1)S(1)}, u32[]{:S(2)}, u32[]{:S(2)}) collective-permute-start(bf16[128,768]{1,0:T(8,128)(2,1)} %get-tuple-element.90), channel_id=1, source_target_pairs={{0,24},{2,26},{4,28},{6,30},{8,16},{10,18},{12,20},{14,22},{16,8},... | collective-permute-start | bytes 589832 | tf_op jit(solution)/shard_map/ppermute | solution.py:686
  113.7 14.1 %copy-start = (bf16[128,768]{1,0:T(8,128)(2,1)S(1)}, bf16[128,768]{1,0:T(8,128)(2,1)}, u32[]{:S(2)}) copy-start(bf16[128,768]{1,0:T(8,128)(2,1)} %get-tuple-element.87.refs_0_) | copy-start | bytes 589828
  128.5 38.8 %copy-start.1 = (bf16[128,768]{1,0:T(8,128)(2,1)}, bf16[128,768]{1,0:T(8,128)(2,1)S(1)}, u32[]{:S(2)}) copy-start(bf16[128,768]{1,0:T(8,128)(2,1)S(1)} %get-tuple-element.94.refs_0_) | copy-start | bytes 589828
  128.5 9.7 %collective-permute-start.39 = (bf16[96,768]{1,0:T(8,128)(2,1)S(1)}, bf16[96,768]{1,0:T(8,128)(2,1)S(1)}, u32[]{:S(2)}, u32[]{:S(2)}) collective-permute-start(bf16[96,768]{1,0:T(8,128)(2,1)S(1)} %get-tuple-element.95), channel_id=1, source_target_pairs={{0,24},{2,26},{4,28},{6,30},{8,16},{10,18},{12,20},{14,22},{16,8},... | collective-permute-start | bytes 442376 | tf_op jit(solution)/shard_map/ppermute | solution.py:686
  130.4 16.8 %collective-permute-start.30 = (bf16[128,768]{1,0:T(8,128)(2,1)S(1)}, bf16[128,768]{1,0:T(8,128)(2,1)S(1)}, u32[]{:S(2)}, u32[]{:S(2)}) collective-permute-start(bf16[128,768]{1,0:T(8,128)(2,1)S(1)} %get-tuple-element.94.refs_0_), channel_id=1, source_target_pairs={{0,6},{2,4},{4,2},{6,0},{8,14},{10,12},{12,10},{14,8},{16,22},{18,... | collective-permute-start | bytes 589832 | tf_op jit(solution)/shard_map/ppermute | solution.py:686
  132.3 15.8 %collective-permute-start.29 = (bf16[128,768]{1,0:T(8,128)(2,1)S(1)}, bf16[128,768]{1,0:T(8,128)(2,1)S(1)}, u32[]{:S(2)}, u32[]{:S(2)}) collective-permute-start(bf16[128,768]{1,0:T(8,128)(2,1)S(1)} %get-tuple-element.94.refs_0_), channel_id=1, source_target_pairs={{0,4},{2,6},{4,0},{6,2},{8,12},{10,14},{12,8},{14,10},{16,20},{18,... | collective-permute-start | bytes 589832 | tf_op jit(solution)/shard_map/ppermute | solution.py:686
  132.7 11.9 %collective-permute-start.35 = (bf16[96,768]{1,0:T(8,128)(2,1)S(1)}, bf16[96,768]{1,0:T(8,128)(2,1)S(1)}, u32[]{:S(2)}, u32[]{:S(2)}) collective-permute-start(bf16[96,768]{1,0:T(8,128)(2,1)S(1)} %get-tuple-element.95), channel_id=1, source_target_pairs={{0,16},{2,18},{4,20},{6,22},{8,24},{10,26},{12,28},{14,30},{16,0},... | collective-permute-start | bytes 442376 | tf_op jit(solution)/shard_map/ppermute | solution.py:686
  138.2 8.7 %collective-permute-start.31 = (bf16[96,768]{1,0:T(8,128)(2,1)S(1)}, bf16[96,768]{1,0:T(8,128)(2,1)S(1)}, u32[]{:S(2)}, u32[]{:S(2)}) collective-permute-start(bf16[96,768]{1,0:T(8,128)(2,1)S(1)} %get-tuple-element.95), channel_id=1, source_target_pairs={{0,8},{2,10},{4,12},{6,14},{8,0},{10,2},{12,4},{14,6},{16,24},{18,... | collective-permute-start | bytes 442376 | tf_op jit(solution)/shard_map/ppermute | solution.py:686
  138.2 29.0 %copy-start.31 = (bf16[96,768]{1,0:T(8,128)(2,1)}, bf16[96,768]{1,0:T(8,128)(2,1)S(1)}, u32[]{:S(2)}) copy-start(bf16[96,768]{1,0:T(8,128)(2,1)S(1)} %collective-permute-done.39.refs_12_) | copy-start | bytes 442372
  138.2 12.2 %collective-permute-start.28 = (bf16[128,768]{1,0:T(8,128)(2,1)S(1)}, bf16[128,768]{1,0:T(8,128)(2,1)S(1)}, u32[]{:S(2)}, u32[]{:S(2)}) collective-permute-start(bf16[128,768]{1,0:T(8,128)(2,1)S(1)} %get-tuple-element.94.refs_0_), channel_id=1, source_target_pairs={{0,2},{2,0},{4,6},{6,4},{8,10},{10,8},{12,14},{14,12},{16,18},{18,... | collective-permute-start | bytes 589832 | tf_op jit(solution)/shard_map/ppermute | solution.py:686
  144.6 22.7 %copy-start.32 = (bf16[96,768]{1,0:T(8,128)(2,1)}, bf16[96,768]{1,0:T(8,128)(2,1)S(1)}, u32[]{:S(2)}) copy-start(bf16[96,768]{1,0:T(8,128)(2,1)S(1)} %collective-permute-done.35.refs_8_) | copy-start | bytes 442372
  144.6 6.7 %collective-permute-start.42 = (bf16[96,768]{1,0:T(8,128)(2,1)S(1)}, bf16[96,768]{1,0:T(8,128)(2,1)S(1)}, u32[]{:S(2)}, u32[]{:S(2)}) collective-permute-start(bf16[96,768]{1,0:T(8,128)(2,1)S(1)} %collective-permute-done.39.refs_12_), channel_id=1, source_target_pairs={{0,6},{2,4},{4,2},{6,0},{8,14},{10,12},{12,10},{14,8},{16,22},{18,... | collective-permute-start | bytes 442376 | tf_op jit(solution)/shard_map/ppermute | solution.py:686
  146.9 20.4 %copy-start.33 = (bf16[96,768]{1,0:T(8,128)(2,1)}, bf16[96,768]{1,0:T(8,128)(2,1)S(1)}, u32[]{:S(2)}) copy-start(bf16[96,768]{1,0:T(8,128)(2,1)S(1)} %collective-permute-done.31.refs_4_) | copy-start | bytes 442372
  146.9 8.4 %collective-permute-start.41 = (bf16[96,768]{1,0:T(8,128)(2,1)S(1)}, bf16[96,768]{1,0:T(8,128)(2,1)S(1)}, u32[]{:S(2)}, u32[]{:S(2)}) collective-permute-start(bf16[96,768]{1,0:T(8,128)(2,1)S(1)} %collective-permute-done.39.refs_12_), channel_id=1, source_target_pairs={{0,4},{2,6},{4,0},{6,2},{8,12},{10,14},{12,8},{14,10},{16,20},{18,... | collective-permute-start | bytes 442376 | tf_op jit(solution)/shard_map/ppermute | solution.py:686
  147.2 20.1 %copy-start.25 = (bf16[128,768]{1,0:T(8,128)(2,1)}, bf16[128,768]{1,0:T(8,128)(2,1)S(1)}, u32[]{:S(2)}) copy-start(bf16[128,768]{1,0:T(8,128)(2,1)S(1)} %collective-permute-done.30.refs_3_) | copy-start | bytes 589828
  147.2 11.7 %collective-permute-start.40 = (bf16[96,768]{1,0:T(8,128)(2,1)S(1)}, bf16[96,768]{1,0:T(8,128)(2,1)S(1)}, u32[]{:S(2)}, u32[]{:S(2)}) collective-permute-start(bf16[96,768]{1,0:T(8,128)(2,1)S(1)} %collective-permute-done.39.refs_12_), channel_id=1, source_target_pairs={{0,2},{2,0},{4,6},{6,4},{8,10},{10,8},{12,14},{14,12},{16,18},{18,... | collective-permute-start | bytes 442376 | tf_op jit(solution)/shard_map/ppermute | solution.py:686
  148.1 19.2 %copy-start.26 = (bf16[128,768]{1,0:T(8,128)(2,1)}, bf16[128,768]{1,0:T(8,128)(2,1)S(1)}, u32[]{:S(2)}) copy-start(bf16[128,768]{1,0:T(8,128)(2,1)S(1)} %collective-permute-done.29.refs_2_) | copy-start | bytes 589828
  148.1 10.8 %collective-permute-start.38 = (bf16[96,768]{1,0:T(8,128)(2,1)S(1)}, bf16[96,768]{1,0:T(8,128)(2,1)S(1)}, u32[]{:S(2)}, u32[]{:S(2)}) collective-permute-start(bf16[96,768]{1,0:T(8,128)(2,1)S(1)} %collective-permute-done.35.refs_8_), channel_id=1, source_target_pairs={{0,6},{2,4},{4,2},{6,0},{8,14},{10,12},{12,10},{14,8},{16,22},{18,... | collective-permute-start | bytes 442376 | tf_op jit(solution)/shard_map/ppermute | solution.py:686
  150.4 16.9 %copy-start.27 = (bf16[128,768]{1,0:T(8,128)(2,1)}, bf16[128,768]{1,0:T(8,128)(2,1)S(1)}, u32[]{:S(2)}) copy-start(bf16[128,768]{1,0:T(8,128)(2,1)S(1)} %collective-permute-done.28.refs_1_) | copy-start | bytes 589828
  150.4 12.0 %collective-permute-start.37 = (bf16[96,768]{1,0:T(8,128)(2,1)S(1)}, bf16[96,768]{1,0:T(8,128)(2,1)S(1)}, u32[]{:S(2)}, u32[]{:S(2)}) collective-permute-start(bf16[96,768]{1,0:T(8,128)(2,1)S(1)} %collective-permute-done.35.refs_8_), channel_id=1, source_target_pairs={{0,4},{2,6},{4,0},{6,2},{8,12},{10,14},{12,8},{14,10},{16,20},{18,... | collective-permute-start | bytes 442376 | tf_op jit(solution)/shard_map/ppermute | solution.py:686
  151.3 16.1 %copy-start.34 = (bf16[96,768]{1,0:T(8,128)(2,1)}, bf16[96,768]{1,0:T(8,128)(2,1)S(1)}, u32[]{:S(2)}) copy-start(bf16[96,768]{1,0:T(8,128)(2,1)S(1)} %collective-permute-done.42.refs_15_) | copy-start | bytes 442372
  151.3 11.2 %collective-permute-start.36 = (bf16[96,768]{1,0:T(8,128)(2,1)S(1)}, bf16[96,768]{1,0:T(8,128)(2,1)S(1)}, u32[]{:S(2)}, u32[]{:S(2)}) collective-permute-start(bf16[96,768]{1,0:T(8,128)(2,1)S(1)} %collective-permute-done.35.refs_8_), channel_id=1, source_target_pairs={{0,2},{2,0},{4,6},{6,4},{8,10},{10,8},{12,14},{14,12},{16,18},{18,... | collective-permute-start | bytes 442376 | tf_op jit(solution)/shard_map/ppermute | solution.py:686
  155.3 12.1 %copy-start.35 = (bf16[96,768]{1,0:T(8,128)(2,1)}, bf16[96,768]{1,0:T(8,128)(2,1)S(1)}, u32[]{:S(2)}) copy-start(bf16[96,768]{1,0:T(8,128)(2,1)S(1)} %collective-permute-done.41.refs_14_) | copy-start | bytes 442372
  155.3 9.4 %collective-permute-start.34 = (bf16[96,768]{1,0:T(8,128)(2,1)S(1)}, bf16[96,768]{1,0:T(8,128)(2,1)S(1)}, u32[]{:S(2)}, u32[]{:S(2)}) collective-permute-start(bf16[96,768]{1,0:T(8,128)(2,1)S(1)} %collective-permute-done.31.refs_4_), channel_id=1, source_target_pairs={{0,6},{2,4},{4,2},{6,0},{8,14},{10,12},{12,10},{14,8},{16,22},{18,... | collective-permute-start | bytes 442376 | tf_op jit(solution)/shard_map/ppermute | solution.py:686
  158.9 8.5 %copy-start.36 = (bf16[96,768]{1,0:T(8,128)(2,1)}, bf16[96,768]{1,0:T(8,128)(2,1)S(1)}, u32[]{:S(2)}) copy-start(bf16[96,768]{1,0:T(8,128)(2,1)S(1)} %collective-permute-done.40.refs_13_) | copy-start | bytes 442372
  158.9 7.7 %collective-permute-start.33 = (bf16[96,768]{1,0:T(8,128)(2,1)S(1)}, bf16[96,768]{1,0:T(8,128)(2,1)S(1)}, u32[]{:S(2)}, u32[]{:S(2)}) collective-permute-start(bf16[96,768]{1,0:T(8,128)(2,1)S(1)} %collective-permute-done.31.refs_4_), channel_id=1, source_target_pairs={{0,4},{2,6},{4,0},{6,2},{8,12},{10,14},{12,8},{14,10},{16,20},{18,... | collective-permute-start | bytes 442376 | tf_op jit(solution)/shard_map/ppermute | solution.py:686
  158.9 8.4 %copy-start.37 = (bf16[96,768]{1,0:T(8,128)(2,1)}, bf16[96,768]{1,0:T(8,128)(2,1)S(1)}, u32[]{:S(2)}) copy-start(bf16[96,768]{1,0:T(8,128)(2,1)S(1)} %collective-permute-done.38.refs_11_) | copy-start | bytes 442372
  158.9 8.4 %collective-permute-start.32 = (bf16[96,768]{1,0:T(8,128)(2,1)S(1)}, bf16[96,768]{1,0:T(8,128)(2,1)S(1)}, u32[]{:S(2)}, u32[]{:S(2)}) collective-permute-start(bf16[96,768]{1,0:T(8,128)(2,1)S(1)} %collective-permute-done.31.refs_4_), channel_id=1, source_target_pairs={{0,2},{2,0},{4,6},{6,4},{8,10},{10,8},{12,14},{14,12},{16,18},{18,... | collective-permute-start | bytes 442376 | tf_op jit(solution)/shard_map/ppermute | solution.py:686
  (26 other events, 57.0 us)

commit v3 on v2

--- a/solution.py
+++ b/solution.py
@@ -283,10 +283,9 @@
     active_came_ref,
     grad_pre_own_ref,
     grad_pre_came_ref,
-    in_held_ref,
-    out_held_ref,
-    arrived,
+    *more,
 ):
+    floor_refs, (in_held_ref, out_held_ref, arrived) = more[:-3], more[-3:]
     width, units = in_own_ref.shape
     copies = [
         pltpu.make_async_copy(source, target, arrived.at[at])
@@ -349,6 +348,7 @@
     grad_back_ref.send()
     back_ref[...] = (gate * produced).astype(LOW)
     grad_router_ref[...] = product(grad_logits, rows, 0, 0)
+    floor_rows(back_ref, floor_refs)
 
 
 def halves(own_rows):
@@ -465,6 +465,45 @@
         ref.send()
 
 
+def floor_rows(back_ref, outs):
+    rows = outs[0].shape[0]
+    for other, ref in enumerate(outs):
+        if len(outs) == 1:
+            ref[...] = back_ref[...]
+        else:
+            mine = lax.rem(lax.axis_index("expert") // PLANE, LINE)
+            at = pl.multiple_of((mine ^ other) * rows, 16)
+            ref[...] = back_ref.ref[pl.ds(at, rows), :]
+        ref.send()
+
+
+def member_rows_kernel(*refs):
+    floors, outs = refs[0:LINE], refs[LINE:]
+    mine = lax.rem(lax.axis_index("expert"), PLANE)
+    rows = outs[0].shape[0] // LINE
+    for other, out_ref in enumerate(outs):
+        at = pl.multiple_of((mine ^ other) * rows, 16)
+        for floor, ref in enumerate(floors):
+            ref.ready()
+            out_ref[floor * rows : (floor + 1) * rows, :] = ref[pl.ds(at, rows), :]
+        out_ref.send()
+
+
+def returned_rows_kernel(*refs):
+    parts, place_ref, hidden_ref, out_ref, done_ref, returned_ref = refs[0:PLANE], *refs[PLANE:]
+    member = lax.rem(lax.axis_index("expert"), PLANE)
+    floor = lax.rem(lax.axis_index("expert") // PLANE, LINE)
+    rows = parts[0].shape[0] // LINE
+    for across, ref in enumerate(parts):
+        for along in range(LINE):
+            at = pl.multiple_of(((floor ^ along) * PLANE + (member ^ across)) * rows, 16)
+            returned_ref[pl.ds(at, rows), :] = ref[along * rows : (along + 1) * rows, :]
+    out_ref[...] = (
+        hidden_ref[...] + product(place_ref[...], returned_ref[...], 0, 0)
+    ).astype(LOW)
+    done_ref[...] = jnp.zeros(done_ref.shape, FULL)
+
+
 def grad_tokens_kernel(
     tokens_ref,
     gain_ref,
@@ -473,7 +512,6 @@
     router_came_ref,
     ffn_ref,
     table_ref,
-    back_ref,
     grads_own_ref,
     value_own_ref,
     query_own_ref,
@@ -484,10 +522,7 @@
     grads_came_ref,
     grad_tokens_ref,
     small_ref,
-    back_out_ref,
 ):
-    back_out_ref[...] = back_ref[...]
-    back_out_ref.send()
     width, columns = value_own_ref.shape
     experts = router_own_ref.shape[0]
     heads, buckets = table_ref.shape
@@ -737,6 +772,7 @@
         (routes.reshape(1, own_rows), cotangent, tokens, own, ffn_gain, normed, swap(other)),
     )
     normed_near = around((normed_own,) * 3, 1)
+    floors = LINE if beyond == 1 else 1
     (
         back,
         grad_back,
@@ -747,6 +783,7 @@
         active_came,
         grad_pre_own,
         grad_pre_came,
+        *floor_back,
     ) = run(
         expert_kernel,
         [
@@ -756,7 +793,8 @@
             ((slots, width), LOW),
             ((slots, width), LOW),
         ]
-        + [((slots, in_own.shape[1]), LOW)] * 4,
+        + [((slots, in_own.shape[1]), LOW)] * 4
+        + [((slots // floors, width), LOW)] * floors,
         (exchange(sent), router_rows, in_own, out_own, in_came, out_came),
         scratch=(
             pltpu.VMEM((2, *in_own.shape), LOW),
@@ -816,12 +854,11 @@
     weights_came = tuple(swap(item) for item in weights)
     normed_far = tuple(swap(item) for item in normed_near)
     late_rows = -(-(heads + 1) // 8) * 8
-    grad_tokens, small, back = run(
+    grad_tokens, small = run(
         grad_tokens_kernel,
         [
             ((group_rows, width), FULL),
             ((small_rows + late_rows, width), LOW),
-            ((slots, width), LOW),
         ],
         (
             tokens,
@@ -831,14 +868,24 @@
             grad_router_came,
             grad_ffn,
             grad_table,
-            back,
             grads_low,
             *weights,
             *weights_came,
             grads_came,
         ),
     )
-    returned = exchange(back)
+    if beyond == 1:
+        floor_back = (floor_back[0],) + around(floor_back[1:], PLANE)
+    chunk_rows = 4 * part_rows // LINE
+    all_rows = chunk_rows + small_rows + late_rows
+    chunks = run(
+        sums_kernel,
+        [((all_rows, width), LOW)] * LINE,
+        parts + normed_near + normed_far + (normed, small),
+        scratch=(pltpu.VMEM((part_rows, width), FULL),) * 4,
+        after=tuple(floor_back[1:]),
+    )
+    chunks = (chunks[0],) + around(chunks[1:], PLANE)
     grad_expert_in, grad_expert_out, done = expert_grads(
         rows,
         rows_far,
@@ -849,18 +896,21 @@
         grad_pre_own,
         grad_pre_far,
     )
-    chunk_rows = 4 * part_rows // LINE
-    all_rows = chunk_rows + small_rows + late_rows
-    chunks = run(
-        sums_kernel,
-        [((all_rows, width), LOW)] * LINE,
-        parts + normed_near + normed_far + (normed, small),
-        scratch=(pltpu.VMEM((part_rows, width), FULL),) * 4,
-    )
-    (block_out,) = run(
-        block_out_kernel, [((own_rows, width), LOW)], (place, returned, hidden)
-    )
-    chunks = (chunks[0],) + around(chunks[1:], PLANE)
+    if beyond == 1:
+        back = run(
+            member_rows_kernel, [((slots // PLANE, width), LOW)] * PLANE, floor_back, after=(chunks[1],)
+        )
+        back = (back[0],) + around(back[1:], 1)
+        block_out, returned_done = run(
+            returned_rows_kernel,
+            [((own_rows, width), LOW), ((8, 128), FULL)],
+            tuple(back) + (place, hidden),
+            scratch=(pltpu.VMEM((slots, width), LOW),),
+        )
+    else:
+        (block_out,) = run(
+            block_out_kernel, [((own_rows, width), LOW)], (place, exchange(back), hidden)
+        )
     if beyond == 1:
         whole, chunk = run(
             line_sum_kernel,
@@ -874,8 +924,14 @@
         whole = beyond_sum(whole).astype(LOW)
         chunk = whole[0:chunk_rows]
     gathered = (whole,) + around((whole,) * 3, 1)
-    for item in around((chunk,) * 3, PLANE):
-        gathered += (item,) + around((item,) * 3, 1)
+    opposite = gathered[PLANE - 1]
+    for along, item in enumerate(around((chunk,) * 3, PLANE)):
+        near_two = around((item,) * 2, 1)
+        if along < 2:
+            third = hop(opposite, PLANE * (along + 1))
+        else:
+            third = hop(item, PLANE - 1)
+        gathered += (item,) + near_two + (third,)
     (
         grad_value,
         grad_query,

time: 174 us -> 172 us (0.989)
  starting transfers between devices: 57.3 us -> 55.1 us
  Pallas kernels: 55.7 us -> 57.8 us
  waiting for transfers between devices: 52.6 us -> 50.6 us
    all_to_all x3 -> x2, starting transfers between devices: 18.9 us -> 15 us  [exchange(): lax.all_to_all(parts, 'expert', split_axis=0, concat_axis=0, tiled=True)]
    ppermute x24 -> x30, waiting for transfers between devices: 39.8 us -> 37.7 us  [hop(): lax.ppermute(item, 'expert', [(at, at ^ distance) for at in range(sources)])]
    pallas_call x9 -> x10, Pallas kernels: 49 us -> 51 us  [run(): pl.pallas_call(body, out_shape=[jax.ShapeDtypeStruct(shape, dtype) for sh...]
    ppermute x24 -> x30, starting transfers between devices: 33.3 us -> 35 us  [hop(): lax.ppermute(item, 'expert', [(at, at ^ distance) for at in range(sources)])]
    all_to_all x3 -> x2, waiting for transfers between devices: 5.66 us -> 4.42 us  [exchange(): lax.all_to_all(parts, 'expert', split_axis=0, concat_axis=0, tiled=True)]
    unnamed x88 -> x116, local copies, waits for them, and re-layouts: 6.47 us -> 6.75 us
  transfers between devices with their start and end apart: 46 -> 51, of which waited for: 17 -> 19; matrix products, arithmetic and copies ran while one was open for 0% -> 0% of each run, Pallas kernels for 22% -> 21%
where the time goes in v3:
time: 172 us
  Pallas kernels  57.8 us (34%)
  starting transfers between devices  55.1 us (32%)
  waiting for transfers between devices  50.6 us (29%)
  local copies, waits for them, and re-layouts  6.75 us (4%)
    pallas_call x10, Pallas kernels, run(): pl.pallas_call(body, out_shape=[jax.ShapeDtypeStruct(shape, dtype) for sh...  51 us
    ppermute x30, waiting for transfers between devices, hop(): lax.ppermute(item, 'expert', [(at, at ^ distance) for at in range(sources)])  37.7 us
    ppermute x30, starting transfers between devices, hop(): lax.ppermute(item, 'expert', [(at, at ^ distance) for at in range(sources)])  35 us
    all_to_all x2, starting transfers between devices, exchange(): lax.all_to_all(parts, 'expert', split_axis=0, concat_axis=0, tiled=True)  15 us
    ppermute x19, waiting for transfers between devices, swap(): return lax.ppermute(item, 'shard', [(0, 1), (1, 0)])  8.54 us
    pallas_call x1, Pallas kernels, expert_grads(): pl.pallas_call(expert_grads_kernel, grid=(units // block,), out_shape=[ja...  6.87 us
    unnamed x116, local copies, waits for them, and re-layouts  6.75 us
    ppermute x19, starting transfers between devices, swap(): return lax.ppermute(item, 'shard', [(0, 1), (1, 0)])  5.05 us
  transfers between devices with their start and end apart: 51, of which 19 were waited for; matrix products, arithmetic and copies ran while one was open for 0% of the time, Pallas kernels for 21%

profile of v3, /device:TPU:0, one launch (start us, length us, event | category | flops | bytes accessed | tf_op | source)
XLA Modules:
  0.0 171.6 jit_solution(1334542024153545708)
XLA Ops:
  1.2 7.0 %shard_map.229 = (f32[128,768]{1,0:T(8,128)}, f32[128,768]{1,0:T(8,128)}, bf16[256,1152]{1,0:T(8,128)(2,1)}, bf16[6,256,256]{2,1,0:T(8,128)(2,1)}, bf16[256,768]{1,0:T(8,128)(2,1)}, /*index=5*/bf16[256,384]{1,0:T(8,128)(2,1)}) custom-call(s32[1,4]{1,0:T(1,128)} %refs_0_.2, bf16[256,768]{1,0:T(8,128)(2,1)} %refs_0_.3, f32[768]{0:T(1024)} %refs_1_.5, ...), custom_call_target="tpu_custom_call" | custom-call | tf_op jit(solution)/shard_map/pallas_call | solution.py:133
  8.7 1.6 collective-permute-done.refs_6_
  10.3 0.7 copy-done.26
  11.0 3.1 %shard_map.230 = (bf16[256,128]{1,0:T(8,128)(2,1)}, f32[128,768]{1,0:T(8,128)}, bf16[256,1536]{1,0:T(8,128)(2,1)}, bf16[128,768]{1,0:T(8,128)(2,1)}) custom-call(s32[1,128]{1,0:T(1,128)} %bitcast.24, bf16[128,768]{1,0:T(8,128)(2,1)} %refs_5_.3, bf16[256,768]{1,0:T(8,128)(2,1)} %refs_0_.3, f32[128,768]{1,0:T(8,128)} %get-tuple-element.66.refs_3_, ...), custom_call_target="tpu_custom_call" | custom-call | tf_op jit(solution)/shard_map/pallas_call | solution.py:133
  14.1 8.2 %all-to-all-start = ((bf16[16,16,1536]{2,1,0:T(8,128)(2,1)}), bf16[16,16,1536]{2,1,0:T(8,128)(2,1)S(1)}, u32[]{:S(2)}, u32[]{:S(2)}) async-start(bf16[16,16,1536]{2,1,0:T(8,128)(2,1)} %bitcast.20), calls=%async_computation | async-start | bytes 1572864 | tf_op jit(solution)/shard_map/all_to_all | solution.py:728
  22.4 2.8 %collective-permute-start.5 = (bf16[128,768]{1,0:T(8,128)(2,1)}, bf16[128,768]{1,0:T(8,128)(2,1)S(1)}, u32[]{:S(2)}, u32[]{:S(2)}) collective-permute-start(bf16[128,768]{1,0:T(8,128)(2,1)} %get-tuple-element.70), channel_id=1, source_target_pairs={{0,6},{2,4},{4,2},{6,0},{8,14},{10,12},{12,10},{14,8},{16,22},{18,... | collective-permute-start | bytes 589832 | tf_op jit(solution)/shard_map/ppermute | solution.py:721
  25.2 0.6 collective-permute-start.4
  25.9 12.3 %collective-permute-done.5.refs_8_.refs_6_ = bf16[128,768]{1,0:T(8,128)(2,1)S(1)} collective-permute-done((bf16[128,768]{1,0:T(8,128)(2,1)}, bf16[128,768]{1,0:T(8,128)(2,1)S(1)}, u32[]{:S(2)}, u32[]{:S(2)}) %collective-permute-start.5) | collective-permute-done | bytes 196640 | tf_op jit(solution)/shard_map/ppermute | solution.py:721
  38.3 3.6 %collective-permute-done.4.refs_7_.refs_5_ = bf16[128,768]{1,0:T(8,128)(2,1)S(1)} collective-permute-done((bf16[128,768]{1,0:T(8,128)(2,1)}, bf16[128,768]{1,0:T(8,128)(2,1)S(1)}, u32[]{:S(2)}, u32[]{:S(2)}) %collective-permute-start.4) | collective-permute-done | bytes 196640 | tf_op jit(solution)/shard_map/ppermute | solution.py:721
  41.9 0.6 collective-permute-done.3.refs_6_.refs_4_
  42.6 0.8 copy-done.5
  43.4 0.8 copy-done.8
  44.2 11.9 %shard_map.231 = (bf16[256,768]{1,0:T(8,128)(2,1)}, bf16[256,768]{1,0:T(8,128)(2,1)}, f32[16,768]{1,0:T(8,128)}, bf16[256,768]{1,0:T(8,128)(2,1)}, bf16[256,768]...) custom-call(bf16[256,1536]{1,0:T(8,128)(2,1)} %bitcast.13, ...), custom_call_target="tpu_custom_call" | custom-call | tf_op jit(solution)/shard_map/pallas_call | solution.py:133
  56.0 6.8 %all-to-all-start.1 = ((bf16[16,16,768]{2,1,0:T(8,128)(2,1)}), bf16[16,16,768]{2,1,0:T(8,128)(2,1)S(1)}, u32[]{:S(2)}, u32[]{:S(2)}) async-start(bf16[16,16,768]{2,1,0:T(8,128)(2,1)} %bitcast.21), calls=%async_computation.1 | async-start | bytes 786432 | tf_op jit(solution)/shard_map/all_to_all | solution.py:728
  64.0 2.0 %collective-permute-done.11.refs_6_ = bf16[128,768]{1,0:T(8,128)(2,1)S(1)} collective-permute-done((bf16[128,768]{1,0:T(8,128)(2,1)}, bf16[128,768]{1,0:T(8,128)(2,1)S(1)}, u32[]{:S(2)}, u32[]{:S(2)}) %collective-permute-start.11) | collective-permute-done | bytes 196640 | tf_op jit(solution)/shard_map/ppermute | solution.py:718
  66.1 1.9 %collective-permute-done.9.refs_1_ = bf16[256,128]{1,0:T(8,128)(2,1)S(1)} collective-permute-done((bf16[256,128]{1,0:T(8,128)(2,1)}, bf16[256,128]{1,0:T(8,128)(2,1)S(1)}, u32[]{:S(2)}, u32[]{:S(2)}) %collective-permute-start.9) | collective-permute-done | bytes 65568 | tf_op jit(solution)/shard_map/ppermute | solution.py:718
  68.0 0.6 copy-done.53
  69.2 1.5 collective-permute-done.17.refs_17_.refs_4_
  70.7 4.4 %all-to-all-done.1 = bf16[16,16,768]{2,1,0:T(8,128)(2,1)S(1)} async-done(((bf16[16,16,768]{2,1,0:T(8,128)(2,1)}), bf16[16,16,768]{2,1,0:T(8,128)(2,1)S(1)}, u32[]{:S(2)}, u32[]{:S(2)}) %all-to-all-start.1) | async-done | bytes 393248 | tf_op jit(solution)/shard_map/all_to_all | solution.py:728
  76.1 0.7 collective-permute-done.12.refs_8_
  77.6 9.5 %shard_map.232 = (bf16[256,768]{1,0:T(8,128)(2,1)}, f32[1,768]{1,0:T(1,128)}, bf16[256,1152]{1,0:T(8,128)(2,1)}, f32[6,32]{1,0:T(8,128)}, bf16[576,256]{1,0:T(8,...) custom-call(bf16[256,128]{1,0:T(8,128)(2,1)} %get-tuple-element.75.refs_0_.refs_4_, ...), custom_call_target="tpu_custom_call" | custom-call | tf_op jit(solution)/shard_map/pallas_call | solution.py:133
  88.3 0.6 collective-permute-start.18
  88.8 0.9 collective-permute-done.23.refs_9_
  89.7 0.9 collective-permute-start.19
  90.6 1.2 collective-permute-start.20
  91.8 1.1 collective-permute-start.6
  92.9 3.5 %collective-permute-done.6.refs_12_.refs_1_ = bf16[64,768]{1,0:T(8,128)(2,1)S(1)} collective-permute-done((bf16[64,768]{1,0:T(8,128)(2,1)S(1)}, bf16[64,768]{1,0:T(8,128)(2,1)S(1)}, u32[]{:S(2)}, u32[]{:S(2)}) %collective-permute-start.6) | collective-permute-done | bytes 98336 | tf_op jit(solution)/shard_map/ppermute | solution.py:721
  96.5 1.4 collective-permute-start.7
  97.8 2.1 %collective-permute-start.8 = (bf16[64,768]{1,0:T(8,128)(2,1)S(1)}, bf16[64,768]{1,0:T(8,128)(2,1)S(1)}, u32[]{:S(2)}, u32[]{:S(2)}) collective-permute-start(bf16[64,768]{1,0:T(8,128)(2,1)S(1)} %copy-done.54), channel_id=1, source_target_pairs={{0,24},{2,26},{4,28},{6,30},{8,16},{10,18},{12,20},{14,22},{16,8},... | collective-permute-start | bytes 294920 | tf_op jit(solution)/shard_map/ppermute | solution.py:721
  100.0 5.6 %shard_map.233 = (f32[256,768]{1,0:T(8,128)}, bf16[32,768]{1,0:T(8,128)(2,1)}) custom-call(bf16[256,768]{1,0:T(8,128)(2,1)} %refs_0_.3, f32[768]{0:T(1024)} %refs_1_.5, bf16[256,768]{1,0:T(8,128)(2,1)} %get-tuple-element.90.refs_2_, f32[16,768]{1,0:T(8,128)} %get-tuple-element.85.refs_3_, f32[16,768]{1,0:T(8,128)} %copy-done.30, ...), custom_call_target="tpu_custom_call" | custom-call | tf_op jit(solution)/shard_map/pallas_call | solution.py:133
  107.0 4.7 %shard_map.234 = (bf16[128,768]{1,0:T(8,128)(2,1)}, bf16[128,768]{1,0:T(8,128)(2,1)}, bf16[128,768]{1,0:T(8,128)(2,1)}, bf16[128,768]{1,0:T(8,128)(2,1)}) custom-call(bf16[576,256]{1,0:T(8,128)(2,1)} %get-tuple-element.86.refs_0_, bf16[576,256]{1,0:T(8,128)(2,1)} %copy-done.27, bf16[576,256]{1,0:T(8,128)(2,1)} %copy-done.28, bf16[576,256]{1,0:T(8,128)(2,1)} %copy-done.29, ...), custom_call_target="tpu_custom_call" | custom-call | tf_op jit(solution)/shard_map/pallas_call | solution.py:133
  111.7 1.7 collective-permute-start.28
  113.3 0.7 collective-permute-start.32
  114.0 2.1 %collective-permute-start.33 = (bf16[128,768]{1,0:T(8,128)(2,1)}, bf16[128,768]{1,0:T(8,128)(2,1)S(1)}, u32[]{:S(2)}, u32[]{:S(2)}) collective-permute-start(bf16[128,768]{1,0:T(8,128)(2,1)} %get-tuple-element.104), channel_id=1, source_target_pairs={{0,24},{2,26},{4,28},{6,30},{8,16},{10,18},{12,20},{14,22},{16,8},... | collective-permute-start | bytes 589832 | tf_op jit(solution)/shard_map/ppermute | solution.py:721
  116.1 4.0 %collective-permute-done.28.refs_4_.refs_1_ = bf16[128,768]{1,0:T(8,128)(2,1)S(1)} collective-permute-done((bf16[128,768]{1,0:T(8,128)(2,1)}, bf16[128,768]{1,0:T(8,128)(2,1)S(1)}, u32[]{:S(2)}, u32[]{:S(2)}) %collective-permute-start.28) | collective-permute-done | bytes 196640 | tf_op jit(solution)/shard_map/ppermute | solution.py:721
  120.2 0.7 copy-done
  120.8 1.9 %shard_map.235 = (bf16[64,768]{1,0:T(8,128)(2,1)}, bf16[64,768]{1,0:T(8,128)(2,1)}, bf16[64,768]{1,0:T(8,128)(2,1)}, bf16[64,768]{1,0:T(8,128)(2,1)}) custom-call(bf16[64,768]{1,0:T(8,128)(2,1)} %get-tuple-element.71.refs_0_, bf16[64,768]{1,0:T(8,128)(2,1)} %copy-done.21, bf16[64,768]{1,0:T(8,128)(2,1)} %copy-done.22, bf16[64,768]{1,0:T(8,128)(2,1)} %copy-done.23, ...), custom_call_target="tpu_custom_call" | custom-call | tf_op jit(solution)/shard_map/pallas_call | solution.py:133
  122.7 0.8 collective-permute-start.29
  123.6 1.4 collective-permute-start.30
  125.0 6.9 %shard_map.237 = (f32[768,1536]{1,0:T(8,128)}, f32[1536,768]{1,0:T(8,128)}, f32[8,128]{1,0:T(8,128)}) custom-call(bf16[256,768]{1,0:T(8,128)(2,1)} %get-tuple-element.81.rows_ref, bf16[256,768]{1,0:T(8,128)(2,1)} %copy-done.9, bf16[256,768]{1,0:T(8,128)(2,1)} %get-tuple-element.82.grad_produced_ref, bf16[256,768]{1,0:T(8,128)(2,1)} %copy-done.10, ...), custom_call_target="tpu_custom_call" | custom-call | tf_op jit(solution)/shard_map/pallas_call | solution.py:663
  131.9 1.4 collective-permute-start.31
  133.3 0.7 copy-done.4
  134.1 1.6 collective-permute-start.45
  135.7 2.0 %collective-permute-start.36 = (bf16[128,768]{1,0:T(8,128)(2,1)S(1)}, bf16[128,768]{1,0:T(8,128)(2,1)S(1)}, u32[]{:S(2)}, u32[]{:S(2)}) collective-permute-start(bf16[128,768]{1,0:T(8,128)(2,1)S(1)} %get-tuple-element.108.refs_0_), channel_id=1, source_target_pairs={{0,6},{2,4},{4,2},{6,0},{8,14},{10,12},{12,10},{14,8},{16,22},{18,... | collective-permute-start | bytes 589832 | tf_op jit(solution)/shard_map/ppermute | solution.py:721
  137.7 0.8 collective-permute-start.35
  138.5 1.3 collective-permute-start.41
  139.7 1.0 collective-permute-start.37
  140.8 1.9 %collective-permute-done.45.refs_12_ = bf16[96,768]{1,0:T(8,128)(2,1)S(1)} collective-permute-done((bf16[96,768]{1,0:T(8,128)(2,1)S(1)}, bf16[96,768]{1,0:T(8,128)(2,1)S(1)}, u32[]{:S(2)}, u32[]{:S(2)}) %collective-permute-start.45) | collective-permute-done | bytes 147488 | tf_op jit(solution)/shard_map/ppermute | solution.py:721
  142.7 0.8 collective-permute-start.34
  143.5 4.2 %collective-permute-done.41.refs_8_ = bf16[96,768]{1,0:T(8,128)(2,1)S(1)} collective-permute-done((bf16[96,768]{1,0:T(8,128)(2,1)S(1)}, bf16[96,768]{1,0:T(8,128)(2,1)S(1)}, u32[]{:S(2)}, u32[]{:S(2)}) %collective-permute-start.41) | collective-permute-done | bytes 147488 | tf_op jit(solution)/shard_map/ppermute | solution.py:721
  147.7 1.6 collective-permute-start.48
  149.3 0.6 collective-permute-start.47
  150.0 1.2 collective-permute-start.46
  151.2 0.8 collective-permute-start.43
  152.0 1.5 collective-permute-start.44
  153.4 1.2 collective-permute-done.48.refs_15_
  154.7 2.6 %collective-permute-done.47.refs_14_ = bf16[96,768]{1,0:T(8,128)(2,1)S(1)} collective-permute-done((bf16[96,768]{1,0:T(8,128)(2,1)S(1)}, bf16[96,768]{1,0:T(8,128)(2,1)S(1)}, u32[]{:S(2)}, u32[]{:S(2)}) %collective-permute-start.47) | collective-permute-done | bytes 147488 | tf_op jit(solution)/shard_map/ppermute | solution.py:721
  157.3 0.8 collective-permute-start.42
  158.1 1.3 collective-permute-start.39
  159.4 1.0 collective-permute-done.43.refs_10_
  160.4 0.8 collective-permute-start.38
  161.2 2.2 %shard_map.236 = (bf16[128,768]{1,0:T(8,128)(2,1)}, f32[8,128]{1,0:T(8,128)}) custom-call(bf16[64,768]{1,0:T(8,128)(2,1)} %get-tuple-element.96.refs_0_, bf16[64,768]{1,0:T(8,128)(2,1)} %copy-done.50, bf16[64,768]{1,0:T(8,128)(2,1)} %copy-done.51, bf16[64,768]{1,0:T(8,128)(2,1)} %copy-done.52, bf16[256,128]{1,0:T(8,128)(2,1)} %get-tuple-element.75.refs_0_.refs_4_, ...), custom_call_target="tpu_custom_call" | custom-call | tf_op jit(solution)/shard_map/pallas_call | solution.py:133
  163.5 2.0 %collective-permute-done.38.refs_5_ = bf16[96,768]{1,0:T(8,128)(2,1)S(1)} collective-permute-done((bf16[96,768]{1,0:T(8,128)(2,1)S(1)}, bf16[96,768]{1,0:T(8,128)(2,1)S(1)}, u32[]{:S(2)}, u32[]{:S(2)}) %collective-permute-start.38) | collective-permute-done | bytes 147488 | tf_op jit(solution)/shard_map/ppermute | solution.py:721
  166.3 5.1 %shard_map.239 = (f32[768,384]{1,0:T(8,128)}, f32[768,384]{1,0:T(8,128)}, f32[768,384]{1,0:T(8,128)}, f32[384,768]{1,0:T(8,128)}, f32[16,768]{1,0:T(8,128)}, /*i...) custom-call(bf16[128,768]{1,0:T(8,128)(2,1)} %copy-done.2, bf16[128,768]{1,0:T(8,128)(2,1)} %copy-done.34, ...), custom_call_target="tpu_custom_call" | custom-call | tf_op jit(solution)/shard_map/pallas_call | solution.py:133
  (165 shorter events, 8.4 us)
Async XLA Ops:
  0.6 41.9 %collective-permute-start.1 = (bf16[768,1536]{1,0:T(8,128)(2,1)}, bf16[768,1536]{1,0:T(8,128)(2,1)S(1)}, u32[]{:S(2)}, u32[]{:S(2)}) collective-permute-start(bf16[768,1536]{1,0:T(8,128)(2,1)} %bitcast.14), channel_id=1, source_target_pairs={{0,1},{1,0},{2,3},{3,2},{4,5},{5,4},{6,7},{7,6},{8,9},{9,8},{10,11... | collective-permute-start | bytes 7077896 | tf_op jit(solution)/shard_map/ppermute | solution.py:718
  1.2 41.4 %collective-permute-start.2 = (bf16[1536,768]{1,0:T(8,128)(2,1)}, bf16[1536,768]{1,0:T(8,128)(2,1)}, u32[]{:S(2)}, u32[]{:S(2)}) collective-permute-start(bf16[1536,768]{1,0:T(8,128)(2,1)} %bitcast.16), channel_id=1, source_target_pairs={{0,1},{1,0},{2,3},{3,2},{4,5},{5,4},{6,7},{7,6},{8,9},{9,8},{10,11... | collective-permute-start | bytes 7077896 | tf_op jit(solution)/shard_map/ppermute | solution.py:718
  8.2 2.1 %collective-permute-start = (f32[128,768]{1,0:T(8,128)}, f32[128,768]{1,0:T(8,128)S(1)}, u32[]{:S(2)}, u32[]{:S(2)}) collective-permute-start(f32[128,768]{1,0:T(8,128)} %get-tuple-element.68), channel_id=1, source_target_pairs={{0,1},{1,0},{2,3},{3,2},{4,5},{5,4},{6,7},{7,6},{8,9},{9,8},{10,11... | collective-permute-start | bytes 1179656 | tf_op jit(solution)/shard_map/ppermute | solution.py:718
  14.1 28.4 %all-to-all-start = ((bf16[16,16,1536]{2,1,0:T(8,128)(2,1)}), bf16[16,16,1536]{2,1,0:T(8,128)(2,1)S(1)}, u32[]{:S(2)}, u32[]{:S(2)}) async-start(bf16[16,16,1536]{2,1,0:T(8,128)(2,1)} %bitcast.20), calls=%async_computation | async-start | bytes 1572864 | tf_op jit(solution)/shard_map/all_to_all | solution.py:728
  22.4 15.9 %collective-permute-start.5 = (bf16[128,768]{1,0:T(8,128)(2,1)}, bf16[128,768]{1,0:T(8,128)(2,1)S(1)}, u32[]{:S(2)}, u32[]{:S(2)}) collective-permute-start(bf16[128,768]{1,0:T(8,128)(2,1)} %get-tuple-element.70), channel_id=1, source_target_pairs={{0,6},{2,4},{4,2},{6,0},{8,14},{10,12},{12,10},{14,8},{16,22},{18,... | collective-permute-start | bytes 589832 | tf_op jit(solution)/shard_map/ppermute | solution.py:721
  25.2 16.7 %collective-permute-start.4 = (bf16[128,768]{1,0:T(8,128)(2,1)}, bf16[128,768]{1,0:T(8,128)(2,1)S(1)}, u32[]{:S(2)}, u32[]{:S(2)}) collective-permute-start(bf16[128,768]{1,0:T(8,128)(2,1)} %get-tuple-element.70), channel_id=1, source_target_pairs={{0,4},{2,6},{4,0},{6,2},{8,12},{10,14},{12,8},{14,10},{16,20},{18,... | collective-permute-start | bytes 589832 | tf_op jit(solution)/shard_map/ppermute | solution.py:721
  25.8 16.7 %collective-permute-start.3 = (bf16[128,768]{1,0:T(8,128)(2,1)}, bf16[128,768]{1,0:T(8,128)(2,1)}, u32[]{:S(2)}, u32[]{:S(2)}) collective-permute-start(bf16[128,768]{1,0:T(8,128)(2,1)} %get-tuple-element.70), channel_id=1, source_target_pairs={{0,2},{2,0},{4,6},{6,4},{8,10},{10,8},{12,14},{14,12},{16,18},{18,... | collective-permute-start | bytes 589832 | tf_op jit(solution)/shard_map/ppermute | solution.py:721
  44.2 19.3 %copy-start.11 = (f32[128,768]{1,0:T(8,128)S(1)}, f32[128,768]{1,0:T(8,128)}, u32[]{:S(2)}) copy-start(f32[128,768]{1,0:T(8,128)} %get-tuple-element.76.refs_2_.refs_5_) | copy-start | bytes 1179652
  56.0 19.0 %all-to-all-start.1 = ((bf16[16,16,768]{2,1,0:T(8,128)(2,1)}), bf16[16,16,768]{2,1,0:T(8,128)(2,1)S(1)}, u32[]{:S(2)}, u32[]{:S(2)}) async-start(bf16[16,16,768]{2,1,0:T(8,128)(2,1)} %bitcast.21), calls=%async_computation.1 | async-start | bytes 786432 | tf_op jit(solution)/shard_map/all_to_all | solution.py:728
  62.9 12.9 %collective-permute-start.15 = (bf16[256,1536]{1,0:T(8,128)(2,1)}, bf16[256,1536]{1,0:T(8,128)(2,1)S(1)}, u32[]{:S(2)}, u32[]{:S(2)}) collective-permute-start(bf16[256,1536]{1,0:T(8,128)(2,1)} %get-tuple-element.83), channel_id=1, source_target_pairs={{0,1},{1,0},{2,3},{3,2},{4,5},{5,4},{6,7},{7,6},{8,9},{9,8},{10,11... | collective-permute-start | bytes 2359304 | tf_op jit(solution)/shard_map/ppermute | solution.py:718
  62.9 3.0 %collective-permute-start.11 = (bf16[128,768]{1,0:T(8,128)(2,1)}, bf16[128,768]{1,0:T(8,128)(2,1)S(1)}, u32[]{:S(2)}, u32[]{:S(2)}) collective-permute-start(bf16[128,768]{1,0:T(8,128)(2,1)} %refs_5_.3), channel_id=1, source_target_pairs={{0,1},{1,0},{2,3},{3,2},{4,5},{5,4},{6,7},{7,6},{8,9},{9,8},{10,11... | collective-permute-start | bytes 589832 | tf_op jit(solution)/shard_map/ppermute | solution.py:718
  63.4 5.4 %collective-permute-start.10 = (f32[128,768]{1,0:T(8,128)S(1)}, f32[128,768]{1,0:T(8,128)S(1)}, u32[]{:S(2)}, u32[]{:S(2)}) collective-permute-start(f32[128,768]{1,0:T(8,128)S(1)} %copy-done.11), channel_id=1, source_target_pairs={{0,1},{1,0},{2,3},{3,2},{4,5},{5,4},{6,7},{7,6},{8,9},{9,8},{10,11... | collective-permute-start | bytes 1179656 | tf_op jit(solution)/shard_map/ppermute | solution.py:718
  63.5 12.6 %collective-permute-start.16 = (bf16[256,1536]{1,0:T(8,128)(2,1)}, bf16[256,1536]{1,0:T(8,128)(2,1)S(1)}, u32[]{:S(2)}, u32[]{:S(2)}) collective-permute-start(bf16[256,1536]{1,0:T(8,128)(2,1)} %get-tuple-element.84), channel_id=1, source_target_pairs={{0,1},{1,0},{2,3},{3,2},{4,5},{5,4},{6,7},{7,6},{8,9},{9,8},{10,11... | collective-permute-start | bytes 2359304 | tf_op jit(solution)/shard_map/ppermute | solution.py:718
  63.9 11.2 %collective-permute-start.13 = (bf16[256,768]{1,0:T(8,128)(2,1)}, bf16[256,768]{1,0:T(8,128)(2,1)S(1)}, u32[]{:S(2)}, u32[]{:S(2)}) collective-permute-start(bf16[256,768]{1,0:T(8,128)(2,1)} %get-tuple-element.81.rows_ref), channel_id=1, source_target_pairs={{0,1},{1,0},{2,3},{3,2},{4,5},{5,4},{6,7},{7,6},{8,9},{9,8},{10,11... | collective-permute-start | bytes 1179656 | tf_op jit(solution)/shard_map/ppermute | solution.py:718
  66.0 2.1 %collective-permute-start.9 = (bf16[256,128]{1,0:T(8,128)(2,1)}, bf16[256,128]{1,0:T(8,128)(2,1)S(1)}, u32[]{:S(2)}, u32[]{:S(2)}) collective-permute-start(bf16[256,128]{1,0:T(8,128)(2,1)} %get-tuple-element.75.refs_0_.refs_4_), channel_id=1, source_target_pairs={{0,1},{1,0},{2,3},{3,2},{4,5},{5,4},{6,7},{7,6},{8,9},{9,8},{10,11... | collective-permute-start | bytes 196616 | tf_op jit(solution)/shard_map/ppermute | solution.py:718
  68.7 6.9 %collective-permute-start.14 = (bf16[256,768]{1,0:T(8,128)(2,1)}, bf16[256,768]{1,0:T(8,128)(2,1)S(1)}, u32[]{:S(2)}, u32[]{:S(2)}) collective-permute-start(bf16[256,768]{1,0:T(8,128)(2,1)} %get-tuple-element.82.grad_produced_ref), channel_id=1, source_target_pairs={{0,1},{1,0},{2,3},{3,2},{4,5},{5,4},{6,7},{7,6},{8,9},{9,8},{10,11... | collective-permute-start | bytes 1179656 | tf_op jit(solution)/shard_map/ppermute | solution.py:718
  68.8 1.9 %collective-permute-start.17 = (f32[16,768]{1,0:T(8,128)}, f32[16,768]{1,0:T(8,128)S(1)}, u32[]{:S(2)}, u32[]{:S(2)}) collective-permute-start(f32[16,768]{1,0:T(8,128)} %get-tuple-element.85.refs_3_), channel_id=1, source_target_pairs={{0,1},{1,0},{2,3},{3,2},{4,5},{5,4},{6,7},{7,6},{8,9},{9,8},{10,11... | collective-permute-start | bytes 147464 | tf_op jit(solution)/shard_map/ppermute | solution.py:718
  75.1 1.7 %collective-permute-start.12 = (bf16[256,768]{1,0:T(8,128)(2,1)S(1)}, bf16[256,768]{1,0:T(8,128)(2,1)S(1)}, u32[]{:S(2)}, u32[]{:S(2)}) collective-permute-start(bf16[256,768]{1,0:T(8,128)(2,1)S(1)} %bitcast.18), channel_id=1, source_target_pairs={{0,1},{1,0},{2,3},{3,2},{4,5},{5,4},{6,7},{7,6},{8,9},{9,8},{10,11... | collective-permute-start | bytes 1179656 | tf_op jit(solution)/shard_map/ppermute | solution.py:718
  75.1 12.6 %collective-permute-start.25 = (bf16[768,384]{1,0:T(8,128)(2,1)}, bf16[768,384]{1,0:T(8,128)(2,1)S(1)}, u32[]{:S(2)}, u32[]{:S(2)}) collective-permute-start(bf16[768,384]{1,0:T(8,128)(2,1)} %refs_9_.3), channel_id=1, source_target_pairs={{0,1},{1,0},{2,3},{3,2},{4,5},{5,4},{6,7},{7,6},{8,9},{9,8},{10,11... | collective-permute-start | bytes 1769480 | tf_op jit(solution)/shard_map/ppermute | solution.py:718
  75.6 12.3 %collective-permute-start.26 = (bf16[768,384]{1,0:T(8,128)(2,1)}, bf16[768,384]{1,0:T(8,128)(2,1)S(1)}, u32[]{:S(2)}, u32[]{:S(2)}) collective-permute-start(bf16[768,384]{1,0:T(8,128)(2,1)} %refs_10_.1), channel_id=1, source_target_pairs={{0,1},{1,0},{2,3},{3,2},{4,5},{5,4},{6,7},{7,6},{8,9},{9,8},{10,11... | collective-permute-start | bytes 1769480 | tf_op jit(solution)/shard_map/ppermute | solution.py:718
  75.7 12.6 %collective-permute-start.24 = (bf16[768,384]{1,0:T(8,128)(2,1)}, bf16[768,384]{1,0:T(8,128)(2,1)S(1)}, u32[]{:S(2)}, u32[]{:S(2)}) collective-permute-start(bf16[768,384]{1,0:T(8,128)(2,1)} %refs_8_.1), channel_id=1, source_target_pairs={{0,1},{1,0},{2,3},{3,2},{4,5},{5,4},{6,7},{7,6},{8,9},{9,8},{10,11... | collective-permute-start | bytes 1769480 | tf_op jit(solution)/shard_map/ppermute | solution.py:718
  77.6 18.9 %copy-start.55 = (bf16[64,768]{1,0:T(8,128)(2,1)S(1)}, bf16[64,768]{1,0:T(8,128)(2,1)}, u32[]{:S(2)}) copy-start(bf16[64,768]{1,0:T(8,128)(2,1)} %get-tuple-element.73) | copy-start | bytes 294916
  77.6 20.3 %copy-start.54 = (bf16[64,768]{1,0:T(8,128)(2,1)S(1)}, bf16[64,768]{1,0:T(8,128)(2,1)}, u32[]{:S(2)}) copy-start(bf16[64,768]{1,0:T(8,128)(2,1)} %get-tuple-element.74) | copy-start | bytes 294916
  87.1 10.7 %collective-permute-start.27 = (bf16[256,1152]{1,0:T(8,128)(2,1)}, bf16[256,1152]{1,0:T(8,128)(2,1)S(1)}, u32[]{:S(2)}, u32[]{:S(2)}) collective-permute-start(bf16[256,1152]{1,0:T(8,128)(2,1)} %get-tuple-element.93.refs_7_), channel_id=1, source_target_pairs={{0,1},{1,0},{2,3},{3,2},{4,5},{5,4},{6,7},{7,6},{8,9},{9,8},{10,11... | collective-permute-start | bytes 1769480 | tf_op jit(solution)/shard_map/ppermute | solution.py:718
  87.3 2.4 %collective-permute-start.23 = (bf16[128,768]{1,0:T(8,128)(2,1)S(1)}, bf16[128,768]{1,0:T(8,128)(2,1)S(1)}, u32[]{:S(2)}, u32[]{:S(2)}) collective-permute-start(bf16[128,768]{1,0:T(8,128)(2,1)S(1)} %copy-done.14), channel_id=1, source_target_pairs={{0,1},{1,0},{2,3},{3,2},{4,5},{5,4},{6,7},{7,6},{8,9},{9,8},{10,11... | collective-permute-start | bytes 589832 | tf_op jit(solution)/shard_map/ppermute | solution.py:718
  87.7 2.9 %collective-permute-start.22 = (bf16[128,768]{1,0:T(8,128)(2,1)S(1)}, bf16[128,768]{1,0:T(8,128)(2,1)S(1)}, u32[]{:S(2)}, u32[]{:S(2)}) collective-permute-start(bf16[128,768]{1,0:T(8,128)(2,1)S(1)} %copy-done.16), channel_id=1, source_target_pairs={{0,1},{1,0},{2,3},{3,2},{4,5},{5,4},{6,7},{7,6},{8,9},{9,8},{10,11... | collective-permute-start | bytes 589832 | tf_op jit(solution)/shard_map/ppermute | solution.py:718
  87.9 3.9 %collective-permute-start.21 = (bf16[128,768]{1,0:T(8,128)(2,1)}, bf16[128,768]{1,0:T(8,128)(2,1)S(1)}, u32[]{:S(2)}, u32[]{:S(2)}) collective-permute-start(bf16[128,768]{1,0:T(8,128)(2,1)} %collective-permute-done.3.refs_6_.refs_4_), channel_id=1, source_target_pairs={{0,1},{1,0},{2,3},{3,2},{4,5},{5,4},{6,7},{7,6},{8,9},{9,8},{10,11... | collective-permute-start | bytes 589832 | tf_op jit(solution)/shard_map/ppermute | solution.py:718
  88.3 17.8 %collective-permute-start.18 = (bf16[576,256]{1,0:T(8,128)(2,1)}, bf16[576,256]{1,0:T(8,128)(2,1)S(1)}, u32[]{:S(2)}, u32[]{:S(2)}) collective-permute-start(bf16[576,256]{1,0:T(8,128)(2,1)} %get-tuple-element.87), channel_id=1, source_target_pairs={{0,2},{2,0},{4,6},{6,4},{8,10},{10,8},{12,14},{14,12},{16,18},{18,... | collective-permute-start | bytes 884744 | tf_op jit(solution)/shard_map/ppermute | solution.py:721
  89.7 16.4 %copy-start.35 = (bf16[128,768]{1,0:T(8,128)(2,1)}, bf16[128,768]{1,0:T(8,128)(2,1)S(1)}, u32[]{:S(2)}) copy-start(bf16[128,768]{1,0:T(8,128)(2,1)S(1)} %collective-permute-done.23.refs_9_) | copy-start | bytes 589828
  89.7 16.3 %collective-permute-start.19 = (bf16[576,256]{1,0:T(8,128)(2,1)}, bf16[576,256]{1,0:T(8,128)(2,1)S(1)}, u32[]{:S(2)}, u32[]{:S(2)}) collective-permute-start(bf16[576,256]{1,0:T(8,128)(2,1)} %get-tuple-element.88), channel_id=1, source_target_pairs={{0,4},{2,6},{4,0},{6,2},{8,12},{10,14},{12,8},{14,10},{16,20},{18,... | collective-permute-start | bytes 884744 | tf_op jit(solution)/shard_map/ppermute | solution.py:721
  90.6 15.5 %copy-start.36 = (bf16[128,768]{1,0:T(8,128)(2,1)}, bf16[128,768]{1,0:T(8,128)(2,1)S(1)}, u32[]{:S(2)}) copy-start(bf16[128,768]{1,0:T(8,128)(2,1)S(1)} %collective-permute-done.22.refs_8_) | copy-start | bytes 589828
  90.6 15.5 %collective-permute-start.20 = (bf16[576,256]{1,0:T(8,128)(2,1)}, bf16[576,256]{1,0:T(8,128)(2,1)S(1)}, u32[]{:S(2)}, u32[]{:S(2)}) collective-permute-start(bf16[576,256]{1,0:T(8,128)(2,1)} %get-tuple-element.89), channel_id=1, source_target_pairs={{0,6},{2,4},{4,2},{6,0},{8,14},{10,12},{12,10},{14,8},{16,22},{18,... | collective-permute-start | bytes 884744 | tf_op jit(solution)/shard_map/ppermute | solution.py:721
  91.8 4.7 %collective-permute-start.6 = (bf16[64,768]{1,0:T(8,128)(2,1)S(1)}, bf16[64,768]{1,0:T(8,128)(2,1)S(1)}, u32[]{:S(2)}, u32[]{:S(2)}) collective-permute-start(bf16[64,768]{1,0:T(8,128)(2,1)S(1)} %copy-done.56), channel_id=1, source_target_pairs={{0,8},{2,10},{4,12},{6,14},{8,0},{10,2},{12,4},{14,6},{16,24},{18,... | collective-permute-start | bytes 294920 | tf_op jit(solution)/shard_map/ppermute | solution.py:721
  96.5 9.6 %collective-permute-start.7 = (bf16[64,768]{1,0:T(8,128)(2,1)S(1)}, bf16[64,768]{1,0:T(8,128)(2,1)S(1)}, u32[]{:S(2)}, u32[]{:S(2)}) collective-permute-start(bf16[64,768]{1,0:T(8,128)(2,1)S(1)} %copy-done.55), channel_id=1, source_target_pairs={{0,16},{2,18},{4,20},{6,22},{8,24},{10,26},{12,28},{14,30},{16,0},... | collective-permute-start | bytes 294920 | tf_op jit(solution)/shard_map/ppermute | solution.py:721
  97.8 8.2 %collective-permute-start.8 = (bf16[64,768]{1,0:T(8,128)(2,1)S(1)}, bf16[64,768]{1,0:T(8,128)(2,1)S(1)}, u32[]{:S(2)}, u32[]{:S(2)}) collective-permute-start(bf16[64,768]{1,0:T(8,128)(2,1)S(1)} %copy-done.54), channel_id=1, source_target_pairs={{0,24},{2,26},{4,28},{6,30},{8,16},{10,18},{12,20},{14,22},{16,8},... | collective-permute-start | bytes 294920 | tf_op jit(solution)/shard_map/ppermute | solution.py:721
  111.7 8.5 %collective-permute-start.28 = (bf16[128,768]{1,0:T(8,128)(2,1)}, bf16[128,768]{1,0:T(8,128)(2,1)S(1)}, u32[]{:S(2)}, u32[]{:S(2)}) collective-permute-start(bf16[128,768]{1,0:T(8,128)(2,1)} %get-tuple-element.95), channel_id=1, source_target_pairs={{0,8},{2,10},{4,12},{6,14},{8,0},{10,2},{12,4},{14,6},{16,24},{18,... | collective-permute-start | bytes 589832 | tf_op jit(solution)/shard_map/ppermute | solution.py:721
  113.3 19.9 %collective-permute-start.32 = (bf16[128,768]{1,0:T(8,128)(2,1)}, bf16[128,768]{1,0:T(8,128)(2,1)S(1)}, u32[]{:S(2)}, u32[]{:S(2)}) collective-permute-start(bf16[128,768]{1,0:T(8,128)(2,1)} %get-tuple-element.103), channel_id=1, source_target_pairs={{0,16},{2,18},{4,20},{6,22},{8,24},{10,26},{12,28},{14,30},{16,0},... | collective-permute-start | bytes 589832 | tf_op jit(solution)/shard_map/ppermute | solution.py:721
  114.0 19.2 %collective-permute-start.33 = (bf16[128,768]{1,0:T(8,128)(2,1)}, bf16[128,768]{1,0:T(8,128)(2,1)S(1)}, u32[]{:S(2)}, u32[]{:S(2)}) collective-permute-start(bf16[128,768]{1,0:T(8,128)(2,1)} %get-tuple-element.104), channel_id=1, source_target_pairs={{0,24},{2,26},{4,28},{6,30},{8,16},{10,18},{12,20},{14,22},{16,8},... | collective-permute-start | bytes 589832 | tf_op jit(solution)/shard_map/ppermute | solution.py:721
  122.7 14.9 %collective-permute-start.29 = (bf16[64,768]{1,0:T(8,128)(2,1)}, bf16[64,768]{1,0:T(8,128)(2,1)S(1)}, u32[]{:S(2)}, u32[]{:S(2)}) collective-permute-start(bf16[64,768]{1,0:T(8,128)(2,1)} %get-tuple-element.97), channel_id=1, source_target_pairs={{0,2},{2,0},{4,6},{6,4},{8,10},{10,8},{12,14},{14,12},{16,18},{18,... | collective-permute-start | bytes 294920 | tf_op jit(solution)/shard_map/ppermute | solution.py:721
  123.6 14.9 %collective-permute-start.30 = (bf16[64,768]{1,0:T(8,128)(2,1)}, bf16[64,768]{1,0:T(8,128)(2,1)S(1)}, u32[]{:S(2)}, u32[]{:S(2)}) collective-permute-start(bf16[64,768]{1,0:T(8,128)(2,1)} %get-tuple-element.98), channel_id=1, source_target_pairs={{0,4},{2,6},{4,0},{6,2},{8,12},{10,14},{12,8},{14,10},{16,20},{18,... | collective-permute-start | bytes 294920 | tf_op jit(solution)/shard_map/ppermute | solution.py:721
  131.9 7.9 %collective-permute-start.31 = (bf16[64,768]{1,0:T(8,128)(2,1)S(1)}, bf16[64,768]{1,0:T(8,128)(2,1)S(1)}, u32[]{:S(2)}, u32[]{:S(2)}) collective-permute-start(bf16[64,768]{1,0:T(8,128)(2,1)S(1)} %copy-done.57), channel_id=1, source_target_pairs={{0,6},{2,4},{4,2},{6,0},{8,14},{10,12},{12,10},{14,8},{16,22},{18,... | collective-permute-start | bytes 294920 | tf_op jit(solution)/shard_map/ppermute | solution.py:721
  134.0 31.5 %copy-start.2 = (bf16[128,768]{1,0:T(8,128)(2,1)}, bf16[128,768]{1,0:T(8,128)(2,1)S(1)}, u32[]{:S(2)}) copy-start(bf16[128,768]{1,0:T(8,128)(2,1)S(1)} %get-tuple-element.108.refs_0_) | copy-start | bytes 589828
  134.1 8.6 %collective-permute-start.45 = (bf16[96,768]{1,0:T(8,128)(2,1)S(1)}, bf16[96,768]{1,0:T(8,128)(2,1)S(1)}, u32[]{:S(2)}, u32[]{:S(2)}) collective-permute-start(bf16[96,768]{1,0:T(8,128)(2,1)S(1)} %get-tuple-element.109), channel_id=1, source_target_pairs={{0,24},{2,26},{4,28},{6,30},{8,16},{10,18},{12,20},{14,22},{16,8},... | collective-permute-start | bytes 442376 | tf_op jit(solution)/shard_map/ppermute | solution.py:721
  135.7 14.3 %collective-permute-start.36 = (bf16[128,768]{1,0:T(8,128)(2,1)S(1)}, bf16[128,768]{1,0:T(8,128)(2,1)S(1)}, u32[]{:S(2)}, u32[]{:S(2)}) collective-permute-start(bf16[128,768]{1,0:T(8,128)(2,1)S(1)} %get-tuple-element.108.refs_0_), channel_id=1, source_target_pairs={{0,6},{2,4},{4,2},{6,0},{8,14},{10,12},{12,10},{14,8},{16,22},{18,... | collective-permute-start | bytes 589832 | tf_op jit(solution)/shard_map/ppermute | solution.py:721
  137.7 23.6 %copy-start.50 = (bf16[64,768]{1,0:T(8,128)(2,1)}, bf16[64,768]{1,0:T(8,128)(2,1)S(1)}, u32[]{:S(2)}) copy-start(bf16[64,768]{1,0:T(8,128)(2,1)S(1)} %collective-permute-done.29.refs_1_) | copy-start | bytes 294916
  137.7 13.5 %collective-permute-start.35 = (bf16[128,768]{1,0:T(8,128)(2,1)S(1)}, bf16[128,768]{1,0:T(8,128)(2,1)S(1)}, u32[]{:S(2)}, u32[]{:S(2)}) collective-permute-start(bf16[128,768]{1,0:T(8,128)(2,1)S(1)} %get-tuple-element.108.refs_0_), channel_id=1, source_target_pairs={{0,4},{2,6},{4,0},{6,2},{8,12},{10,14},{12,8},{14,10},{16,20},{18,... | collective-permute-start | bytes 589832 | tf_op jit(solution)/shard_map/ppermute | solution.py:721
  138.5 22.8 %copy-start.51 = (bf16[64,768]{1,0:T(8,128)(2,1)}, bf16[64,768]{1,0:T(8,128)(2,1)S(1)}, u32[]{:S(2)}) copy-start(bf16[64,768]{1,0:T(8,128)(2,1)S(1)} %collective-permute-done.30.refs_2_) | copy-start | bytes 294916
  138.5 9.2 %collective-permute-start.41 = (bf16[96,768]{1,0:T(8,128)(2,1)S(1)}, bf16[96,768]{1,0:T(8,128)(2,1)S(1)}, u32[]{:S(2)}, u32[]{:S(2)}) collective-permute-start(bf16[96,768]{1,0:T(8,128)(2,1)S(1)} %get-tuple-element.109), channel_id=1, source_target_pairs={{0,16},{2,18},{4,20},{6,22},{8,24},{10,26},{12,28},{14,30},{16,0},... | collective-permute-start | bytes 442376 | tf_op jit(solution)/shard_map/ppermute | solution.py:721
  139.7 21.5 %copy-start.52 = (bf16[64,768]{1,0:T(8,128)(2,1)}, bf16[64,768]{1,0:T(8,128)(2,1)S(1)}, u32[]{:S(2)}) copy-start(bf16[64,768]{1,0:T(8,128)(2,1)S(1)} %collective-permute-done.31.refs_3_) | copy-start | bytes 294916
  139.7 9.6 %collective-permute-start.37 = (bf16[96,768]{1,0:T(8,128)(2,1)S(1)}, bf16[96,768]{1,0:T(8,128)(2,1)S(1)}, u32[]{:S(2)}, u32[]{:S(2)}) collective-permute-start(bf16[96,768]{1,0:T(8,128)(2,1)S(1)} %get-tuple-element.109), channel_id=1, source_target_pairs={{0,8},{2,10},{4,12},{6,14},{8,0},{10,2},{12,4},{14,6},{16,24},{18,... | collective-permute-start | bytes 442376 | tf_op jit(solution)/shard_map/ppermute | solution.py:721
  142.7 22.9 %copy-start.40 = (bf16[96,768]{1,0:T(8,128)(2,1)}, bf16[96,768]{1,0:T(8,128)(2,1)S(1)}, u32[]{:S(2)}) copy-start(bf16[96,768]{1,0:T(8,128)(2,1)S(1)} %collective-permute-done.45.refs_12_) | copy-start | bytes 442372
  142.7 9.3 %collective-permute-start.34 = (bf16[128,768]{1,0:T(8,128)(2,1)S(1)}, bf16[128,768]{1,0:T(8,128)(2,1)S(1)}, u32[]{:S(2)}, u32[]{:S(2)}) collective-permute-start(bf16[128,768]{1,0:T(8,128)(2,1)S(1)} %get-tuple-element.108.refs_0_), channel_id=1, source_target_pairs={{0,2},{2,0},{4,6},{6,4},{8,10},{10,8},{12,14},{14,12},{16,18},{18,... | collective-permute-start | bytes 589832 | tf_op jit(solution)/shard_map/ppermute | solution.py:721
  147.7 17.9 %copy-start.41 = (bf16[96,768]{1,0:T(8,128)(2,1)}, bf16[96,768]{1,0:T(8,128)(2,1)S(1)}, u32[]{:S(2)}) copy-start(bf16[96,768]{1,0:T(8,128)(2,1)S(1)} %collective-permute-done.41.refs_8_) | copy-start | bytes 442372
  147.7 7.0 %collective-permute-start.48 = (bf16[96,768]{1,0:T(8,128)(2,1)S(1)}, bf16[96,768]{1,0:T(8,128)(2,1)S(1)}, u32[]{:S(2)}, u32[]{:S(2)}) collective-permute-start(bf16[96,768]{1,0:T(8,128)(2,1)S(1)} %collective-permute-done.45.refs_12_), channel_id=1, source_target_pairs={{0,6},{2,4},{4,2},{6,0},{8,14},{10,12},{12,10},{14,8},{16,22},{18,... | collective-permute-start | bytes 442376 | tf_op jit(solution)/shard_map/ppermute | solution.py:721
  149.3 16.3 %copy-start.42 = (bf16[96,768]{1,0:T(8,128)(2,1)}, bf16[96,768]{1,0:T(8,128)(2,1)S(1)}, u32[]{:S(2)}) copy-start(bf16[96,768]{1,0:T(8,128)(2,1)S(1)} %collective-permute-done.37.refs_4_) | copy-start | bytes 442372
  149.3 8.0 %collective-permute-start.47 = (bf16[96,768]{1,0:T(8,128)(2,1)S(1)}, bf16[96,768]{1,0:T(8,128)(2,1)S(1)}, u32[]{:S(2)}, u32[]{:S(2)}) collective-permute-start(bf16[96,768]{1,0:T(8,128)(2,1)S(1)} %collective-permute-done.45.refs_12_), channel_id=1, source_target_pairs={{0,4},{2,6},{4,0},{6,2},{8,12},{10,14},{12,8},{14,10},{16,20},{18,... | collective-permute-start | bytes 442376 | tf_op jit(solution)/shard_map/ppermute | solution.py:721
  150.0 15.6 %copy-start.32 = (bf16[128,768]{1,0:T(8,128)(2,1)}, bf16[128,768]{1,0:T(8,128)(2,1)S(1)}, u32[]{:S(2)}) copy-start(bf16[128,768]{1,0:T(8,128)(2,1)S(1)} %collective-permute-done.36.refs_3_) | copy-start | bytes 589828
  150.0 8.1 %collective-permute-start.46 = (bf16[96,768]{1,0:T(8,128)(2,1)S(1)}, bf16[96,768]{1,0:T(8,128)(2,1)S(1)}, u32[]{:S(2)}, u32[]{:S(2)}) collective-permute-start(bf16[96,768]{1,0:T(8,128)(2,1)S(1)} %collective-permute-done.45.refs_12_), channel_id=1, source_target_pairs={{0,2},{2,0},{4,6},{6,4},{8,10},{10,8},{12,14},{14,12},{16,18},{18,... | collective-permute-start | bytes 442376 | tf_op jit(solution)/shard_map/ppermute | solution.py:721
  151.2 9.2 %collective-permute-start.43 = (bf16[96,768]{1,0:T(8,128)(2,1)S(1)}, bf16[96,768]{1,0:T(8,128)(2,1)S(1)}, u32[]{:S(2)}, u32[]{:S(2)}) collective-permute-start(bf16[96,768]{1,0:T(8,128)(2,1)S(1)} %collective-permute-done.41.refs_8_), channel_id=1, source_target_pairs={{0,4},{2,6},{4,0},{6,2},{8,12},{10,14},{12,8},{14,10},{16,20},{18,... | collective-permute-start | bytes 442376 | tf_op jit(solution)/shard_map/ppermute | solution.py:721
  152.0 13.5 %collective-permute-start.44 = (bf16[128,768]{1,0:T(8,128)(2,1)S(1)}, bf16[128,768]{1,0:T(8,128)(2,1)S(1)}, u32[]{:S(2)}, u32[]{:S(2)}) collective-permute-start(bf16[128,768]{1,0:T(8,128)(2,1)S(1)} %collective-permute-done.36.refs_3_), channel_id=1, source_target_pairs={{0,16},{2,18},{4,20},{6,22},{8,24},{10,26},{12,28},{14,30},{16,0},... | collective-permute-start | bytes 589832 | tf_op jit(solution)/shard_map/ppermute | solution.py:721
  154.7 10.9 %collective-permute-start.40 = (bf16[128,768]{1,0:T(8,128)(2,1)S(1)}, bf16[128,768]{1,0:T(8,128)(2,1)S(1)}, u32[]{:S(2)}, u32[]{:S(2)}) collective-permute-start(bf16[128,768]{1,0:T(8,128)(2,1)S(1)} %collective-permute-done.36.refs_3_), channel_id=1, source_target_pairs={{0,8},{2,10},{4,12},{6,14},{8,0},{10,2},{12,4},{14,6},{16,24},{18,... | collective-permute-start | bytes 589832 | tf_op jit(solution)/shard_map/ppermute | solution.py:721
  157.3 6.2 %collective-permute-start.42 = (bf16[96,768]{1,0:T(8,128)(2,1)S(1)}, bf16[96,768]{1,0:T(8,128)(2,1)S(1)}, u32[]{:S(2)}, u32[]{:S(2)}) collective-permute-start(bf16[96,768]{1,0:T(8,128)(2,1)S(1)} %collective-permute-done.41.refs_8_), channel_id=1, source_target_pairs={{0,2},{2,0},{4,6},{6,4},{8,10},{10,8},{12,14},{14,12},{16,18},{18,... | collective-permute-start | bytes 442376 | tf_op jit(solution)/shard_map/ppermute | solution.py:721
  158.1 5.4 %collective-permute-start.39 = (bf16[96,768]{1,0:T(8,128)(2,1)S(1)}, bf16[96,768]{1,0:T(8,128)(2,1)S(1)}, u32[]{:S(2)}, u32[]{:S(2)}) collective-permute-start(bf16[96,768]{1,0:T(8,128)(2,1)S(1)} %collective-permute-done.37.refs_4_), channel_id=1, source_target_pairs={{0,4},{2,6},{4,0},{6,2},{8,12},{10,14},{12,8},{14,10},{16,20},{18,... | collective-permute-start | bytes 442376 | tf_op jit(solution)/shard_map/ppermute | solution.py:721
  160.4 5.1 %collective-permute-start.38 = (bf16[96,768]{1,0:T(8,128)(2,1)S(1)}, bf16[96,768]{1,0:T(8,128)(2,1)S(1)}, u32[]{:S(2)}, u32[]{:S(2)}) collective-permute-start(bf16[96,768]{1,0:T(8,128)(2,1)S(1)} %collective-permute-done.37.refs_4_), channel_id=1, source_target_pairs={{0,2},{2,0},{4,6},{6,4},{8,10},{10,8},{12,14},{14,12},{16,18},{18,... | collective-permute-start | bytes 442376 | tf_op jit(solution)/shard_map/ppermute | solution.py:721
  (45 other events, 224.2 us)

commit v4 on v3

--- a/solution.py
+++ b/solution.py
@@ -89,7 +89,7 @@
             self.started = True
 
 
-def run(kernel, outs, operands, scratch=(), scalars=0, raw=(), after=(), near=False):
+def run(kernel, outs, operands, scratch=(), scalars=0, raw=(), after=(), near=False, grant=56):
     count, results = len(operands), len(outs)
     brought = [] if near else [at for at in range(scalars, count) if at not in raw]
 
@@ -136,7 +136,7 @@
         in_specs=in_specs,
         out_specs=[placed] * results,
         scratch_shapes=scratch_shapes,
-        compiler_params=pltpu.CompilerParams(vmem_limit_bytes=(4 if near else 56) * MEGABYTE),
+        compiler_params=pltpu.CompilerParams(vmem_limit_bytes=(4 if near else grant) * MEGABYTE),
         cost_estimate=pl.CostEstimate(flops=0, bytes_accessed=0, transcendentals=0),
     )(*operands, *after)
 
@@ -883,6 +883,7 @@
         [((all_rows, width), LOW)] * LINE,
         parts + normed_near + normed_far + (normed, small),
         scratch=(pltpu.VMEM((part_rows, width), FULL),) * 4,
+        grant=24,
         after=tuple(floor_back[1:]),
     )
     chunks = (chunks[0],) + around(chunks[1:], PLANE)

time: 172 us -> 171 us (level)
    unnamed x116 -> x106, local copies, waits for them, and re-layouts: 6.75 us -> 6.18 us
  transfers between devices with their start and end apart: 51 -> 51, of which waited for: 19 -> 18; matrix products, arithmetic and copies ran while one was open for 0% -> 0% of each run, Pallas kernels for 21% -> 21%
where the time goes in v4:
time: 171 us; the launch traced here: 170 us
  Pallas kernels  58.5 us (34%)
  starting transfers between devices  55.3 us (32%)
  waiting for transfers between devices  49.2 us (29%)
  local copies, waits for them, and re-layouts  6.18 us (4%)
    pallas_call x10, Pallas kernels, run(): pl.pallas_call(body, out_shape=[jax.ShapeDtypeStruct(shape, dtype) for sh...  51.6 us
    ppermute x30, waiting for transfers between devices, hop(): lax.ppermute(item, 'expert', [(at, at ^ distance) for at in range(sources)])  36.6 us
    ppermute x30, starting transfers between devices, hop(): lax.ppermute(item, 'expert', [(at, at ^ distance) for at in range(sources)])  34.8 us
    all_to_all x2, starting transfers between devices, exchange(): lax.all_to_all(parts, 'expert', split_axis=0, concat_axis=0, tiled=True)  15.1 us
    ppermute x19, waiting for transfers between devices, swap(): return lax.ppermute(item, 'shard', [(0, 1), (1, 0)])  7.54 us
    pallas_call x1, Pallas kernels, expert_grads(): pl.pallas_call(expert_grads_kernel, grid=(units // block,), out_shape=[ja...  6.88 us
    unnamed x106, local copies, waits for them, and re-layouts  6.18 us
    ppermute x19, starting transfers between devices, swap(): return lax.ppermute(item, 'shard', [(0, 1), (1, 0)])  5.36 us
  transfers between devices with their start and end apart: 51, of which 18 were waited for; matrix products, arithmetic and copies ran while one was open for 0% of the time, Pallas kernels for 21%

profile of v4, /device:TPU:0, one launch (start us, length us, event | category | flops | bytes accessed | tf_op | source)
XLA Modules:
  0.0 170.4 jit_solution(16019565748918144206)
XLA Ops:
  0.6 0.5 collective-permute-start.1
  1.2 7.0 %shard_map.229 = (f32[128,768]{1,0:T(8,128)}, f32[128,768]{1,0:T(8,128)}, bf16[256,1152]{1,0:T(8,128)(2,1)}, bf16[6,256,256]{2,1,0:T(8,128)(2,1)}, bf16[256,768]{1,0:T(8,128)(2,1)}, /*index=5*/bf16[256,384]{1,0:T(8,128)(2,1)}) custom-call(s32[1,4]{1,0:T(1,128)} %refs_0_.2, bf16[256,768]{1,0:T(8,128)(2,1)} %refs_0_.3, f32[768]{0:T(1024)} %refs_1_.5, ...), custom_call_target="tpu_custom_call" | custom-call | tf_op jit(solution)/shard_map/pallas_call | solution.py:133
  8.2 0.5 collective-permute-start
  8.7 1.6 collective-permute-done.refs_6_
  10.3 0.7 copy-done.27
  11.0 3.1 %shard_map.230 = (bf16[256,128]{1,0:T(8,128)(2,1)}, f32[128,768]{1,0:T(8,128)}, bf16[256,1536]{1,0:T(8,128)(2,1)}, bf16[128,768]{1,0:T(8,128)(2,1)}) custom-call(s32[1,128]{1,0:T(1,128)} %bitcast.22, bf16[128,768]{1,0:T(8,128)(2,1)} %refs_5_.3, bf16[256,768]{1,0:T(8,128)(2,1)} %refs_0_.3, f32[128,768]{1,0:T(8,128)} %get-tuple-element.66.refs_3_, ...), custom_call_target="tpu_custom_call" | custom-call | tf_op jit(solution)/shard_map/pallas_call | solution.py:133
  14.1 8.2 %all-to-all-start = ((bf16[16,16,1536]{2,1,0:T(8,128)(2,1)}), bf16[16,16,1536]{2,1,0:T(8,128)(2,1)S(1)}, u32[]{:S(2)}, u32[]{:S(2)}) async-start(bf16[16,16,1536]{2,1,0:T(8,128)(2,1)} %bitcast.18), calls=%async_computation | async-start | bytes 1572864 | tf_op jit(solution)/shard_map/all_to_all | solution.py:728
  22.4 2.8 %collective-permute-start.5 = (bf16[128,768]{1,0:T(8,128)(2,1)}, bf16[128,768]{1,0:T(8,128)(2,1)S(1)}, u32[]{:S(2)}, u32[]{:S(2)}) collective-permute-start(bf16[128,768]{1,0:T(8,128)(2,1)} %get-tuple-element.70), channel_id=1, source_target_pairs={{0,6},{2,4},{4,2},{6,0},{8,14},{10,12},{12,10},{14,8},{16,22},{18,... | collective-permute-start | bytes 589832 | tf_op jit(solution)/shard_map/ppermute | solution.py:721
  25.2 0.6 collective-permute-start.4
  25.9 12.3 %collective-permute-done.5.refs_8_.refs_6_ = bf16[128,768]{1,0:T(8,128)(2,1)S(1)} collective-permute-done((bf16[128,768]{1,0:T(8,128)(2,1)}, bf16[128,768]{1,0:T(8,128)(2,1)S(1)}, u32[]{:S(2)}, u32[]{:S(2)}) %collective-permute-start.5) | collective-permute-done | bytes 196640 | tf_op jit(solution)/shard_map/ppermute | solution.py:721
  38.3 3.6 %collective-permute-done.4.refs_7_.refs_5_ = bf16[128,768]{1,0:T(8,128)(2,1)S(1)} collective-permute-done((bf16[128,768]{1,0:T(8,128)(2,1)}, bf16[128,768]{1,0:T(8,128)(2,1)S(1)}, u32[]{:S(2)}, u32[]{:S(2)}) %collective-permute-start.4) | collective-permute-done | bytes 196640 | tf_op jit(solution)/shard_map/ppermute | solution.py:721
  43.4 12.0 %shard_map.231 = (bf16[256,768]{1,0:T(8,128)(2,1)}, bf16[256,768]{1,0:T(8,128)(2,1)}, f32[16,768]{1,0:T(8,128)}, bf16[256,768]{1,0:T(8,128)(2,1)}, bf16[256,768]...) custom-call(bf16[256,1536]{1,0:T(8,128)(2,1)} %bitcast.13, ...), custom_call_target="tpu_custom_call" | custom-call | tf_op jit(solution)/shard_map/pallas_call | solution.py:133
  55.3 6.9 %all-to-all-start.1 = ((bf16[16,16,768]{2,1,0:T(8,128)(2,1)}), bf16[16,16,768]{2,1,0:T(8,128)(2,1)}, u32[]{:S(2)}, u32[]{:S(2)}) async-start(bf16[16,16,768]{2,1,0:T(8,128)(2,1)} %bitcast.19), calls=%async_computation.1 | async-start | bytes 786432 | tf_op jit(solution)/shard_map/all_to_all | solution.py:728
  62.3 0.5 collective-permute-start.11
  63.4 1.6 collective-permute-done.11.refs_6_
  65.4 2.0 %collective-permute-done.9.refs_1_ = bf16[256,128]{1,0:T(8,128)(2,1)S(1)} collective-permute-done((bf16[256,128]{1,0:T(8,128)(2,1)}, bf16[256,128]{1,0:T(8,128)(2,1)S(1)}, u32[]{:S(2)}, u32[]{:S(2)}) %collective-permute-start.9) | collective-permute-done | bytes 65568 | tf_op jit(solution)/shard_map/ppermute | solution.py:718
  67.9 1.5 collective-permute-done.17.refs_17_.refs_4_
  69.4 5.1 %all-to-all-done.1 = bf16[16,16,768]{2,1,0:T(8,128)(2,1)} async-done(((bf16[16,16,768]{2,1,0:T(8,128)(2,1)}), bf16[16,16,768]{2,1,0:T(8,128)(2,1)}, u32[]{:S(2)}, u32[]{:S(2)}) %all-to-all-start.1) | async-done | bytes 393248 | tf_op jit(solution)/shard_map/all_to_all | solution.py:728
  74.5 0.5 collective-permute-start.25
  75.6 0.8 collective-permute-done.12.refs_8_
  76.5 0.7 copy-done.26
  77.2 9.5 %shard_map.232 = (bf16[256,768]{1,0:T(8,128)(2,1)}, f32[1,768]{1,0:T(1,128)}, bf16[256,1152]{1,0:T(8,128)(2,1)}, f32[6,32]{1,0:T(8,128)}, bf16[576,256]{1,0:T(8,...) custom-call(bf16[256,128]{1,0:T(8,128)(2,1)} %get-tuple-element.75.refs_0_.refs_4_, ...), custom_call_target="tpu_custom_call" | custom-call | tf_op jit(solution)/shard_map/pallas_call | solution.py:133
  87.9 0.8 copy-done.24
  88.7 0.6 collective-permute-start.18
  89.3 0.9 collective-permute-start.19
  90.1 2.0 %collective-permute-start.20 = (bf16[576,256]{1,0:T(8,128)(2,1)}, bf16[576,256]{1,0:T(8,128)(2,1)S(1)}, u32[]{:S(2)}, u32[]{:S(2)}) collective-permute-start(bf16[576,256]{1,0:T(8,128)(2,1)} %get-tuple-element.89), channel_id=1, source_target_pairs={{0,6},{2,4},{4,2},{6,0},{8,14},{10,12},{12,10},{14,8},{16,22},{18,... | collective-permute-start | bytes 884744 | tf_op jit(solution)/shard_map/ppermute | solution.py:721
  92.2 1.1 collective-permute-start.6
  93.3 3.5 %collective-permute-done.6.refs_12_.refs_1_ = bf16[64,768]{1,0:T(8,128)(2,1)S(1)} collective-permute-done((bf16[64,768]{1,0:T(8,128)(2,1)S(1)}, bf16[64,768]{1,0:T(8,128)(2,1)S(1)}, u32[]{:S(2)}, u32[]{:S(2)}) %collective-permute-start.6) | collective-permute-done | bytes 98336 | tf_op jit(solution)/shard_map/ppermute | solution.py:721
  97.3 3.1 %collective-permute-start.8 = (bf16[64,768]{1,0:T(8,128)(2,1)S(1)}, bf16[64,768]{1,0:T(8,128)(2,1)S(1)}, u32[]{:S(2)}, u32[]{:S(2)}) collective-permute-start(bf16[64,768]{1,0:T(8,128)(2,1)S(1)} %copy-done.49), channel_id=1, source_target_pairs={{0,24},{2,26},{4,28},{6,30},{8,16},{10,18},{12,20},{14,22},{16,8},... | collective-permute-start | bytes 294920 | tf_op jit(solution)/shard_map/ppermute | solution.py:721
  100.3 5.6 %shard_map.233 = (f32[256,768]{1,0:T(8,128)}, bf16[32,768]{1,0:T(8,128)(2,1)}) custom-call(bf16[256,768]{1,0:T(8,128)(2,1)} %refs_0_.3, f32[768]{0:T(1024)} %refs_1_.5, bf16[256,768]{1,0:T(8,128)(2,1)} %get-tuple-element.90.refs_2_, f32[16,768]{1,0:T(8,128)} %get-tuple-element.85.refs_3_, f32[16,768]{1,0:T(8,128)} %copy-done.28, ...), custom_call_target="tpu_custom_call" | custom-call | tf_op jit(solution)/shard_map/pallas_call | solution.py:133
  106.1 0.8 copy-done.14
  106.9 5.2 %shard_map.234 = (bf16[128,768]{1,0:T(8,128)(2,1)S(1)}, bf16[128,768]{1,0:T(8,128)(2,1)S(1)}, bf16[128,768]{1,0:T(8,128)(2,1)S(1)}, bf16[128,768]{1,0:T(8,128)(2,1)S(1)}) custom-call(bf16[576,256]{1,0:T(8,128)(2,1)S(1)} %copy-done.12, bf16[576,256]{1,0:T(8,128)(2,1)S(1)} %collective-permute-done.18.refs_1_, ...), custom_call_target="tpu_custom_call" | custom-call | tf_op jit(solution)/shard_map/pallas_call | solution.py:133
  112.0 1.8 %collective-permute-start.28 = (bf16[128,768]{1,0:T(8,128)(2,1)S(1)}, bf16[128,768]{1,0:T(8,128)(2,1)S(1)}, u32[]{:S(2)}, u32[]{:S(2)}) collective-permute-start(bf16[128,768]{1,0:T(8,128)(2,1)S(1)} %get-tuple-element.95), channel_id=1, source_target_pairs={{0,8},{2,10},{4,12},{6,14},{8,0},{10,2},{12,4},{14,6},{16,24},{18,... | collective-permute-start | bytes 589832 | tf_op jit(solution)/shard_map/ppermute | solution.py:721
  114.3 2.2 %collective-permute-start.33 = (bf16[128,768]{1,0:T(8,128)(2,1)S(1)}, bf16[128,768]{1,0:T(8,128)(2,1)S(1)}, u32[]{:S(2)}, u32[]{:S(2)}) collective-permute-start(bf16[128,768]{1,0:T(8,128)(2,1)S(1)} %get-tuple-element.104), channel_id=1, source_target_pairs={{0,24},{2,26},{4,28},{6,30},{8,16},{10,18},{12,20},{14,22},{16,8},... | collective-permute-start | bytes 589832 | tf_op jit(solution)/shard_map/ppermute | solution.py:721
  116.5 3.2 %collective-permute-done.28.refs_4_.refs_1_ = bf16[128,768]{1,0:T(8,128)(2,1)S(1)} collective-permute-done((bf16[128,768]{1,0:T(8,128)(2,1)S(1)}, bf16[128,768]{1,0:T(8,128)(2,1)S(1)}, u32[]{:S(2)}, u32[]{:S(2)}) %collective-permute-start.28) | collective-permute-done | bytes 196640 | tf_op jit(solution)/shard_map/ppermute | solution.py:721
  119.7 0.7 copy-done.1
  120.4 1.9 %shard_map.235 = (bf16[64,768]{1,0:T(8,128)(2,1)}, bf16[64,768]{1,0:T(8,128)(2,1)}, bf16[64,768]{1,0:T(8,128)(2,1)}, bf16[64,768]{1,0:T(8,128)(2,1)}) custom-call(bf16[64,768]{1,0:T(8,128)(2,1)} %get-tuple-element.71.refs_0_, bf16[64,768]{1,0:T(8,128)(2,1)} %copy-done.9, bf16[64,768]{1,0:T(8,128)(2,1)} %copy-done.10, bf16[64,768]{1,0:T(8,128)(2,1)} %copy-done.11, ...), custom_call_target="tpu_custom_call" | custom-call | tf_op jit(solution)/shard_map/pallas_call | solution.py:133
  122.3 0.8 collective-permute-start.29
  123.0 1.0 collective-permute-start.30
  124.0 6.9 %shard_map.237 = (f32[768,1536]{1,0:T(8,128)}, f32[1536,768]{1,0:T(8,128)}, f32[8,128]{1,0:T(8,128)}) custom-call(bf16[256,768]{1,0:T(8,128)(2,1)} %get-tuple-element.81.rows_ref, bf16[256,768]{1,0:T(8,128)(2,1)} %collective-permute-done.13.refs_13_.rows_far_ref, bf16[256,768]{1,0:T(8,128)(2,1)} %get-tuple-element.82.grad_produced_ref, ...), custom_call_target="tpu_custom_call" | custom-call | tf_op jit(solution)/shard_map/pallas_call | solution.py:663
  130.9 1.8 %collective-permute-start.31 = (bf16[64,768]{1,0:T(8,128)(2,1)S(1)}, bf16[64,768]{1,0:T(8,128)(2,1)S(1)}, u32[]{:S(2)}, u32[]{:S(2)}) collective-permute-start(bf16[64,768]{1,0:T(8,128)(2,1)S(1)} %copy-done.52), channel_id=1, source_target_pairs={{0,6},{2,4},{4,2},{6,0},{8,14},{10,12},{12,10},{14,8},{16,22},{18,... | collective-permute-start | bytes 294920 | tf_op jit(solution)/shard_map/ppermute | solution.py:721
  132.8 0.7 copy-done.15
  133.6 2.1 %collective-permute-start.45 = (bf16[96,768]{1,0:T(8,128)(2,1)S(1)}, bf16[96,768]{1,0:T(8,128)(2,1)S(1)}, u32[]{:S(2)}, u32[]{:S(2)}) collective-permute-start(bf16[96,768]{1,0:T(8,128)(2,1)S(1)} %get-tuple-element.109), channel_id=1, source_target_pairs={{0,24},{2,26},{4,28},{6,30},{8,16},{10,18},{12,20},{14,22},{16,8},... | collective-permute-start | bytes 442376 | tf_op jit(solution)/shard_map/ppermute | solution.py:721
  135.7 1.2 collective-permute-start.36
  136.8 1.0 collective-permute-start.35
  137.8 1.3 collective-permute-start.41
  139.2 1.0 collective-permute-start.37
  140.2 2.0 %collective-permute-done.45.refs_12_ = bf16[96,768]{1,0:T(8,128)(2,1)S(1)} collective-permute-done((bf16[96,768]{1,0:T(8,128)(2,1)S(1)}, bf16[96,768]{1,0:T(8,128)(2,1)S(1)}, u32[]{:S(2)}, u32[]{:S(2)}) %collective-permute-start.45) | collective-permute-done | bytes 147488 | tf_op jit(solution)/shard_map/ppermute | solution.py:721
  142.2 0.6 collective-permute-start.34
  142.8 4.3 %collective-permute-done.41.refs_8_ = bf16[96,768]{1,0:T(8,128)(2,1)S(1)} collective-permute-done((bf16[96,768]{1,0:T(8,128)(2,1)S(1)}, bf16[96,768]{1,0:T(8,128)(2,1)S(1)}, u32[]{:S(2)}, u32[]{:S(2)}) %collective-permute-start.41) | collective-permute-done | bytes 147488 | tf_op jit(solution)/shard_map/ppermute | solution.py:721
  147.1 1.8 %collective-permute-start.48 = (bf16[96,768]{1,0:T(8,128)(2,1)S(1)}, bf16[96,768]{1,0:T(8,128)(2,1)S(1)}, u32[]{:S(2)}, u32[]{:S(2)}) collective-permute-start(bf16[96,768]{1,0:T(8,128)(2,1)S(1)} %collective-permute-done.45.refs_12_), channel_id=1, source_target_pairs={{0,6},{2,4},{4,2},{6,0},{8,14},{10,12},{12,10},{14,8},{16,22},{18,... | collective-permute-start | bytes 442376 | tf_op jit(solution)/shard_map/ppermute | solution.py:721
  148.8 1.1 collective-permute-start.47
  149.9 0.7 collective-permute-start.46
  150.6 1.0 collective-permute-start.43
  151.8 1.8 %collective-permute-done.48.refs_15_ = bf16[96,768]{1,0:T(8,128)(2,1)S(1)} collective-permute-done((bf16[96,768]{1,0:T(8,128)(2,1)S(1)}, bf16[96,768]{1,0:T(8,128)(2,1)S(1)}, u32[]{:S(2)}, u32[]{:S(2)}) %collective-permute-start.48) | collective-permute-done | bytes 147488 | tf_op jit(solution)/shard_map/ppermute | solution.py:721
  153.8 3.0 %collective-permute-done.47.refs_14_ = bf16[96,768]{1,0:T(8,128)(2,1)S(1)} collective-permute-done((bf16[96,768]{1,0:T(8,128)(2,1)S(1)}, bf16[96,768]{1,0:T(8,128)(2,1)S(1)}, u32[]{:S(2)}, u32[]{:S(2)}) %collective-permute-start.47) | collective-permute-done | bytes 147488 | tf_op jit(solution)/shard_map/ppermute | solution.py:721
  156.8 1.0 collective-permute-start.42
  157.8 1.0 collective-permute-start.39
  159.2 0.9 collective-permute-start.38
  160.1 2.2 %shard_map.236 = (bf16[128,768]{1,0:T(8,128)(2,1)}, f32[8,128]{1,0:T(8,128)}) custom-call(bf16[64,768]{1,0:T(8,128)(2,1)} %get-tuple-element.96.refs_0_, bf16[64,768]{1,0:T(8,128)(2,1)} %copy-done.45, bf16[64,768]{1,0:T(8,128)(2,1)} %copy-done.46, bf16[64,768]{1,0:T(8,128)(2,1)} %copy-done.47, bf16[256,128]{1,0:T(8,128)(2,1)} %get-tuple-element.75.refs_0_.refs_4_, ...), custom_call_target="tpu_custom_call" | custom-call | tf_op jit(solution)/shard_map/pallas_call | solution.py:133
  162.4 0.6 collective-permute-done.39.refs_6_
  163.0 1.4 collective-permute-done.38.refs_5_
  164.5 0.5 copy-done.44
  165.2 5.1 %shard_map.239 = (f32[768,384]{1,0:T(8,128)}, f32[768,384]{1,0:T(8,128)}, f32[768,384]{1,0:T(8,128)}, f32[384,768]{1,0:T(8,128)}, f32[16,768]{1,0:T(8,128)}, /*i...) custom-call(bf16[128,768]{1,0:T(8,128)(2,1)} %copy-done.13, bf16[128,768]{1,0:T(8,128)(2,1)} %copy-done.32, ...), custom_call_target="tpu_custom_call" | custom-call | tf_op jit(solution)/shard_map/pallas_call | solution.py:133
  (155 shorter events, 7.2 us)
Async XLA Ops:
  0.6 41.8 %collective-permute-start.1 = (bf16[768,1536]{1,0:T(8,128)(2,1)}, bf16[768,1536]{1,0:T(8,128)(2,1)}, u32[]{:S(2)}, u32[]{:S(2)}) collective-permute-start(bf16[768,1536]{1,0:T(8,128)(2,1)} %bitcast.14), channel_id=1, source_target_pairs={{0,1},{1,0},{2,3},{3,2},{4,5},{5,4},{6,7},{7,6},{8,9},{9,8},{10,11... | collective-permute-start | bytes 7077896 | tf_op jit(solution)/shard_map/ppermute | solution.py:718
  1.2 41.3 %collective-permute-start.2 = (bf16[1536,768]{1,0:T(8,128)(2,1)}, bf16[1536,768]{1,0:T(8,128)(2,1)}, u32[]{:S(2)}, u32[]{:S(2)}) collective-permute-start(bf16[1536,768]{1,0:T(8,128)(2,1)} %bitcast.16), channel_id=1, source_target_pairs={{0,1},{1,0},{2,3},{3,2},{4,5},{5,4},{6,7},{7,6},{8,9},{9,8},{10,11... | collective-permute-start | bytes 7077896 | tf_op jit(solution)/shard_map/ppermute | solution.py:718
  8.2 2.1 %collective-permute-start = (f32[128,768]{1,0:T(8,128)}, f32[128,768]{1,0:T(8,128)S(1)}, u32[]{:S(2)}, u32[]{:S(2)}) collective-permute-start(f32[128,768]{1,0:T(8,128)} %get-tuple-element.68), channel_id=1, source_target_pairs={{0,1},{1,0},{2,3},{3,2},{4,5},{5,4},{6,7},{7,6},{8,9},{9,8},{10,11... | collective-permute-start | bytes 1179656 | tf_op jit(solution)/shard_map/ppermute | solution.py:718
  14.1 28.3 %all-to-all-start = ((bf16[16,16,1536]{2,1,0:T(8,128)(2,1)}), bf16[16,16,1536]{2,1,0:T(8,128)(2,1)S(1)}, u32[]{:S(2)}, u32[]{:S(2)}) async-start(bf16[16,16,1536]{2,1,0:T(8,128)(2,1)} %bitcast.18), calls=%async_computation | async-start | bytes 1572864 | tf_op jit(solution)/shard_map/all_to_all | solution.py:728
  22.4 15.9 %collective-permute-start.5 = (bf16[128,768]{1,0:T(8,128)(2,1)}, bf16[128,768]{1,0:T(8,128)(2,1)S(1)}, u32[]{:S(2)}, u32[]{:S(2)}) collective-permute-start(bf16[128,768]{1,0:T(8,128)(2,1)} %get-tuple-element.70), channel_id=1, source_target_pairs={{0,6},{2,4},{4,2},{6,0},{8,14},{10,12},{12,10},{14,8},{16,22},{18,... | collective-permute-start | bytes 589832 | tf_op jit(solution)/shard_map/ppermute | solution.py:721
  25.2 16.7 %collective-permute-start.4 = (bf16[128,768]{1,0:T(8,128)(2,1)}, bf16[128,768]{1,0:T(8,128)(2,1)S(1)}, u32[]{:S(2)}, u32[]{:S(2)}) collective-permute-start(bf16[128,768]{1,0:T(8,128)(2,1)} %get-tuple-element.70), channel_id=1, source_target_pairs={{0,4},{2,6},{4,0},{6,2},{8,12},{10,14},{12,8},{14,10},{16,20},{18,... | collective-permute-start | bytes 589832 | tf_op jit(solution)/shard_map/ppermute | solution.py:721
  25.8 16.6 %collective-permute-start.3 = (bf16[128,768]{1,0:T(8,128)(2,1)}, bf16[128,768]{1,0:T(8,128)(2,1)S(1)}, u32[]{:S(2)}, u32[]{:S(2)}) collective-permute-start(bf16[128,768]{1,0:T(8,128)(2,1)} %get-tuple-element.70), channel_id=1, source_target_pairs={{0,2},{2,0},{4,6},{6,4},{8,10},{10,8},{12,14},{14,12},{16,18},{18,... | collective-permute-start | bytes 589832 | tf_op jit(solution)/shard_map/ppermute | solution.py:721
  43.3 18.9 %copy-start.22 = (bf16[128,768]{1,0:T(8,128)(2,1)S(1)}, bf16[128,768]{1,0:T(8,128)(2,1)}, u32[]{:S(2)}) copy-start(bf16[128,768]{1,0:T(8,128)(2,1)} %refs_5_.3) | copy-start | bytes 589828
  43.3 31.1 %copy-start.19 = (bf16[768,384]{1,0:T(8,128)(2,1)S(1)}, bf16[768,384]{1,0:T(8,128)(2,1)}, u32[]{:S(2)}) copy-start(bf16[768,384]{1,0:T(8,128)(2,1)} %refs_9_.3) | copy-start | bytes 1769476
  43.3 31.7 %copy-start.20 = (bf16[768,384]{1,0:T(8,128)(2,1)S(1)}, bf16[768,384]{1,0:T(8,128)(2,1)}, u32[]{:S(2)}) copy-start(bf16[768,384]{1,0:T(8,128)(2,1)} %refs_10_.1) | copy-start | bytes 1769476
  43.3 31.7 %copy-start.21 = (bf16[768,384]{1,0:T(8,128)(2,1)S(1)}, bf16[768,384]{1,0:T(8,128)(2,1)}, u32[]{:S(2)}) copy-start(bf16[768,384]{1,0:T(8,128)(2,1)} %refs_8_.1) | copy-start | bytes 1769476
  55.3 19.1 %all-to-all-start.1 = ((bf16[16,16,768]{2,1,0:T(8,128)(2,1)}), bf16[16,16,768]{2,1,0:T(8,128)(2,1)}, u32[]{:S(2)}, u32[]{:S(2)}) async-start(bf16[16,16,768]{2,1,0:T(8,128)(2,1)} %bitcast.19), calls=%async_computation.1 | async-start | bytes 786432 | tf_op jit(solution)/shard_map/all_to_all | solution.py:728
  62.2 12.9 %collective-permute-start.15 = (bf16[256,1536]{1,0:T(8,128)(2,1)}, bf16[256,1536]{1,0:T(8,128)(2,1)S(1)}, u32[]{:S(2)}, u32[]{:S(2)}) collective-permute-start(bf16[256,1536]{1,0:T(8,128)(2,1)} %get-tuple-element.83), channel_id=1, source_target_pairs={{0,1},{1,0},{2,3},{3,2},{4,5},{5,4},{6,7},{7,6},{8,9},{9,8},{10,11... | collective-permute-start | bytes 2359304 | tf_op jit(solution)/shard_map/ppermute | solution.py:718
  62.3 2.7 %collective-permute-start.11 = (bf16[128,768]{1,0:T(8,128)(2,1)S(1)}, bf16[128,768]{1,0:T(8,128)(2,1)S(1)}, u32[]{:S(2)}, u32[]{:S(2)}) collective-permute-start(bf16[128,768]{1,0:T(8,128)(2,1)S(1)} %copy-done.22), channel_id=1, source_target_pairs={{0,1},{1,0},{2,3},{3,2},{4,5},{5,4},{6,7},{7,6},{8,9},{9,8},{10,11... | collective-permute-start | bytes 589832 | tf_op jit(solution)/shard_map/ppermute | solution.py:718
  62.8 4.7 %collective-permute-start.10 = (f32[128,768]{1,0:T(8,128)}, f32[128,768]{1,0:T(8,128)}, u32[]{:S(2)}, u32[]{:S(2)}) collective-permute-start(f32[128,768]{1,0:T(8,128)} %get-tuple-element.76.refs_2_.refs_5_), channel_id=1, source_target_pairs={{0,1},{1,0},{2,3},{3,2},{4,5},{5,4},{6,7},{7,6},{8,9},{9,8},{10,11... | collective-permute-start | bytes 1179656 | tf_op jit(solution)/shard_map/ppermute | solution.py:718
  62.9 12.7 %collective-permute-start.16 = (bf16[256,1536]{1,0:T(8,128)(2,1)}, bf16[256,1536]{1,0:T(8,128)(2,1)S(1)}, u32[]{:S(2)}, u32[]{:S(2)}) collective-permute-start(bf16[256,1536]{1,0:T(8,128)(2,1)} %get-tuple-element.84), channel_id=1, source_target_pairs={{0,1},{1,0},{2,3},{3,2},{4,5},{5,4},{6,7},{7,6},{8,9},{9,8},{10,11... | collective-permute-start | bytes 2359304 | tf_op jit(solution)/shard_map/ppermute | solution.py:718
  63.3 11.2 %collective-permute-start.13 = (bf16[256,768]{1,0:T(8,128)(2,1)}, bf16[256,768]{1,0:T(8,128)(2,1)}, u32[]{:S(2)}, u32[]{:S(2)}) collective-permute-start(bf16[256,768]{1,0:T(8,128)(2,1)} %get-tuple-element.81.rows_ref), channel_id=1, source_target_pairs={{0,1},{1,0},{2,3},{3,2},{4,5},{5,4},{6,7},{7,6},{8,9},{9,8},{10,11... | collective-permute-start | bytes 1179656 | tf_op jit(solution)/shard_map/ppermute | solution.py:718
  65.0 2.4 %collective-permute-start.9 = (bf16[256,128]{1,0:T(8,128)(2,1)}, bf16[256,128]{1,0:T(8,128)(2,1)S(1)}, u32[]{:S(2)}, u32[]{:S(2)}) collective-permute-start(bf16[256,128]{1,0:T(8,128)(2,1)} %get-tuple-element.75.refs_0_.refs_4_), channel_id=1, source_target_pairs={{0,1},{1,0},{2,3},{3,2},{4,5},{5,4},{6,7},{7,6},{8,9},{9,8},{10,11... | collective-permute-start | bytes 196616 | tf_op jit(solution)/shard_map/ppermute | solution.py:718
  67.4 7.6 %collective-permute-start.14 = (bf16[256,768]{1,0:T(8,128)(2,1)}, bf16[256,768]{1,0:T(8,128)(2,1)}, u32[]{:S(2)}, u32[]{:S(2)}) collective-permute-start(bf16[256,768]{1,0:T(8,128)(2,1)} %get-tuple-element.82.grad_produced_ref), channel_id=1, source_target_pairs={{0,1},{1,0},{2,3},{3,2},{4,5},{5,4},{6,7},{7,6},{8,9},{9,8},{10,11... | collective-permute-start | bytes 1179656 | tf_op jit(solution)/shard_map/ppermute | solution.py:718
  67.5 1.9 %collective-permute-start.17 = (f32[16,768]{1,0:T(8,128)}, f32[16,768]{1,0:T(8,128)S(1)}, u32[]{:S(2)}, u32[]{:S(2)}) collective-permute-start(f32[16,768]{1,0:T(8,128)} %get-tuple-element.85.refs_3_), channel_id=1, source_target_pairs={{0,1},{1,0},{2,3},{3,2},{4,5},{5,4},{6,7},{7,6},{8,9},{9,8},{10,11... | collective-permute-start | bytes 147464 | tf_op jit(solution)/shard_map/ppermute | solution.py:718
  74.5 1.9 %collective-permute-start.12 = (bf16[256,768]{1,0:T(8,128)(2,1)}, bf16[256,768]{1,0:T(8,128)(2,1)S(1)}, u32[]{:S(2)}, u32[]{:S(2)}) collective-permute-start(bf16[256,768]{1,0:T(8,128)(2,1)} %bitcast.8.refs_7_), channel_id=1, source_target_pairs={{0,1},{1,0},{2,3},{3,2},{4,5},{5,4},{6,7},{7,6},{8,9},{9,8},{10,11... | collective-permute-start | bytes 1179656 | tf_op jit(solution)/shard_map/ppermute | solution.py:718
  74.5 12.8 %collective-permute-start.25 = (bf16[768,384]{1,0:T(8,128)(2,1)S(1)}, bf16[768,384]{1,0:T(8,128)(2,1)S(1)}, u32[]{:S(2)}, u32[]{:S(2)}) collective-permute-start(bf16[768,384]{1,0:T(8,128)(2,1)S(1)} %copy-done.19), channel_id=1, source_target_pairs={{0,1},{1,0},{2,3},{3,2},{4,5},{5,4},{6,7},{7,6},{8,9},{9,8},{10,11... | collective-permute-start | bytes 1769480 | tf_op jit(solution)/shard_map/ppermute | solution.py:718
  75.0 12.5 %collective-permute-start.26 = (bf16[768,384]{1,0:T(8,128)(2,1)S(1)}, bf16[768,384]{1,0:T(8,128)(2,1)}, u32[]{:S(2)}, u32[]{:S(2)}) collective-permute-start(bf16[768,384]{1,0:T(8,128)(2,1)S(1)} %copy-done.20), channel_id=1, source_target_pairs={{0,1},{1,0},{2,3},{3,2},{4,5},{5,4},{6,7},{7,6},{8,9},{9,8},{10,11... | collective-permute-start | bytes 1769480 | tf_op jit(solution)/shard_map/ppermute | solution.py:718
  75.1 12.8 %collective-permute-start.24 = (bf16[768,384]{1,0:T(8,128)(2,1)S(1)}, bf16[768,384]{1,0:T(8,128)(2,1)S(1)}, u32[]{:S(2)}, u32[]{:S(2)}) collective-permute-start(bf16[768,384]{1,0:T(8,128)(2,1)S(1)} %copy-done.21), channel_id=1, source_target_pairs={{0,1},{1,0},{2,3},{3,2},{4,5},{5,4},{6,7},{7,6},{8,9},{9,8},{10,11... | collective-permute-start | bytes 1769480 | tf_op jit(solution)/shard_map/ppermute | solution.py:718
  77.2 19.6 %copy-start.50 = (bf16[64,768]{1,0:T(8,128)(2,1)S(1)}, bf16[64,768]{1,0:T(8,128)(2,1)}, u32[]{:S(2)}) copy-start(bf16[64,768]{1,0:T(8,128)(2,1)} %get-tuple-element.73) | copy-start | bytes 294916
  77.2 20.1 %copy-start.49 = (bf16[64,768]{1,0:T(8,128)(2,1)S(1)}, bf16[64,768]{1,0:T(8,128)(2,1)}, u32[]{:S(2)}) copy-start(bf16[64,768]{1,0:T(8,128)(2,1)} %get-tuple-element.74) | copy-start | bytes 294916
  86.7 10.6 %collective-permute-start.27 = (bf16[256,1152]{1,0:T(8,128)(2,1)}, bf16[256,1152]{1,0:T(8,128)(2,1)S(1)}, u32[]{:S(2)}, u32[]{:S(2)}) collective-permute-start(bf16[256,1152]{1,0:T(8,128)(2,1)} %get-tuple-element.93.refs_7_), channel_id=1, source_target_pairs={{0,1},{1,0},{2,3},{3,2},{4,5},{5,4},{6,7},{7,6},{8,9},{9,8},{10,11... | collective-permute-start | bytes 1769480 | tf_op jit(solution)/shard_map/ppermute | solution.py:718
  86.9 2.4 %collective-permute-start.23 = (bf16[128,768]{1,0:T(8,128)(2,1)S(1)}, bf16[128,768]{1,0:T(8,128)(2,1)S(1)}, u32[]{:S(2)}, u32[]{:S(2)}) collective-permute-start(bf16[128,768]{1,0:T(8,128)(2,1)S(1)} %copy-done.4), channel_id=1, source_target_pairs={{0,1},{1,0},{2,3},{3,2},{4,5},{5,4},{6,7},{7,6},{8,9},{9,8},{10,11... | collective-permute-start | bytes 589832 | tf_op jit(solution)/shard_map/ppermute | solution.py:718
  87.3 2.9 %collective-permute-start.22 = (bf16[128,768]{1,0:T(8,128)(2,1)S(1)}, bf16[128,768]{1,0:T(8,128)(2,1)S(1)}, u32[]{:S(2)}, u32[]{:S(2)}) collective-permute-start(bf16[128,768]{1,0:T(8,128)(2,1)S(1)} %copy-done.6), channel_id=1, source_target_pairs={{0,1},{1,0},{2,3},{3,2},{4,5},{5,4},{6,7},{7,6},{8,9},{9,8},{10,11... | collective-permute-start | bytes 589832 | tf_op jit(solution)/shard_map/ppermute | solution.py:718
  87.5 4.7 %collective-permute-start.21 = (bf16[128,768]{1,0:T(8,128)(2,1)S(1)}, bf16[128,768]{1,0:T(8,128)(2,1)S(1)}, u32[]{:S(2)}, u32[]{:S(2)}) collective-permute-start(bf16[128,768]{1,0:T(8,128)(2,1)S(1)} %copy-done.8), channel_id=1, source_target_pairs={{0,1},{1,0},{2,3},{3,2},{4,5},{5,4},{6,7},{7,6},{8,9},{9,8},{10,11... | collective-permute-start | bytes 589832 | tf_op jit(solution)/shard_map/ppermute | solution.py:718
  88.7 17.3 %collective-permute-start.18 = (bf16[576,256]{1,0:T(8,128)(2,1)}, bf16[576,256]{1,0:T(8,128)(2,1)S(1)}, u32[]{:S(2)}, u32[]{:S(2)}) collective-permute-start(bf16[576,256]{1,0:T(8,128)(2,1)} %get-tuple-element.87), channel_id=1, source_target_pairs={{0,2},{2,0},{4,6},{6,4},{8,10},{10,8},{12,14},{14,12},{16,18},{18,... | collective-permute-start | bytes 884744 | tf_op jit(solution)/shard_map/ppermute | solution.py:721
  89.3 16.8 %collective-permute-start.19 = (bf16[576,256]{1,0:T(8,128)(2,1)}, bf16[576,256]{1,0:T(8,128)(2,1)S(1)}, u32[]{:S(2)}, u32[]{:S(2)}) collective-permute-start(bf16[576,256]{1,0:T(8,128)(2,1)} %get-tuple-element.88), channel_id=1, source_target_pairs={{0,4},{2,6},{4,0},{6,2},{8,12},{10,14},{12,8},{14,10},{16,20},{18,... | collective-permute-start | bytes 884744 | tf_op jit(solution)/shard_map/ppermute | solution.py:721
  90.1 15.9 %collective-permute-start.20 = (bf16[576,256]{1,0:T(8,128)(2,1)}, bf16[576,256]{1,0:T(8,128)(2,1)S(1)}, u32[]{:S(2)}, u32[]{:S(2)}) collective-permute-start(bf16[576,256]{1,0:T(8,128)(2,1)} %get-tuple-element.89), channel_id=1, source_target_pairs={{0,6},{2,4},{4,2},{6,0},{8,14},{10,12},{12,10},{14,8},{16,22},{18,... | collective-permute-start | bytes 884744 | tf_op jit(solution)/shard_map/ppermute | solution.py:721
  92.2 4.6 %collective-permute-start.6 = (bf16[64,768]{1,0:T(8,128)(2,1)S(1)}, bf16[64,768]{1,0:T(8,128)(2,1)S(1)}, u32[]{:S(2)}, u32[]{:S(2)}) collective-permute-start(bf16[64,768]{1,0:T(8,128)(2,1)S(1)} %copy-done.51), channel_id=1, source_target_pairs={{0,8},{2,10},{4,12},{6,14},{8,0},{10,2},{12,4},{14,6},{16,24},{18,... | collective-permute-start | bytes 294920 | tf_op jit(solution)/shard_map/ppermute | solution.py:721
  96.8 9.2 %collective-permute-start.7 = (bf16[64,768]{1,0:T(8,128)(2,1)S(1)}, bf16[64,768]{1,0:T(8,128)(2,1)S(1)}, u32[]{:S(2)}, u32[]{:S(2)}) collective-permute-start(bf16[64,768]{1,0:T(8,128)(2,1)S(1)} %copy-done.50), channel_id=1, source_target_pairs={{0,16},{2,18},{4,20},{6,22},{8,24},{10,26},{12,28},{14,30},{16,0},... | collective-permute-start | bytes 294920 | tf_op jit(solution)/shard_map/ppermute | solution.py:721
  97.3 8.7 %collective-permute-start.8 = (bf16[64,768]{1,0:T(8,128)(2,1)S(1)}, bf16[64,768]{1,0:T(8,128)(2,1)S(1)}, u32[]{:S(2)}, u32[]{:S(2)}) collective-permute-start(bf16[64,768]{1,0:T(8,128)(2,1)S(1)} %copy-done.49), channel_id=1, source_target_pairs={{0,24},{2,26},{4,28},{6,30},{8,16},{10,18},{12,20},{14,22},{16,8},... | collective-permute-start | bytes 294920 | tf_op jit(solution)/shard_map/ppermute | solution.py:721
  112.0 7.7 %collective-permute-start.28 = (bf16[128,768]{1,0:T(8,128)(2,1)S(1)}, bf16[128,768]{1,0:T(8,128)(2,1)S(1)}, u32[]{:S(2)}, u32[]{:S(2)}) collective-permute-start(bf16[128,768]{1,0:T(8,128)(2,1)S(1)} %get-tuple-element.95), channel_id=1, source_target_pairs={{0,8},{2,10},{4,12},{6,14},{8,0},{10,2},{12,4},{14,6},{16,24},{18,... | collective-permute-start | bytes 589832 | tf_op jit(solution)/shard_map/ppermute | solution.py:721
  113.8 19.0 %collective-permute-start.32 = (bf16[128,768]{1,0:T(8,128)(2,1)S(1)}, bf16[128,768]{1,0:T(8,128)(2,1)S(1)}, u32[]{:S(2)}, u32[]{:S(2)}) collective-permute-start(bf16[128,768]{1,0:T(8,128)(2,1)S(1)} %get-tuple-element.103), channel_id=1, source_target_pairs={{0,16},{2,18},{4,20},{6,22},{8,24},{10,26},{12,28},{14,30},{16,0},... | collective-permute-start | bytes 589832 | tf_op jit(solution)/shard_map/ppermute | solution.py:721
  114.3 18.5 %collective-permute-start.33 = (bf16[128,768]{1,0:T(8,128)(2,1)S(1)}, bf16[128,768]{1,0:T(8,128)(2,1)S(1)}, u32[]{:S(2)}, u32[]{:S(2)}) collective-permute-start(bf16[128,768]{1,0:T(8,128)(2,1)S(1)} %get-tuple-element.104), channel_id=1, source_target_pairs={{0,24},{2,26},{4,28},{6,30},{8,16},{10,18},{12,20},{14,22},{16,8},... | collective-permute-start | bytes 589832 | tf_op jit(solution)/shard_map/ppermute | solution.py:721
  122.3 14.6 %collective-permute-start.29 = (bf16[64,768]{1,0:T(8,128)(2,1)}, bf16[64,768]{1,0:T(8,128)(2,1)S(1)}, u32[]{:S(2)}, u32[]{:S(2)}) collective-permute-start(bf16[64,768]{1,0:T(8,128)(2,1)} %get-tuple-element.97), channel_id=1, source_target_pairs={{0,2},{2,0},{4,6},{6,4},{8,10},{10,8},{12,14},{14,12},{16,18},{18,... | collective-permute-start | bytes 294920 | tf_op jit(solution)/shard_map/ppermute | solution.py:721
  123.0 14.8 %collective-permute-start.30 = (bf16[64,768]{1,0:T(8,128)(2,1)}, bf16[64,768]{1,0:T(8,128)(2,1)S(1)}, u32[]{:S(2)}, u32[]{:S(2)}) collective-permute-start(bf16[64,768]{1,0:T(8,128)(2,1)} %get-tuple-element.98), channel_id=1, source_target_pairs={{0,4},{2,6},{4,0},{6,2},{8,12},{10,14},{12,8},{14,10},{16,20},{18,... | collective-permute-start | bytes 294920 | tf_op jit(solution)/shard_map/ppermute | solution.py:721
  130.9 8.3 %collective-permute-start.31 = (bf16[64,768]{1,0:T(8,128)(2,1)S(1)}, bf16[64,768]{1,0:T(8,128)(2,1)S(1)}, u32[]{:S(2)}, u32[]{:S(2)}) collective-permute-start(bf16[64,768]{1,0:T(8,128)(2,1)S(1)} %copy-done.52), channel_id=1, source_target_pairs={{0,6},{2,4},{4,2},{6,0},{8,14},{10,12},{12,10},{14,8},{16,22},{18,... | collective-permute-start | bytes 294920 | tf_op jit(solution)/shard_map/ppermute | solution.py:721
  133.6 30.8 %copy-start.13 = (bf16[128,768]{1,0:T(8,128)(2,1)}, bf16[128,768]{1,0:T(8,128)(2,1)S(1)}, u32[]{:S(2)}) copy-start(bf16[128,768]{1,0:T(8,128)(2,1)S(1)} %get-tuple-element.108.refs_0_) | copy-start | bytes 589828
  133.6 8.6 %collective-permute-start.45 = (bf16[96,768]{1,0:T(8,128)(2,1)S(1)}, bf16[96,768]{1,0:T(8,128)(2,1)S(1)}, u32[]{:S(2)}, u32[]{:S(2)}) collective-permute-start(bf16[96,768]{1,0:T(8,128)(2,1)S(1)} %get-tuple-element.109), channel_id=1, source_target_pairs={{0,24},{2,26},{4,28},{6,30},{8,16},{10,18},{12,20},{14,22},{16,8},... | collective-permute-start | bytes 442376 | tf_op jit(solution)/shard_map/ppermute | solution.py:721
  135.7 14.2 %collective-permute-start.36 = (bf16[128,768]{1,0:T(8,128)(2,1)S(1)}, bf16[128,768]{1,0:T(8,128)(2,1)S(1)}, u32[]{:S(2)}, u32[]{:S(2)}) collective-permute-start(bf16[128,768]{1,0:T(8,128)(2,1)S(1)} %get-tuple-element.108.refs_0_), channel_id=1, source_target_pairs={{0,6},{2,4},{4,2},{6,0},{8,14},{10,12},{12,10},{14,8},{16,22},{18,... | collective-permute-start | bytes 589832 | tf_op jit(solution)/shard_map/ppermute | solution.py:721
  136.8 23.3 %copy-start.45 = (bf16[64,768]{1,0:T(8,128)(2,1)}, bf16[64,768]{1,0:T(8,128)(2,1)S(1)}, u32[]{:S(2)}) copy-start(bf16[64,768]{1,0:T(8,128)(2,1)S(1)} %collective-permute-done.29.refs_1_) | copy-start | bytes 294916
  136.8 13.7 %collective-permute-start.35 = (bf16[128,768]{1,0:T(8,128)(2,1)S(1)}, bf16[128,768]{1,0:T(8,128)(2,1)S(1)}, u32[]{:S(2)}, u32[]{:S(2)}) collective-permute-start(bf16[128,768]{1,0:T(8,128)(2,1)S(1)} %get-tuple-element.108.refs_0_), channel_id=1, source_target_pairs={{0,4},{2,6},{4,0},{6,2},{8,12},{10,14},{12,8},{14,10},{16,20},{18,... | collective-permute-start | bytes 589832 | tf_op jit(solution)/shard_map/ppermute | solution.py:721
  137.8 22.3 %copy-start.46 = (bf16[64,768]{1,0:T(8,128)(2,1)}, bf16[64,768]{1,0:T(8,128)(2,1)S(1)}, u32[]{:S(2)}) copy-start(bf16[64,768]{1,0:T(8,128)(2,1)S(1)} %collective-permute-done.30.refs_2_) | copy-start | bytes 294916
  137.8 9.2 %collective-permute-start.41 = (bf16[96,768]{1,0:T(8,128)(2,1)S(1)}, bf16[96,768]{1,0:T(8,128)(2,1)S(1)}, u32[]{:S(2)}, u32[]{:S(2)}) collective-permute-start(bf16[96,768]{1,0:T(8,128)(2,1)S(1)} %get-tuple-element.109), channel_id=1, source_target_pairs={{0,16},{2,18},{4,20},{6,22},{8,24},{10,26},{12,28},{14,30},{16,0},... | collective-permute-start | bytes 442376 | tf_op jit(solution)/shard_map/ppermute | solution.py:721
  139.2 21.0 %copy-start.47 = (bf16[64,768]{1,0:T(8,128)(2,1)}, bf16[64,768]{1,0:T(8,128)(2,1)S(1)}, u32[]{:S(2)}) copy-start(bf16[64,768]{1,0:T(8,128)(2,1)S(1)} %collective-permute-done.31.refs_3_) | copy-start | bytes 294916
  139.2 9.7 %collective-permute-start.37 = (bf16[96,768]{1,0:T(8,128)(2,1)S(1)}, bf16[96,768]{1,0:T(8,128)(2,1)S(1)}, u32[]{:S(2)}, u32[]{:S(2)}) collective-permute-start(bf16[96,768]{1,0:T(8,128)(2,1)S(1)} %get-tuple-element.109), channel_id=1, source_target_pairs={{0,8},{2,10},{4,12},{6,14},{8,0},{10,2},{12,4},{14,6},{16,24},{18,... | collective-permute-start | bytes 442376 | tf_op jit(solution)/shard_map/ppermute | solution.py:721
  142.2 22.2 %copy-start.35 = (bf16[96,768]{1,0:T(8,128)(2,1)}, bf16[96,768]{1,0:T(8,128)(2,1)S(1)}, u32[]{:S(2)}) copy-start(bf16[96,768]{1,0:T(8,128)(2,1)S(1)} %collective-permute-done.45.refs_12_) | copy-start | bytes 442372
  142.2 9.3 %collective-permute-start.34 = (bf16[128,768]{1,0:T(8,128)(2,1)S(1)}, bf16[128,768]{1,0:T(8,128)(2,1)S(1)}, u32[]{:S(2)}, u32[]{:S(2)}) collective-permute-start(bf16[128,768]{1,0:T(8,128)(2,1)S(1)} %get-tuple-element.108.refs_0_), channel_id=1, source_target_pairs={{0,2},{2,0},{4,6},{6,4},{8,10},{10,8},{12,14},{14,12},{16,18},{18,... | collective-permute-start | bytes 589832 | tf_op jit(solution)/shard_map/ppermute | solution.py:721
  147.1 17.3 %copy-start.36 = (bf16[96,768]{1,0:T(8,128)(2,1)}, bf16[96,768]{1,0:T(8,128)(2,1)S(1)}, u32[]{:S(2)}) copy-start(bf16[96,768]{1,0:T(8,128)(2,1)S(1)} %collective-permute-done.41.refs_8_) | copy-start | bytes 442372
  147.1 6.6 %collective-permute-start.48 = (bf16[96,768]{1,0:T(8,128)(2,1)S(1)}, bf16[96,768]{1,0:T(8,128)(2,1)S(1)}, u32[]{:S(2)}, u32[]{:S(2)}) collective-permute-start(bf16[96,768]{1,0:T(8,128)(2,1)S(1)} %collective-permute-done.45.refs_12_), channel_id=1, source_target_pairs={{0,6},{2,4},{4,2},{6,0},{8,14},{10,12},{12,10},{14,8},{16,22},{18,... | collective-permute-start | bytes 442376 | tf_op jit(solution)/shard_map/ppermute | solution.py:721
  148.8 15.6 %copy-start.37 = (bf16[96,768]{1,0:T(8,128)(2,1)}, bf16[96,768]{1,0:T(8,128)(2,1)S(1)}, u32[]{:S(2)}) copy-start(bf16[96,768]{1,0:T(8,128)(2,1)S(1)} %collective-permute-done.37.refs_4_) | copy-start | bytes 442372
  148.8 8.0 %collective-permute-start.47 = (bf16[96,768]{1,0:T(8,128)(2,1)S(1)}, bf16[96,768]{1,0:T(8,128)(2,1)S(1)}, u32[]{:S(2)}, u32[]{:S(2)}) collective-permute-start(bf16[96,768]{1,0:T(8,128)(2,1)S(1)} %collective-permute-done.45.refs_12_), channel_id=1, source_target_pairs={{0,4},{2,6},{4,0},{6,2},{8,12},{10,14},{12,8},{14,10},{16,20},{18,... | collective-permute-start | bytes 442376 | tf_op jit(solution)/shard_map/ppermute | solution.py:721
  149.9 7.9 %collective-permute-start.46 = (bf16[96,768]{1,0:T(8,128)(2,1)S(1)}, bf16[96,768]{1,0:T(8,128)(2,1)S(1)}, u32[]{:S(2)}, u32[]{:S(2)}) collective-permute-start(bf16[96,768]{1,0:T(8,128)(2,1)S(1)} %collective-permute-done.45.refs_12_), channel_id=1, source_target_pairs={{0,2},{2,0},{4,6},{6,4},{8,10},{10,8},{12,14},{14,12},{16,18},{18,... | collective-permute-start | bytes 442376 | tf_op jit(solution)/shard_map/ppermute | solution.py:721
  150.6 8.6 %collective-permute-start.43 = (bf16[96,768]{1,0:T(8,128)(2,1)S(1)}, bf16[96,768]{1,0:T(8,128)(2,1)S(1)}, u32[]{:S(2)}, u32[]{:S(2)}) collective-permute-start(bf16[96,768]{1,0:T(8,128)(2,1)S(1)} %collective-permute-done.41.refs_8_), channel_id=1, source_target_pairs={{0,4},{2,6},{4,0},{6,2},{8,12},{10,14},{12,8},{14,10},{16,20},{18,... | collective-permute-start | bytes 442376 | tf_op jit(solution)/shard_map/ppermute | solution.py:721
  151.5 12.8 %collective-permute-start.44 = (bf16[128,768]{1,0:T(8,128)(2,1)S(1)}, bf16[128,768]{1,0:T(8,128)(2,1)S(1)}, u32[]{:S(2)}, u32[]{:S(2)}) collective-permute-start(bf16[128,768]{1,0:T(8,128)(2,1)S(1)} %collective-permute-done.36.refs_3_), channel_id=1, source_target_pairs={{0,16},{2,18},{4,20},{6,22},{8,24},{10,26},{12,28},{14,30},{16,0},... | collective-permute-start | bytes 589832 | tf_op jit(solution)/shard_map/ppermute | solution.py:721
  153.6 10.7 %collective-permute-start.40 = (bf16[128,768]{1,0:T(8,128)(2,1)S(1)}, bf16[128,768]{1,0:T(8,128)(2,1)S(1)}, u32[]{:S(2)}, u32[]{:S(2)}) collective-permute-start(bf16[128,768]{1,0:T(8,128)(2,1)S(1)} %collective-permute-done.36.refs_3_), channel_id=1, source_target_pairs={{0,8},{2,10},{4,12},{6,14},{8,0},{10,2},{12,4},{14,6},{16,24},{18,... | collective-permute-start | bytes 589832 | tf_op jit(solution)/shard_map/ppermute | solution.py:721
  156.8 5.6 %collective-permute-start.42 = (bf16[96,768]{1,0:T(8,128)(2,1)S(1)}, bf16[96,768]{1,0:T(8,128)(2,1)S(1)}, u32[]{:S(2)}, u32[]{:S(2)}) collective-permute-start(bf16[96,768]{1,0:T(8,128)(2,1)S(1)} %collective-permute-done.41.refs_8_), channel_id=1, source_target_pairs={{0,2},{2,0},{4,6},{6,4},{8,10},{10,8},{12,14},{14,12},{16,18},{18,... | collective-permute-start | bytes 442376 | tf_op jit(solution)/shard_map/ppermute | solution.py:721
  157.8 5.1 %collective-permute-start.39 = (bf16[96,768]{1,0:T(8,128)(2,1)S(1)}, bf16[96,768]{1,0:T(8,128)(2,1)S(1)}, u32[]{:S(2)}, u32[]{:S(2)}) collective-permute-start(bf16[96,768]{1,0:T(8,128)(2,1)S(1)} %collective-permute-done.37.refs_4_), channel_id=1, source_target_pairs={{0,4},{2,6},{4,0},{6,2},{8,12},{10,14},{12,8},{14,10},{16,20},{18,... | collective-permute-start | bytes 442376 | tf_op jit(solution)/shard_map/ppermute | solution.py:721
  159.2 5.1 %collective-permute-start.38 = (bf16[96,768]{1,0:T(8,128)(2,1)S(1)}, bf16[96,768]{1,0:T(8,128)(2,1)S(1)}, u32[]{:S(2)}, u32[]{:S(2)}) collective-permute-start(bf16[96,768]{1,0:T(8,128)(2,1)S(1)} %collective-permute-done.37.refs_4_), channel_id=1, source_target_pairs={{0,2},{2,0},{4,6},{6,4},{8,10},{10,8},{12,14},{14,12},{16,18},{18,... | collective-permute-start | bytes 442376 | tf_op jit(solution)/shard_map/ppermute | solution.py:721
  (40 other events, 234.3 us)
